TPU v7x, 32 devices: a whole 2x2x4 slice. The times are simulated.
32 devices in a mesh: groups: 2 (over x), wide: 16 (over z, y, core).
Axes of the slice: x: 2, y: 2, z: 4, core: 2. Of those that a mesh axis runs over, the one named last changes fastest.
Arguments:
- tokens: bfloat16 [8192, 8192], P(('groups', 'wide')), parts along dimension 0, may hold values from -6 to 6
- cotangent: bfloat16 [8192, 1024], P(('groups', 'wide')), parts along dimension 0, may hold values from -6 to 6
- frozen_key_matrix: bfloat16 [8192, 1024], P('wide'), may hold values from -0.0625 to 0.0625
- adapter_down_weight: bfloat16 [64, 8192, 64], P(('groups', 'wide')), parts along dimension 0, may hold values from -0.0625 to 0.0625
- adapter_up_weight: bfloat16 [64, 64, 1024], P(('groups', 'wide')), parts along dimension 0, may hold values from -0.75 to 0.75
- token_adapter_index: int32 [8192, 1], P(('groups', 'wide')), parts along dimension 0, may hold values from 0 to 31; in each aligned block of 256 rows (0 to 255, 256 to 511, ...) at most 13 rows name the same one
- adapter_storage_index: int32 [64], P('groups'), parts along dimension 0, may hold values from 0 to 31, each once
Outputs:
- key_output: bfloat16 [8192, 1024], P(('groups', 'wide')), parts along dimension 0
- token_input_gradient: bfloat16 [8192, 8192], P(('groups', 'wide')), parts along dimension 0
- down_matrix_gradient: float32 [64, 8192, 64], P(('groups', 'wide')), parts along dimension 0
- up_matrix_gradient: float32 [64, 64, 1024], P(('groups', 'wide')), parts along dimension 0
There are 2 independent parts, one for each index of `groups`. A program takes and returns all parts, laid end to end along the dimension named above; an argument that names none is the same for every part. Nothing has to cross between parts.
Inputs may be any that keep to these rules, and one draw needn't show every extreme that they name: `token_adapter_index`: among the rows of one device, each adapter is named by at most 13 rows. A permutation: the weights of adapter a stand at position adapter_storage_index[a] of adapter_down_weight and adapter_up_weight, on device adapter_storage_index[a] // 2 of wide.
All inputs are finite; a program needn't handle non-finite values.
Results may differ from a plain program's by a relative error of at most 0.0029.
Values may be sent and summed in bfloat16 or wider, within the bound.
No kernel may reach another device: no remote copies, remote signals or barrier semaphores. Data moves between devices by JAX's collectives and lax.ppermute only.
A program may use at most 128 MiB of HBM per device.

v0:
```python
import jax
import jax.numpy as jnp
from jax import lax
from jax.sharding import PartitionSpec as P

adapter_scale = 0.25


def route_slots(token_adapter_index, adapter_storage_index, capacity):
    flat_ids = token_adapter_index[:, 0]
    adapter_entries = adapter_storage_index.shape[0]
    onehot = (flat_ids[:, None] == jnp.arange(adapter_entries, dtype=jnp.int32)[None, :]).astype(
        jnp.int32
    )
    earlier = jnp.cumsum(onehot, axis=0) * onehot
    within = jnp.sum(earlier, axis=1) - 1
    storage_position = jnp.sum(onehot * adapter_storage_index[None, :], axis=1)
    return storage_position * capacity + within


def shards(
    tokens,
    cotangent,
    frozen_key_matrix,
    adapter_down_weight,
    adapter_up_weight,
    token_adapter_index,
    adapter_storage_index,
):
    devices = lax.axis_size("wide")
    tok_count = tokens.shape[0]
    adapter_token_count = adapter_down_weight.shape[0]
    adapter_entries = adapter_storage_index.shape[0]
    capacity = max(2, 5 * tok_count // (3 * adapter_token_count * devices))
    total_slots = adapter_entries * capacity
    slots = route_slots(token_adapter_index, adapter_storage_index, capacity)

    def dispatch(values):
        buffer = jnp.zeros((total_slots, values.shape[1]), values.dtype).at[slots].set(values)
        return buffer.reshape(devices, adapter_token_count, capacity, values.shape[1])

    def collect(values):
        return values.reshape(total_slots, values.shape[3])[slots]

    token_inputs = lax.all_to_all(dispatch(tokens), "wide", split_axis=0, concat_axis=0, tiled=True)
    narrowed_rows = jnp.einsum(
        "ylem,lmv->ylev", token_inputs, adapter_down_weight, preferred_element_type=jnp.float32
    ).astype(jnp.bfloat16)
    widened_rows = (
        adapter_scale
        * jnp.einsum(
            "pxze,xey->pxzy", narrowed_rows, adapter_up_weight, preferred_element_type=jnp.float32
        )
    ).astype(jnp.bfloat16)
    narrowed_rows, widened_rows = (narrowed_rows, widened_rows)
    expanded_back = lax.all_to_all(widened_rows, "wide", split_axis=0, concat_axis=0, tiled=True)
    gradient_tuple = lax.all_to_all(
        dispatch(cotangent), "wide", split_axis=0, concat_axis=0, tiled=True
    )
    hidden_gradient = jnp.einsum(
        "fxuh,xmh->fxum", gradient_tuple, adapter_up_weight, preferred_element_type=jnp.float32
    ).astype(jnp.bfloat16)
    down_gradient_piece = adapter_scale * jnp.einsum(
        "sjcd,sjcr->jdr", token_inputs, hidden_gradient, preferred_element_type=jnp.float32
    )
    up_gradient_piece = adapter_scale * jnp.einsum(
        "sjcr,sjck->jrk", narrowed_rows, gradient_tuple, preferred_element_type=jnp.float32
    )
    adapter_input = (
        adapter_scale
        * jnp.einsum(
            "yegp,ezp->yegz",
            hidden_gradient,
            adapter_down_weight,
            preferred_element_type=jnp.float32,
        )
    ).astype(jnp.bfloat16)
    down_matrix_gradient, up_matrix_gradient, adapter_input = (
        down_gradient_piece,
        up_gradient_piece,
        adapter_input,
    )
    input_gradient_piece = lax.all_to_all(
        adapter_input, "wide", split_axis=0, concat_axis=0, tiled=True
    )
    whole = lax.all_gather(frozen_key_matrix, "wide", axis=0, tiled=True)
    frozen_path_output = jnp.dot(tokens, whole, preferred_element_type=jnp.float32)
    frozen_path_gradient = lax.dot_general(
        cotangent, whole, (((1,), (1,)), ((), ())), preferred_element_type=jnp.float32
    )
    key_output = (frozen_path_output + collect(expanded_back).astype(jnp.float32)).astype(
        jnp.bfloat16
    )
    token_input_gradient = (
        frozen_path_gradient + collect(input_gradient_piece).astype(jnp.float32)
    ).astype(jnp.bfloat16)
    return (key_output, token_input_gradient, down_matrix_gradient, up_matrix_gradient)


def solution(mesh):
    return jax.shard_map(
        shards,
        mesh=mesh,
        in_specs=(
            P(("groups", "wide"), None),
            P(("groups", "wide"), None),
            P("wide", None),
            P(("groups", "wide"), None, None),
            P(("groups", "wide"), None, None),
            P(("groups", "wide"), None),
            P("groups"),
        ),
        out_specs=(
            P(("groups", "wide"), None),
            P(("groups", "wide"), None),
            P(("groups", "wide"), None, None),
            P(("groups", "wide"), None, None),
        ),
        check_vma=False,
    )
```

profile of v0, /device:TPU:0, one launch (start us, length us, event | category | flops | bytes accessed | tf_op | source)
XLA Modules:
  0.0 523.4 jit_solution(5084833822649230804)
XLA Ops:
  7.2 0.0 copy-start
  7.2 0.0 all-gather.2.cloned.1.call-start
  7.2 0.7 all-gather.2.cloned.1.call-update
  7.9 0.7 fusion.34
  8.6 0.6 reduce-window.6
  9.2 0.2 slice_reduce_fusion
  9.4 0.8 select_reduce_fusion
  10.2 3.1 scatter_custom_fusion.1
  13.4 1.4 reshape.71
  14.8 1.8 copy.29
  16.6 7.4 %all-to-all-start.2 = ((bf16[16,2,13,1024]{3,1,2,0:T(2,128)(2,1)}), bf16[16,2,13,1024]{3,1,2,0:T(2,128)(2,1)S(1)}, u32[]{:S(2)}, u32[]{:S(2)}) async-start(bf16[16,2,13,1024]{3,1,2,0:T(2,128)(2,1)} %copy.29), calls=%async_computation.2 | async-start | bytes 1703936 | tf_op jit(solution)/shard_map/all_to_all | solution.py:57
  24.0 12.0 %scatter_custom_fusion = bf16[416,8192]{1,0:T(8,128)(2,1)} fusion(s32[256]{0:T(256)S(1)} %bitcast.64, bf16[256,8192]{1,0:T(8,128)(2,1)} %param.7, bf16[]{:T(256)} %constant.6.clone.1), kind=kCustom, calls=%fused_computation.13 | custom fusion | bytes 6816256 | tf_op jit(solution)/shard_map/scatter | solution.py:39
  36.0 7.7 %reshape.69 = bf16[16,2,13,8192]{3,2,1,0:T(8,128)(2,1)} reshape(bf16[416,8192]{1,0:T(8,128)(2,1)} %scatter_custom_fusion) | data formatting | bytes 13631488 | tf_op jit(solution)/shard_map/reshape | solution.py:40
  43.7 12.0 %copy.24 = bf16[16,2,13,8192]{3,1,2,0:T(2,128)(2,1)} copy(bf16[16,2,13,8192]{3,2,1,0:T(8,128)(2,1)} %reshape.69) | data formatting | bytes 13631488 | tf_op jit(solution)/shard_map/reshape | solution.py:40
  55.7 0.0 copy-start.2
  55.7 1.9 all-to-all-done.2
  57.6 15.5 %all-to-all-start = ((bf16[16,2,13,8192]{3,1,2,0:T(2,128)(2,1)}), bf16[16,2,13,8192]{3,1,2,0:T(2,128)(2,1)}, u32[]{:S(2)}, u32[]{:S(2)}) async-start(bf16[16,2,13,8192]{3,1,2,0:T(2,128)(2,1)} %copy.24), calls=%async_computation | async-start | bytes 13631488 | tf_op jit(solution)/shard_map/all_to_all | solution.py:45
  73.1 0.0 copy-done.2
  73.1 0.4 fusion.18
  73.6 0.0 copy-done
  73.6 1.9 fusion
  75.5 7.3 %copy.32 = bf16[16,2,13,8192]{3,1,2,0:T(2,128)(2,1)} copy(bf16[16,2,13,8192]{3,0,2,1:T(8,128)(2,1)S(1)} %fusion) | data formatting | bytes 13631488 | tf_op jit(solution)/shard_map/convert_element_type | solution.py:77
  82.8 181.1 %all-to-all-done = bf16[16,2,13,8192]{3,1,2,0:T(2,128)(2,1)} async-done(((bf16[16,2,13,8192]{3,1,2,0:T(2,128)(2,1)}), bf16[16,2,13,8192]{3,1,2,0:T(2,128)(2,1)}, u32[]{:S(2)}, u32[]{:S(2)}) %all-to-all-start) | async-done | bytes 6815776 | tf_op jit(solution)/shard_map/all_to_all | solution.py:45
  263.9 30.4 %all-to-all-start.3 = ((bf16[16,2,13,8192]{3,1,2,0:T(2,128)(2,1)}), bf16[16,2,13,8192]{3,1,2,0:T(2,128)(2,1)}, u32[]{:S(2)}, u32[]{:S(2)}) async-start(bf16[16,2,13,8192]{3,1,2,0:T(2,128)(2,1)} %copy.32), calls=%async_computation.3 | async-start | bytes 13631488 | tf_op jit(solution)/shard_map/all_to_all | solution.py:83
  294.3 6.8 %fusion.19 = bf16[16,2,13,64]{3,2,0,1:T(8,128)(2,1)S(1)} fusion(bf16[2,8192,64]{1,2,0:T(8,128)(2,1)S(1)} %copy-done, bf16[16,2,13,8192]{3,1,2,0:T(2,128)(2,1)} %all-to-all-done), kind=kOutput, calls=%fused_computation.26 | convolution fusion | flops 436234240 | bytes 8966144 | tf_op jit(solution)/shard_map/ylem,lmv->ylev/dot_general | solution.py:46
  301.1 0.4 fusion.10
  301.5 1.8 copy.27
  303.3 114.3 %all-to-all-done.3 = bf16[16,2,13,8192]{3,1,2,0:T(2,128)(2,1)} async-done(((bf16[16,2,13,8192]{3,1,2,0:T(2,128)(2,1)}), bf16[16,2,13,8192]{3,1,2,0:T(2,128)(2,1)}, u32[]{:S(2)}, u32[]{:S(2)}) %all-to-all-start.3) | async-done | bytes 6815776 | tf_op jit(solution)/shard_map/all_to_all | solution.py:83
  417.6 30.4 %all-to-all-start.1 = ((bf16[16,2,13,1024]{3,1,2,0:T(2,128)(2,1)}), bf16[16,2,13,1024]{3,1,2,0:T(2,128)(2,1)S(1)}, u32[]{:S(2)}, u32[]{:S(2)}) async-start(bf16[16,2,13,1024]{3,1,2,0:T(2,128)(2,1)} %copy.27), calls=%async_computation.1 | async-start | bytes 1703936 | tf_op jit(solution)/shard_map/all_to_all | solution.py:56
  448.0 1.3 fusion.12
  449.3 12.7 %fusion.2 = f32[2,8192,64]{1,2,0:T(8,128)} fusion(bf16[16,2,13,64]{3,2,0,1:T(8,128)(2,1)S(1)} %fusion.18, bf16[16,2,13,8192]{3,1,2,0:T(2,128)(2,1)} %all-to-all-done), kind=kOutput, calls=%fused_computation.9 | convolution fusion | flops 437256192 | bytes 11063296 | tf_op jit(solution)/shard_map/sjcd,sjcr->jdr/dot_general | solution.py:63
  462.0 11.6 %copy.33 = bf16[16,2,13,8192]{3,2,1,0:T(8,128)(2,1)} copy(bf16[16,2,13,8192]{3,1,2,0:T(2,128)(2,1)} %all-to-all-done.3) | data formatting | bytes 13631488 | tf_op jit(solution)/shard_map/all_to_all | solution.py:83
  473.5 7.6 %reshape.72 = bf16[416,8192]{1,0:T(8,128)(2,1)} reshape(bf16[16,2,13,8192]{3,2,1,0:T(8,128)(2,1)} %copy.33) | data formatting | bytes 13631488 | tf_op jit(solution)/shard_map/reshape | solution.py:43
  481.2 0.0 all-to-all-done.1
  481.2 0.3 copy.28
  481.4 0.3 reshape.70
  481.7 0.0 copy-start.4
  481.7 12.9 %gather_fusion.1 = bf16[256,8192]{1,0:T(8,128)(2,1)} fusion(bf16[416,8192]{1,0:T(8,128)(2,1)} %reshape.72, s32[1024]{0:T(1024)S(1)} %pad_clamp_fusion), kind=kCustom, calls=%fused_computation.1 | custom fusion | bytes 8389632 | tf_op jit(solution)/shard_map/gather | solution.py:43
  494.6 1.2 gather_fusion
  495.8 0.0 all-gather.2.cloned.1.call-done
  495.8 0.0 copy-done.4
  495.8 0.0 copy-start.3
  495.8 11.1 %fusion.1 = bf16[256,8192]{1,0:T(8,128)(2,1)} fusion(bf16[256,1024]{1,0:T(8,128)(2,1)S(1)} %copy-done.4, bf16[8192,1024]{1,0:T(8,128)(2,1)} %all-gather.2.cloned.1.call-done, bf16[256,8192]{1,0:T(8,128)(2,1)} %gather_fusion.1), kind=kOutput, calls=%fused_computation.7 | convolution fusion | flops 4301258752 | bytes 25690112 | tf_op jit(solution)/shard_map/dot_general | solution.py:88
  506.9 0.0 copy-done.3
  506.9 0.0 copy-start.1
  506.9 9.2 %fusion.11 = bf16[256,1024]{1,0:T(8,128)(2,1)} fusion(bf16[256,8192]{1,0:T(8,128)(2,1)S(1)} %copy-done.3, bf16[8192,1024]{1,0:T(8,128)(2,1)} %all-gather.2.cloned.1.call-done, bf16[256,1024]{1,0:T(8,128)(2,1)S(1)} %gather_fusion), kind=kOutput, calls=%fused_computation.20 | convolution fusion | flops 4295753728 | bytes 22020096 | tf_op jit(solution)/shard_map/dot_general | solution.py:87
  516.1 0.0 copy-done.1
  (5 shorter events, 0.1 us)
Async XLA Ops:
  7.2 66.4 %copy-start = (bf16[2,8192,64]{1,2,0:T(8,128)(2,1)S(1)}, bf16[2,8192,64]{1,2,0:T(8,128)(2,1)}, u32[]{:S(2)}) copy-start(bf16[2,8192,64]{1,2,0:T(8,128)(2,1)} %param.10) | copy-start | bytes 6291460
  7.2 488.6 %all-gather.2.cloned.1.call-start = ((), (), s32[]{:S(2)}) async-start(), calls=%async_computation.4 | async-start | bytes 17825792 | tf_op jit(solution)/shard_map/all_gather | solution.py:86
  16.6 41.0 %all-to-all-start.2 = ((bf16[16,2,13,1024]{3,1,2,0:T(2,128)(2,1)}), bf16[16,2,13,1024]{3,1,2,0:T(2,128)(2,1)S(1)}, u32[]{:S(2)}, u32[]{:S(2)}) async-start(bf16[16,2,13,1024]{3,1,2,0:T(2,128)(2,1)} %copy.29), calls=%async_computation.2 | async-start | bytes 1703936 | tf_op jit(solution)/shard_map/all_to_all | solution.py:57
  55.7 17.5 %copy-start.2 = (bf16[2,64,1024]{2,1,0:T(8,128)(2,1)S(1)}, bf16[2,64,1024]{2,1,0:T(8,128)(2,1)}, u32[]{:S(2)}) copy-start(bf16[2,64,1024]{2,1,0:T(8,128)(2,1)} %param.11) | copy-start | bytes 786436
  57.6 206.3 %all-to-all-start = ((bf16[16,2,13,8192]{3,1,2,0:T(2,128)(2,1)}), bf16[16,2,13,8192]{3,1,2,0:T(2,128)(2,1)}, u32[]{:S(2)}, u32[]{:S(2)}) async-start(bf16[16,2,13,8192]{3,1,2,0:T(2,128)(2,1)} %copy.24), calls=%async_computation | async-start | bytes 13631488 | tf_op jit(solution)/shard_map/all_to_all | solution.py:45
  263.9 153.7 %all-to-all-start.3 = ((bf16[16,2,13,8192]{3,1,2,0:T(2,128)(2,1)}), bf16[16,2,13,8192]{3,1,2,0:T(2,128)(2,1)}, u32[]{:S(2)}, u32[]{:S(2)}) async-start(bf16[16,2,13,8192]{3,1,2,0:T(2,128)(2,1)} %copy.32), calls=%async_computation.3 | async-start | bytes 13631488 | tf_op jit(solution)/shard_map/all_to_all | solution.py:83
  417.6 63.5 %all-to-all-start.1 = ((bf16[16,2,13,1024]{3,1,2,0:T(2,128)(2,1)}), bf16[16,2,13,1024]{3,1,2,0:T(2,128)(2,1)S(1)}, u32[]{:S(2)}, u32[]{:S(2)}) async-start(bf16[16,2,13,1024]{3,1,2,0:T(2,128)(2,1)} %copy.27), calls=%async_computation.1 | async-start | bytes 1703936 | tf_op jit(solution)/shard_map/all_to_all | solution.py:56
  481.7 14.1 %copy-start.4 = (bf16[256,1024]{1,0:T(8,128)(2,1)S(1)}, bf16[256,1024]{1,0:T(8,128)(2,1)}, u32[]{:S(2)}) copy-start(bf16[256,1024]{1,0:T(8,128)(2,1)} %param.8) | copy-start | bytes 1572868
  495.8 11.1 %copy-start.3 = (bf16[256,8192]{1,0:T(8,128)(2,1)S(1)}, bf16[256,8192]{1,0:T(8,128)(2,1)}, u32[]{:S(2)}) copy-start(bf16[256,8192]{1,0:T(8,128)(2,1)} %param.7) | copy-start | bytes 12582916
  506.9 9.2 %copy-start.1 = (bf16[2,8192,64]{1,2,0:T(8,128)(2,1)S(1)}, bf16[2,8192,64]{1,2,0:T(8,128)(2,1)}, u32[]{:S(2)}) copy-start(bf16[2,8192,64]{1,2,0:T(8,128)(2,1)} %param.10) | copy-start | bytes 6291460
Sparse Core Ops, SparseCore 0:
  10.2 250.9 all-gather.1
where the time goes:
time: 532 us; the launch traced here: 523 us
  waiting for transfers between devices  298 us (56%)
  starting transfers between devices  83.7 us (16%)
  local copies, waits for them, and re-layouts  81.1 us (15%)
  matrix products  43.9 us (8%)
  between operations  14.6 us (3%)
    all_to_all x1, waiting for transfers between devices, shards(): lax.all_to_all(dispatch(tokens), 'wide', split_axis=0, concat_axis=0, til...  181 us
    all_to_all x1, waiting for transfers between devices, shards(): lax.all_to_all(adapter_input, 'wide', split_axis=0, concat_axis=0, tiled=...  114 us
    all_to_all x1, starting transfers between devices, shards(): lax.all_to_all(adapter_input, 'wide', split_axis=0, concat_axis=0, tiled=...  30.4 us
    all_to_all x1, starting transfers between devices, shards(): lax.all_to_all(widened_rows, 'wide', split_axis=0, concat_axis=0, tiled=T...  30.4 us
    reshape x4, local copies, waits for them, and re-layouts, dispatch(): buffer.reshape(devices, adapter_token_count, capacity, values.shape[1])  22.9 us
    all_to_all x1, starting transfers between devices, shards(): lax.all_to_all(dispatch(tokens), 'wide', split_axis=0, concat_axis=0, til...  15.5 us
    scatter x2, local copies, waits for them, and re-layouts, dispatch(): jnp.zeros((total_slots, values.shape[1]), values.dtype).at[slots]  15.1 us
    gather x2, local copies, waits for them, and re-layouts, collect(): return values.reshape(total_slots, values.shape[3])[slots]  14 us
  transfers between devices with their start and end apart: 5, of which 3 were waited for; matrix products, arithmetic and copies ran while one was open for 20% of the time, Pallas kernels for 0%

commit v1 on v0

v1 whole, which is shorter than its diff:
```python
import jax
import jax.numpy as jnp
from jax import lax
from jax.sharding import PartitionSpec as P

adapter_scale = 0.25
bf16 = jnp.bfloat16
f32 = jnp.float32
CHAIN = 4


def dot(a, b, dims):
    return lax.dot_general(a, b, (dims, ((), ())), preferred_element_type=f32)


def shards(
    tokens,
    cotangent,
    frozen_key_matrix,
    adapter_down_weight,
    adapter_up_weight,
    token_adapter_index,
    adapter_storage_index,
):
    devices = lax.axis_size("wide")
    groups = lax.axis_size("groups")
    tok_count = tokens.shape[0]
    locals_, width, rank = adapter_down_weight.shape
    features = cotangent.shape[1]
    entries = adapter_storage_index.shape[0]
    capacity = max(2, 5 * tok_count // (3 * locals_ * devices))
    depth = CHAIN
    plane = devices // depth
    block = locals_ * rank
    me = lax.axis_index("wide")
    z, q = me // plane, me % plane
    group = lax.axis_index("groups")

    def shift(values, step, sources):
        pairs = [
            (s * plane + i, (s + step) * plane + i) for s in sources for i in range(plane)
        ]
        return lax.ppermute(values, "wide", pairs)

    def swap(values, mask):
        return lax.ppermute(values, "wide", [(i, i ^ mask) for i in range(devices)])

    def chain_gather(values):
        ups, downs = [], []
        up = down = values
        for k in range(1, depth):
            up = shift(up, 1, range(k - 1, depth - 1))
            down = shift(down, -1, range(1, depth - k + 1))
            ups.append(up)
            downs.append(down)
        line = jnp.concatenate(ups[::-1] + [values] + downs, axis=0)
        rows = values.shape[0]
        return lax.dynamic_slice_in_dim(line, (depth - 1 - z) * rows, depth * rows, 0)

    def chain_reduce(parts, own):
        up = down = None
        for k in range(1, depth):
            far = depth - k
            here_up = lax.dynamic_index_in_dim(parts, jnp.minimum(z + far, depth - 1), 0, False)
            here_down = lax.dynamic_index_in_dim(parts, jnp.maximum(z - far, 0), 0, False)
            if up is not None:
                here_up = (here_up.astype(f32) + up.astype(f32)).astype(bf16)
                here_down = (here_down.astype(f32) + down.astype(f32)).astype(bf16)
            up = shift(here_up, 1, range(0, k))
            down = shift(here_down, -1, range(depth - k, depth))
        return own + up.astype(f32) + down.astype(f32)

    share = frozen_key_matrix.shape[0] // groups
    down_rows = jnp.transpose(adapter_down_weight, (0, 2, 1)).reshape(block, width)
    up_rows = adapter_up_weight.reshape(block, features)

    flat_ids = token_adapter_index[:, 0]
    onehot = (flat_ids[:, None] == jnp.arange(entries, dtype=jnp.int32)[None, :]).astype(jnp.int32)
    within = jnp.sum(jnp.cumsum(onehot, axis=0) * onehot, axis=1) - 1
    position = jnp.sum(onehot * adapter_storage_index[None, :], axis=1)
    home, local = position // locals_, position % locals_
    relative = (home % plane) ^ q
    rows = depth * locals_ * capacity
    slots = ((relative * depth + home // plane) * locals_ + local) * capacity + within
    spread = (
        jnp.arange(plane * rows, dtype=jnp.int32)[:, None] == slots[None, :]
    ).astype(bf16)

    def dispatch(values):
        out = []
        for m in range(plane):
            part = dot(spread[m * rows : (m + 1) * rows], values, ((1,), (0,))).astype(bf16)
            out.append(part if m == 0 else swap(part, m))
        return jnp.concatenate(out, axis=0)

    def give_back(values):
        out = []
        for m in range(plane):
            part = values[m * rows : (m + 1) * rows]
            out.append(part if m == 0 else swap(part, m))
        return jnp.concatenate(out, axis=0)

    up_all = chain_gather(up_rows)
    down_all = chain_gather(down_rows)
    cot = dispatch(cotangent)
    token_inputs = dispatch(tokens)

    row_adapter = (jnp.arange(plane * rows) % rows) // capacity
    col_adapter = jnp.arange(depth * block) // rank
    mask = row_adapter[:, None] == col_adapter[None, :]

    def masked(values):
        return jnp.where(mask, values, 0.0).astype(bf16)

    hidden = masked(dot(cot, up_all, ((1,), (1,))))
    own_cols = lambda v: lax.dynamic_slice_in_dim(v, z * block, block, 1)
    down_parts = (adapter_scale * dot(hidden, token_inputs, ((0,), (0,)))).astype(bf16)
    down_own = adapter_scale * dot(own_cols(hidden), token_inputs, ((0,), (0,)))
    down_grad = chain_reduce(down_parts.reshape(depth, block, width), down_own)

    lora_input = (adapter_scale * dot(hidden, down_all, ((1,), (0,)))).astype(bf16)
    lora_back = give_back(lora_input)

    shrunk = masked(dot(token_inputs, down_all, ((1,), (1,))))
    expanded = (adapter_scale * dot(shrunk, up_all, ((1,), (0,)))).astype(bf16)
    expanded_back = give_back(expanded)
    up_parts = (adapter_scale * dot(shrunk, cot, ((0,), (0,)))).astype(bf16)
    up_own = adapter_scale * dot(own_cols(shrunk), cot, ((0,), (0,)))
    up_grad = chain_reduce(up_parts.reshape(depth, block, features), up_own)

    piece = lax.dynamic_slice_in_dim(frozen_key_matrix, group * share, share, 0)
    gathered = chain_gather(piece).reshape(depth, 1, 1, share, features)

    def join(values, mask):
        other = swap(values, mask)
        low = (q & mask) == 0
        return jnp.where(
            low, jnp.concatenate([values, other], 1), jnp.concatenate([other, values], 1)
        )

    bit = 2
    while bit < plane:
        gathered = join(gathered, bit)
        bit *= 2
    sides = [gathered] + [
        lax.ppermute(gathered, "groups", [(i, (i + s) % groups) for i in range(groups)])
        for s in range(1, groups)
    ]
    sides = jnp.concatenate(sides[::-1] + sides[:0:-1], 2)
    gathered = lax.dynamic_slice_in_dim(sides, groups - 1 - group, groups, 2)
    mate = swap(gathered, 1)
    even = jnp.where(q % 2 == 0, gathered, mate)
    odd = jnp.where(q % 2 == 0, mate, gathered)
    whole = jnp.stack([even, odd], 2).reshape(width, features)

    frozen_out = dot(tokens, whole, ((1,), (0,)))
    frozen_grad = dot(cotangent, whole, ((1,), (1,)))
    key_output = (frozen_out + dot(spread, expanded_back, ((0,), (0,)))).astype(bf16)
    token_grad = (frozen_grad + dot(spread, lora_back, ((0,), (0,)))).astype(bf16)
    down_grad = jnp.transpose(down_grad.reshape(locals_, rank, width), (0, 2, 1))
    up_grad = up_grad.reshape(locals_, rank, features)
    return key_output, token_grad, down_grad, up_grad


def solution(mesh):
    return jax.shard_map(
        shards,
        mesh=mesh,
        in_specs=(
            P(("groups", "wide"), None),
            P(("groups", "wide"), None),
            P("wide", None),
            P(("groups", "wide"), None, None),
            P(("groups", "wide"), None, None),
            P(("groups", "wide"), None),
            P("groups"),
        ),
        out_specs=(
            P(("groups", "wide"), None),
            P(("groups", "wide"), None),
            P(("groups", "wide"), None, None),
            P(("groups", "wide"), None, None),
        ),
        check_vma=False,
    )
```

time: 532 us -> 525 us (0.987)
  the two profiles are of different devices: /device:TPU:0 before, /device:TPU:18 now
where the time goes in v1:
time: 525 us; the launch traced here: 515 us
  waiting for transfers between devices  239 us (46%)
  starting transfers between devices  93.6 us (18%)
  matrix products  86 us (16%)
  other arithmetic  49.3 us (9%)
  local copies, waits for them, and re-layouts  45 us (9%)
    ppermute x30, waiting for transfers between devices, shift(): return lax.ppermute(values, 'wide', pairs)  129 us
    ppermute x14, waiting for transfers between devices, swap(): return lax.ppermute(values, 'wide', [(i, i ^ mask) for i in range(devices)])  104 us
    dot_general x20, matrix products, dot(): return lax.dot_general(a, b, (dims, ((), ())), preferred_element_type=f32)  86 us
    ppermute x30, starting transfers between devices, shift(): return lax.ppermute(values, 'wide', pairs)  82.7 us
    unnamed x82, local copies, waits for them, and re-layouts  37.2 us
    another operation x2, other arithmetic, shards(): whole = jnp.stack([even, odd], 2).reshape(width, features)  17.3 us
    convert_element_type x4, other arithmetic, chain_reduce(): here_up = (here_up.astype(f32) + up.astype(f32)).astype(bf16)  11.4 us
  transfers between devices with their start and end apart: 45, of which 18 were waited for; matrix products, arithmetic and copies ran while one was open for 24% of the time, Pallas kernels for 0%

profile of v1, /device:TPU:18, one launch (start us, length us, event | category | flops | bytes accessed | tf_op | source)
XLA Modules:
  0.0 514.8 jit_solution(10838711173132026900)
XLA Ops:
  0.6 3.6 collective-permute-start.18
  9.2 4.4 convolution_convert_fusion.1
  23.3 4.0 collective-permute-start.19
  28.2 3.3 collective-permute-start.22
  33.7 4.7 collective-permute-start.20
  38.8 4.1 collective-permute-done.20
  51.3 43.7 %collective-permute-done.28 = bf16[104,1024]{1,0:T(8,128)(2,1)S(1)} collective-permute-done((bf16[104,1024]{1,0:T(8,128)(2,1)}, bf16[104,1024]{1,0:T(8,128)(2,1)S(1)}, u32[]{:S(2)}, u32[]{:S(2)}) %collective-permute-start.28) | collective-permute-done | bytes 213024 | tf_op jit(solution)/shard_map/ppermute | solution.py:46
  95.0 4.1 collective-permute-start.12
  101.8 5.3 %collective-permute-start = (bf16[256,1024]{1,0:T(8,128)(2,1)S(1)}, bf16[256,1024]{1,0:T(8,128)(2,1)S(1)}, u32[]{:S(2)}, u32[]{:S(2)}) collective-permute-start(bf16[256,1024]{1,0:T(8,128)(2,1)S(1)} %copy-done.13), channel_id=1, source_target_pairs={{0,4},{1,5},{2,6},{3,7},{4,8},{5,9},{6,10},{7,11},{8,12},{9,13},{1... | collective-permute-start | bytes 1572872 | tf_op jit(solution)/shard_map/ppermute | solution.py:43
  107.2 6.5 %multiply_convert_fusion = bf16[512,8192]{1,0:T(8,128)(2,1)S(1)} fusion(bf16[416,512]{1,0:T(8,128)(2,1)S(1)} %fusion.26, bf16[104,8192]{1,0:T(8,128)(2,1)} %collective-permute-done.11, bf16[104,8192]{1,0:T(8,128)(2,1)} %collective-permute-done.10, bf16[104,8192]{1,0:T(8,128)(2,1)} %collective-permute-done.9, bf16[104,8192]{1,0:T(8,128)(2,1)S(1)} %convolution_convert_fusion.3), kind=kOutput, calls=%fused_computation.1 | convolution fusion | flops 3525312512 | bytes 15630336 | tf_op jit(solution)/shard_map/dot_general | solution.py:13
  122.2 30.2 %collective-permute-done = bf16[256,1024]{1,0:T(8,128)(2,1)S(1)} collective-permute-done((bf16[256,1024]{1,0:T(8,128)(2,1)S(1)}, bf16[256,1024]{1,0:T(8,128)(2,1)S(1)}, u32[]{:S(2)}, u32[]{:S(2)}) %collective-permute-start) | collective-permute-done | bytes 524320 | tf_op jit(solution)/shard_map/ppermute | solution.py:43
  153.2 4.4 collective-permute-start.1
  158.5 3.6 collective-permute-start.4
  162.1 5.1 %collective-permute-done.1 = bf16[256,1024]{1,0:T(8,128)(2,1)S(1)} collective-permute-done((bf16[256,1024]{1,0:T(8,128)(2,1)S(1)}, bf16[256,1024]{1,0:T(8,128)(2,1)S(1)}, u32[]{:S(2)}, u32[]{:S(2)}) %collective-permute-start.1) | collective-permute-done | bytes 524320 | tf_op jit(solution)/shard_map/ppermute | solution.py:43
  167.3 3.2 collective-permute-start.2
  172.3 4.0 collective-permute-done.2
  181.8 5.8 %collective-permute-start.13 = (bf16[128,8192]{1,0:T(8,128)(2,1)}, bf16[128,8192]{1,0:T(8,128)(2,1)}, u32[]{:S(2)}, u32[]{:S(2)}) collective-permute-start(bf16[128,8192]{1,0:T(8,128)(2,1)} %collective-permute-done.12), channel_id=1, source_target_pairs={{4,8},{5,9},{6,10},{7,11},{8,12},{9,13},{10,14},{11,15},{20,24},{2... | collective-permute-start | bytes 6291464 | tf_op jit(solution)/shard_map/ppermute | solution.py:43
  187.7 6.7 %collective-permute-start.16 = (bf16[128,8192]{1,0:T(8,128)(2,1)}, bf16[128,8192]{1,0:T(8,128)(2,1)}, u32[]{:S(2)}, u32[]{:S(2)}) collective-permute-start(bf16[128,8192]{1,0:T(8,128)(2,1)} %collective-permute-done.15), channel_id=1, source_target_pairs={{4,0},{5,1},{6,2},{7,3},{8,4},{9,5},{10,6},{11,7},{20,16},{21,17},... | collective-permute-start | bytes 6291464 | tf_op jit(solution)/shard_map/ppermute | solution.py:43
  194.4 4.0 fusion.19
  199.7 36.9 %collective-permute-done.13 = bf16[128,8192]{1,0:T(8,128)(2,1)} collective-permute-done((bf16[128,8192]{1,0:T(8,128)(2,1)}, bf16[128,8192]{1,0:T(8,128)(2,1)}, u32[]{:S(2)}, u32[]{:S(2)}) %collective-permute-start.13) | collective-permute-done | bytes 2097184 | tf_op jit(solution)/shard_map/ppermute | solution.py:43
  238.1 4.2 maximum_select_fusion
  244.4 32.5 %collective-permute-done.34 = bf16[128,8192]{1,0:T(8,128)(2,1)} collective-permute-done((bf16[128,8192]{1,0:T(8,128)(2,1)}, bf16[128,8192]{1,0:T(8,128)(2,1)}, u32[]{:S(2)}, u32[]{:S(2)}) %collective-permute-start.34) | collective-permute-done | bytes 2097184 | tf_op jit(solution)/shard_map/ppermute | solution.py:43
  276.9 7.1 %fusion.20 = (bf16[128,8192]{1,0:T(8,128)(2,1)}, bf16[128,8192]{1,0:T(8,128)(2,1)}) fusion(bf16[128,8192]{1,0:T(8,128)(2,1)} %collective-permute-done.34, bf16[4,128,8192]{2,1,0:T(8,128)(2,1)} %bitcast.97, s32[]{:T(128)S(6)} %select_n.179, bf16[128,8192]{1,0:T(8,128)(2,1)} %collective-permute-done.36, s32[]{:T(128)S(6)} %max.13), kind=kLoop, calls=%fused_computation.40 | loop fusion | flops 8388608 | bytes 12582920 | tf_op jit(solution)/shard_map/convert_element_type | solution.py:67
  287.5 3.1 constant_dynamic-update-slice_fusion.12
  290.6 3.1 constant_dynamic-update-slice_fusion.11
  293.7 3.1 constant_dynamic-update-slice_fusion.10
  296.8 3.1 constant_dynamic-update-slice_fusion.9
  299.9 3.2 constant_dynamic-update-slice_fusion.8
  304.7 12.0 %fusion.27 = bf16[416,512]{1,0:T(8,128)(2,1)} fusion(bf16[896,8192]{1,0:T(8,128)(2,1)} %constant_dynamic-update-slice_fusion.7, s32[]{:T(128)S(6)} %select_n.175, s32[512]{0:T(512)S(1)} %add_select_fusion, s32[416]{0:T(512)S(1)} %add_select_fusion.1, bf16[104,8192]{1,0:T(8,128)(2,1)} %collective-permute-done.11, ...), kind=kOutput, calls=%fused_computation.51 | convolution fusion | flops 3517562880 | bytes 15634052 | tf_op jit(solution)/shard_map/dot_general | solution.py:13
  319.6 6.2 %collective-permute-done.7 = bf16[4,2,1,256,1024]{4,3,2,1,0:T(8,128)(2,1)} collective-permute-done((bf16[4,2,1,256,1024]{4,3,2,1,0:T(8,128)(2,1)S(1)}, bf16[4,2,1,256,1024]{4,3,2,1,0:T(8,128)(2,1)}, u32[]{:S(2)}, u32[]{:S(2)}) %collective-permute-start.7) | collective-permute-done | bytes 4194336 | tf_op jit(solution)/shard_map/ppermute | solution.py:146
  325.8 9.9 %fusion.5 = bf16[4,2,2,256,1024]{4,3,2,1,0:T(8,128)(2,1)} fusion(s32[]{:T(128)S(6)} %select_n.165, bf16[4,2,1,256,1024]{4,3,2,1,0:T(8,128)(2,1)} %collective-permute-done.7, bf16[4,2,1,256,1024]{4,3,2,1,0:T(8,128)(2,1)S(1)} %maximum_select_fusion), kind=kLoop, calls=%fused_computation.17 | loop fusion | flops 8388608 | bytes 16777220 | tf_op jit(solution)/shard_map/concatenate | solution.py:149
  335.7 7.5 %multiply_convert_fusion.1 = bf16[416,8192]{1,0:T(8,128)(2,1)S(1)} fusion(bf16[416,512]{1,0:T(8,128)(2,1)S(1)} %copy-done.30, bf16[896,8192]{1,0:T(8,128)(2,1)} %constant_dynamic-update-slice_fusion.7, s32[]{:T(128)S(6)} %select_n.175), kind=kOutput, calls=%fused_computation.2 | convolution fusion | flops 3496476672 | bytes 15630340 | tf_op jit(solution)/shard_map/dot_general | solution.py:13
  347.0 6.6 %collective-permute-done.42 = bf16[128,1024]{1,0:T(8,128)(2,1)S(1)} collective-permute-done((bf16[128,1024]{1,0:T(8,128)(2,1)S(1)}, bf16[128,1024]{1,0:T(8,128)(2,1)S(1)}, u32[]{:S(2)}, u32[]{:S(2)}) %collective-permute-start.42) | collective-permute-done | bytes 262176 | tf_op jit(solution)/shard_map/ppermute | solution.py:43
  357.2 3.9 collective-permute-start.41
  365.3 6.0 %collective-permute-done.25 = bf16[104,1024]{1,0:T(8,128)(2,1)S(1)} collective-permute-done((bf16[104,1024]{1,0:T(8,128)(2,1)S(1)}, bf16[104,1024]{1,0:T(8,128)(2,1)S(1)}, u32[]{:S(2)}, u32[]{:S(2)}) %collective-permute-start.25) | collective-permute-done | bytes 213024 | tf_op jit(solution)/shard_map/ppermute | solution.py:46
  377.9 4.1 fusion.18
  382.0 3.6 collective-permute-done.44
  388.8 3.9 collective-permute-start.38
  392.8 2.8 fusion.34
  398.0 15.8 %collective-permute-done.31 = bf16[104,8192]{1,0:T(8,128)(2,1)} collective-permute-done((bf16[104,8192]{1,0:T(8,128)(2,1)}, bf16[104,8192]{1,0:T(8,128)(2,1)}, u32[]{:S(2)}, u32[]{:S(2)}) %collective-permute-start.31) | collective-permute-done | bytes 1703968 | tf_op jit(solution)/shard_map/ppermute | solution.py:46
  413.8 36.1 %collective-permute-done.32 = bf16[104,8192]{1,0:T(8,128)(2,1)} collective-permute-done((bf16[104,8192]{1,0:T(8,128)(2,1)}, bf16[104,8192]{1,0:T(8,128)(2,1)}, u32[]{:S(2)}, u32[]{:S(2)}) %collective-permute-start.32) | collective-permute-done | bytes 1703968 | tf_op jit(solution)/shard_map/ppermute | solution.py:46
  449.9 7.0 %fusion.9 = f32[256,8192]{0,1:T(8,128)} fusion(bf16[104,8192]{1,0:T(8,128)(2,1)} %collective-permute-done.32, bf16[104,8192]{1,0:T(8,128)(2,1)} %collective-permute-done.31, bf16[104,8192]{1,0:T(8,128)(2,1)S(1)} %copy-done.19, bf16[104,8192]{1,0:T(8,128)(2,1)S(1)} %copy-done.10, s32[256]{0:T(256)S(1)} %add_add_fusion), kind=kOutput, calls=%fused_computation.24 | convolution fusion | flops 1772199936 | bytes 15205376 | tf_op jit(solution)/shard_map/dot_general | solution.py:13
  456.9 6.2 %fusion.3 = f32[128,8192]{1,0:T(8,128)} fusion(bf16[128,8192]{1,0:T(8,128)(2,1)} %collective-permute-done.38, bf16[128,8192]{1,0:T(8,128)(2,1)} %collective-permute-done.35, bf16[416,512]{1,0:T(8,128)(2,1)} %copy-done.29, s32[]{:T(128)S(6)} %select_n.178, bf16[104,8192]{1,0:T(8,128)(2,1)} %collective-permute-done.11, ...), kind=kOutput, calls=%fused_computation.11 | convolution fusion | flops 904921088 | bytes 15310852 | tf_op jit(solution)/shard_map/dot_general | solution.py:13
  463.1 10.4 %select_bitcast_fusion.1 = (bf16[4,2,1,2,256,1024]{5,4,3,2,1,0:T(8,128)(2,1)S(1)}, bf16[4,2,1,2,256,1024]{5,4,3,2,1,0:T(8,128)(2,1)S(1)}) fusion(bf16[4,2,2,256,1024]{4,3,2,1,0:T(8,128)(2,1)} %collective-permute-done.8, pred[]{:T(512)S(6)} %eq.73, s32[]{:T(128)S(6)} %select_n.165, bf16[4,2,1,256,1024]{4,3,2,1,0:T(8,128)(2,1)} %collective-permute-done.7, ...), kind=kLoop, calls=%fused_computation.19 | loop fusion | flops 16777216 | bytes 33554436 | tf_op jit(solution)/shard_map/stack | solution.py:154
  473.5 6.9 %pad_maximum_fusion = bf16[4,2,2,2,256,1024]{5,4,3,2,1,0:T(8,128)(2,1)} fusion(bf16[4,2,1,2,256,1024]{5,4,3,2,1,0:T(8,128)(2,1)S(1)} %get-tuple-element.15, bf16[4,2,1,2,256,1024]{5,4,3,2,1,0:T(8,128)(2,1)S(1)} %get-tuple-element.14), kind=kLoop, calls=%fused_computation | loop fusion | flops 8388608 | bytes 33554432 | tf_op jit(solution)/shard_map/stack | solution.py:154
  480.4 14.7 %fusion.1 = bf16[256,8192]{0,1:T(8,128)(2,1)} fusion(f32[256,8192]{0,1:T(8,128)} %fusion.9, bf16[8192,1024]{1,0:T(8,128)(2,1)} %bitcast.99, bf16[256,1024]{1,0:T(8,128)(2,1)S(1)} %copy-done), kind=kOutput, calls=%fused_computation.8 | convolution fusion | flops 4299161600 | bytes 29884416 | tf_op jit(solution)/shard_map/dot_general | solution.py:13
  495.1 6.6 %copy.20 = bf16[256,8192]{1,0:T(8,128)(2,1)} copy(bf16[256,8192]{0,1:T(8,128)(2,1)} %fusion.1) | data formatting | bytes 8388608
  501.8 11.5 %fusion.22 = bf16[256,1024]{0,1:T(8,128)(2,1)S(1)} fusion(f32[256,1024]{0,1:T(8,128)S(1)} %copy-done.28, bf16[8192,1024]{1,0:T(8,128)(2,1)} %bitcast.100, bf16[256,8192]{1,0:T(8,128)(2,1)} %param.7), kind=kOutput, calls=%fused_computation.48 | convolution fusion | flops 4295491584 | bytes 22544384 | tf_op jit(solution)/shard_map/dot_general | solution.py:13
  (173 shorter events, 83.6 us)
Async XLA Ops:
  0.6 22.6 %collective-permute-start.18 = (bf16[128,1024]{1,0:T(8,128)(2,1)}, bf16[128,1024]{1,0:T(8,128)(2,1)}, u32[]{:S(2)}, u32[]{:S(2)}) collective-permute-start(bf16[128,1024]{1,0:T(8,128)(2,1)} %bitcast.107), channel_id=1, source_target_pairs={{0,4},{1,5},{2,6},{3,7},{4,8},{5,9},{6,10},{7,11},{8,12},{9,13},{1... | collective-permute-start | bytes 786440 | tf_op jit(solution)/shard_map/ppermute | solution.py:43
  4.3 23.9 %collective-permute-start.21 = (bf16[128,1024]{1,0:T(8,128)(2,1)}, bf16[128,1024]{1,0:T(8,128)(2,1)}, u32[]{:S(2)}, u32[]{:S(2)}) collective-permute-start(bf16[128,1024]{1,0:T(8,128)(2,1)} %bitcast.108), channel_id=1, source_target_pairs={{4,0},{5,1},{6,2},{7,3},{8,4},{9,5},{10,6},{11,7},{12,8},{13,9},{1... | collective-permute-start | bytes 786440 | tf_op jit(solution)/shard_map/ppermute | solution.py:43
  13.6 88.2 %collective-permute-start.10 = (bf16[104,8192]{1,0:T(8,128)(2,1)}, bf16[104,8192]{1,0:T(8,128)(2,1)}, u32[]{:S(2)}, u32[]{:S(2)}) collective-permute-start(bf16[104,8192]{1,0:T(8,128)(2,1)} %convolution_convert_fusion.1), channel_id=1, source_target_pairs={{0,2},{1,3},{2,0},{3,1},{4,6},{5,7},{6,4},{7,5},{8,10},{9,11},{10,... | collective-permute-start | bytes 5111816 | tf_op jit(solution)/shard_map/ppermute | solution.py:46
  16.9 90.2 %collective-permute-start.11 = (bf16[104,8192]{1,0:T(8,128)(2,1)}, bf16[104,8192]{1,0:T(8,128)(2,1)}, u32[]{:S(2)}, u32[]{:S(2)}) collective-permute-start(bf16[104,8192]{1,0:T(8,128)(2,1)} %convolution_convert_fusion), channel_id=1, source_target_pairs={{0,3},{1,2},{2,1},{3,0},{4,7},{5,6},{6,5},{7,4},{8,11},{9,10},{10,... | collective-permute-start | bytes 5111816 | tf_op jit(solution)/shard_map/ppermute | solution.py:46
  18.9 88.3 %collective-permute-start.9 = (bf16[104,8192]{1,0:T(8,128)(2,1)}, bf16[104,8192]{1,0:T(8,128)(2,1)}, u32[]{:S(2)}, u32[]{:S(2)}) collective-permute-start(bf16[104,8192]{1,0:T(8,128)(2,1)} %convolution_convert_fusion.2), channel_id=1, source_target_pairs={{0,1},{1,0},{2,3},{3,2},{4,5},{5,4},{6,7},{7,6},{8,9},{9,8},{10,11... | collective-permute-start | bytes 5111816 | tf_op jit(solution)/shard_map/ppermute | solution.py:46
  20.4 86.7 %copy-start.7 = (bf16[104,8192]{1,0:T(8,128)(2,1)}, bf16[104,8192]{1,0:T(8,128)(2,1)S(1)}, u32[]{:S(2)}) copy-start(bf16[104,8192]{1,0:T(8,128)(2,1)S(1)} %convolution_convert_fusion.3) | copy-start | bytes 5111812
  23.3 10.4 %collective-permute-start.19 = (bf16[128,1024]{1,0:T(8,128)(2,1)}, bf16[128,1024]{1,0:T(8,128)(2,1)}, u32[]{:S(2)}, u32[]{:S(2)}) collective-permute-start(bf16[128,1024]{1,0:T(8,128)(2,1)} %collective-permute-done.18), channel_id=1, source_target_pairs={{4,8},{5,9},{6,10},{7,11},{8,12},{9,13},{10,14},{11,15},{20,24},{2... | collective-permute-start | bytes 786440 | tf_op jit(solution)/shard_map/ppermute | solution.py:43
  28.2 10.5 %collective-permute-start.22 = (bf16[128,1024]{1,0:T(8,128)(2,1)}, bf16[128,1024]{1,0:T(8,128)(2,1)}, u32[]{:S(2)}, u32[]{:S(2)}) collective-permute-start(bf16[128,1024]{1,0:T(8,128)(2,1)} %collective-permute-done.21), channel_id=1, source_target_pairs={{4,0},{5,1},{6,2},{7,3},{8,4},{9,5},{10,6},{11,7},{20,16},{21,17},... | collective-permute-start | bytes 786440 | tf_op jit(solution)/shard_map/ppermute | solution.py:43
  33.7 9.2 %collective-permute-start.20 = (bf16[128,1024]{1,0:T(8,128)(2,1)}, bf16[128,1024]{1,0:T(8,128)(2,1)}, u32[]{:S(2)}, u32[]{:S(2)}) collective-permute-start(bf16[128,1024]{1,0:T(8,128)(2,1)} %collective-permute-done.19), channel_id=1, source_target_pairs={{8,12},{9,13},{10,14},{11,15},{24,28},{25,29},{26,30},{27,31}} | collective-permute-start | bytes 786440 | tf_op jit(solution)/shard_map/ppermute | solution.py:43
  38.7 9.8 %collective-permute-start.27 = (bf16[104,1024]{1,0:T(8,128)(2,1)}, bf16[104,1024]{1,0:T(8,128)(2,1)S(1)}, u32[]{:S(2)}, u32[]{:S(2)}) collective-permute-start(bf16[104,1024]{1,0:T(8,128)(2,1)} %convolution_convert_fusion.6), channel_id=1, source_target_pairs={{0,1},{1,0},{2,3},{3,2},{4,5},{5,4},{6,7},{7,6},{8,9},{9,8},{10,11... | collective-permute-start | bytes 638984 | tf_op jit(solution)/shard_map/ppermute | solution.py:46
  42.9 7.4 %collective-permute-start.23 = (bf16[128,1024]{1,0:T(8,128)(2,1)}, bf16[128,1024]{1,0:T(8,128)(2,1)S(1)}, u32[]{:S(2)}, u32[]{:S(2)}) collective-permute-start(bf16[128,1024]{1,0:T(8,128)(2,1)} %collective-permute-done.22), channel_id=1, source_target_pairs={{4,0},{5,1},{6,2},{7,3},{20,16},{21,17},{22,18},{23,19}} | collective-permute-start | bytes 786440 | tf_op jit(solution)/shard_map/ppermute | solution.py:43
  48.5 65.1 %copy-start.21 = (bf16[104,1024]{1,0:T(8,128)(2,1)}, bf16[104,1024]{1,0:T(8,128)(2,1)S(1)}, u32[]{:S(2)}) copy-start(bf16[104,1024]{1,0:T(8,128)(2,1)S(1)} %collective-permute-done.27) | copy-start | bytes 638980
  48.6 46.5 %collective-permute-start.28 = (bf16[104,1024]{1,0:T(8,128)(2,1)}, bf16[104,1024]{1,0:T(8,128)(2,1)S(1)}, u32[]{:S(2)}, u32[]{:S(2)}) collective-permute-start(bf16[104,1024]{1,0:T(8,128)(2,1)} %convolution_convert_fusion.5), channel_id=1, source_target_pairs={{0,2},{1,3},{2,0},{3,1},{4,6},{5,7},{6,4},{7,5},{8,10},{9,11},{10,... | collective-permute-start | bytes 638984 | tf_op jit(solution)/shard_map/ppermute | solution.py:46
  50.3 48.9 %collective-permute-start.29 = (bf16[104,1024]{1,0:T(8,128)(2,1)}, bf16[104,1024]{1,0:T(8,128)(2,1)S(1)}, u32[]{:S(2)}, u32[]{:S(2)}) collective-permute-start(bf16[104,1024]{1,0:T(8,128)(2,1)} %convolution_convert_fusion.4), channel_id=1, source_target_pairs={{0,3},{1,2},{2,1},{3,0},{4,7},{5,6},{6,5},{7,4},{8,11},{9,10},{10,... | collective-permute-start | bytes 638984 | tf_op jit(solution)/shard_map/ppermute | solution.py:46
  95.0 86.8 %collective-permute-start.12 = (bf16[128,8192]{1,0:T(8,128)(2,1)}, bf16[128,8192]{1,0:T(8,128)(2,1)}, u32[]{:S(2)}, u32[]{:S(2)}) collective-permute-start(bf16[128,8192]{1,0:T(8,128)(2,1)} %bitcast.10), channel_id=1, source_target_pairs={{0,4},{1,5},{2,6},{3,7},{4,8},{5,9},{6,10},{7,11},{8,12},{9,13},{1... | collective-permute-start | bytes 6291464 | tf_op jit(solution)/shard_map/ppermute | solution.py:43
  99.2 88.5 %collective-permute-start.15 = (bf16[128,8192]{1,0:T(8,128)(2,1)}, bf16[128,8192]{1,0:T(8,128)(2,1)}, u32[]{:S(2)}, u32[]{:S(2)}) collective-permute-start(bf16[128,8192]{1,0:T(8,128)(2,1)} %bitcast.10), channel_id=1, source_target_pairs={{4,0},{5,1},{6,2},{7,3},{8,4},{9,5},{10,6},{11,7},{12,8},{13,9},{1... | collective-permute-start | bytes 6291464 | tf_op jit(solution)/shard_map/ppermute | solution.py:43
  101.8 50.6 %collective-permute-start = (bf16[256,1024]{1,0:T(8,128)(2,1)S(1)}, bf16[256,1024]{1,0:T(8,128)(2,1)S(1)}, u32[]{:S(2)}, u32[]{:S(2)}) collective-permute-start(bf16[256,1024]{1,0:T(8,128)(2,1)S(1)} %copy-done.13), channel_id=1, source_target_pairs={{0,4},{1,5},{2,6},{3,7},{4,8},{5,9},{6,10},{7,11},{8,12},{9,13},{1... | collective-permute-start | bytes 1572872 | tf_op jit(solution)/shard_map/ppermute | solution.py:43
  118.2 76.2 %collective-permute-start.33 = (bf16[128,8192]{1,0:T(8,128)(2,1)}, bf16[128,8192]{1,0:T(8,128)(2,1)}, u32[]{:S(2)}, u32[]{:S(2)}) collective-permute-start(bf16[128,8192]{1,0:T(8,128)(2,1)} %get-tuple-element.18), channel_id=1, source_target_pairs={{0,4},{1,5},{2,6},{3,7},{16,20},{17,21},{18,22},{19,23}} | collective-permute-start | bytes 6291464 | tf_op jit(solution)/shard_map/ppermute | solution.py:43
  120.3 38.2 %collective-permute-start.3 = (bf16[256,1024]{1,0:T(8,128)(2,1)S(1)}, bf16[256,1024]{1,0:T(8,128)(2,1)S(1)}, u32[]{:S(2)}, u32[]{:S(2)}) collective-permute-start(bf16[256,1024]{1,0:T(8,128)(2,1)S(1)} %copy-done.13), channel_id=1, source_target_pairs={{4,0},{5,1},{6,2},{7,3},{8,4},{9,5},{10,6},{11,7},{12,8},{13,9},{1... | collective-permute-start | bytes 1572872 | tf_op jit(solution)/shard_map/ppermute | solution.py:43
  153.2 14.1 %collective-permute-start.1 = (bf16[256,1024]{1,0:T(8,128)(2,1)S(1)}, bf16[256,1024]{1,0:T(8,128)(2,1)S(1)}, u32[]{:S(2)}, u32[]{:S(2)}) collective-permute-start(bf16[256,1024]{1,0:T(8,128)(2,1)S(1)} %collective-permute-done), channel_id=1, source_target_pairs={{4,8},{5,9},{6,10},{7,11},{8,12},{9,13},{10,14},{11,15},{20,24},{2... | collective-permute-start | bytes 1572872 | tf_op jit(solution)/shard_map/ppermute | solution.py:43
  158.5 13.2 %collective-permute-start.4 = (bf16[256,1024]{1,0:T(8,128)(2,1)S(1)}, bf16[256,1024]{1,0:T(8,128)(2,1)S(1)}, u32[]{:S(2)}, u32[]{:S(2)}) collective-permute-start(bf16[256,1024]{1,0:T(8,128)(2,1)S(1)} %collective-permute-done.3), channel_id=1, source_target_pairs={{4,0},{5,1},{6,2},{7,3},{8,4},{9,5},{10,6},{11,7},{20,16},{21,17},... | collective-permute-start | bytes 1572872 | tf_op jit(solution)/shard_map/ppermute | solution.py:43
  167.3 9.1 %collective-permute-start.2 = (bf16[256,1024]{1,0:T(8,128)(2,1)S(1)}, bf16[256,1024]{1,0:T(8,128)(2,1)}, u32[]{:S(2)}, u32[]{:S(2)}) collective-permute-start(bf16[256,1024]{1,0:T(8,128)(2,1)S(1)} %collective-permute-done.1), channel_id=1, source_target_pairs={{8,12},{9,13},{10,14},{11,15},{24,28},{25,29},{26,30},{27,31}} | collective-permute-start | bytes 1572872 | tf_op jit(solution)/shard_map/ppermute | solution.py:43
  171.6 7.0 %collective-permute-start.5 = (bf16[256,1024]{1,0:T(8,128)(2,1)S(1)}, bf16[256,1024]{1,0:T(8,128)(2,1)S(1)}, u32[]{:S(2)}, u32[]{:S(2)}) collective-permute-start(bf16[256,1024]{1,0:T(8,128)(2,1)S(1)} %collective-permute-done.4), channel_id=1, source_target_pairs={{4,0},{5,1},{6,2},{7,3},{20,16},{21,17},{22,18},{23,19}} | collective-permute-start | bytes 1572872 | tf_op jit(solution)/shard_map/ppermute | solution.py:43
  178.9 59.1 %collective-permute-start.6 = (bf16[4,1,1,256,1024]{4,3,2,1,0:T(8,128)(2,1)S(1)}, bf16[4,1,1,256,1024]{4,3,2,1,0:T(8,128)(2,1)}, u32[]{:S(2)}, u32[]{:S(2)}) collective-permute-start(bf16[4,1,1,256,1024]{4,3,2,1,0:T(8,128)(2,1)S(1)} %bitcast.101), channel_id=1, source_target_pairs={{0,2},{1,3},{2,0},{3,1},{4,6},{5,7},{6,4},{7,5},{8,10},{9,11},{10,... | collective-permute-start | bytes 6291464 | tf_op jit(solution)/shard_map/ppermute | solution.py:46
  180.5 63.9 %collective-permute-start.36 = (bf16[128,8192]{1,0:T(8,128)(2,1)}, bf16[128,8192]{1,0:T(8,128)(2,1)}, u32[]{:S(2)}, u32[]{:S(2)}) collective-permute-start(bf16[128,8192]{1,0:T(8,128)(2,1)} %get-tuple-element.19), channel_id=1, source_target_pairs={{12,8},{13,9},{14,10},{15,11},{28,24},{29,25},{30,26},{31,27}} | collective-permute-start | bytes 6291464 | tf_op jit(solution)/shard_map/ppermute | solution.py:43
  181.8 54.8 %collective-permute-start.13 = (bf16[128,8192]{1,0:T(8,128)(2,1)}, bf16[128,8192]{1,0:T(8,128)(2,1)}, u32[]{:S(2)}, u32[]{:S(2)}) collective-permute-start(bf16[128,8192]{1,0:T(8,128)(2,1)} %collective-permute-done.12), channel_id=1, source_target_pairs={{4,8},{5,9},{6,10},{7,11},{8,12},{9,13},{10,14},{11,15},{20,24},{2... | collective-permute-start | bytes 6291464 | tf_op jit(solution)/shard_map/ppermute | solution.py:43
  187.7 55.8 %collective-permute-start.16 = (bf16[128,8192]{1,0:T(8,128)(2,1)}, bf16[128,8192]{1,0:T(8,128)(2,1)}, u32[]{:S(2)}, u32[]{:S(2)}) collective-permute-start(bf16[128,8192]{1,0:T(8,128)(2,1)} %collective-permute-done.15), channel_id=1, source_target_pairs={{4,0},{5,1},{6,2},{7,3},{8,4},{9,5},{10,6},{11,7},{20,16},{21,17},... | collective-permute-start | bytes 6291464 | tf_op jit(solution)/shard_map/ppermute | solution.py:43
  198.4 78.5 %collective-permute-start.34 = (bf16[128,8192]{1,0:T(8,128)(2,1)}, bf16[128,8192]{1,0:T(8,128)(2,1)}, u32[]{:S(2)}, u32[]{:S(2)}) collective-permute-start(bf16[128,8192]{1,0:T(8,128)(2,1)} %fusion.19), channel_id=1, source_target_pairs={{0,4},{1,5},{2,6},{3,7},{4,8},{5,9},{6,10},{7,11},{16,20},{17,21},... | collective-permute-start | bytes 6291464 | tf_op jit(solution)/shard_map/ppermute | solution.py:43
  236.6 49.3 %collective-permute-start.14 = (bf16[128,8192]{1,0:T(8,128)(2,1)}, bf16[128,8192]{1,0:T(8,128)(2,1)S(1)}, u32[]{:S(2)}, u32[]{:S(2)}) collective-permute-start(bf16[128,8192]{1,0:T(8,128)(2,1)} %collective-permute-done.13), channel_id=1, source_target_pairs={{8,12},{9,13},{10,14},{11,15},{24,28},{25,29},{26,30},{27,31}} | collective-permute-start | bytes 6291464 | tf_op jit(solution)/shard_map/ppermute | solution.py:43
  242.3 83.5 %copy-start.2 = (bf16[4,2,1,256,1024]{4,3,2,1,0:T(8,128)(2,1)}, bf16[4,2,1,256,1024]{4,3,2,1,0:T(8,128)(2,1)S(1)}, u32[]{:S(2)}) copy-start(bf16[4,2,1,256,1024]{4,3,2,1,0:T(8,128)(2,1)S(1)} %maximum_select_fusion) | copy-start | bytes 12582916
  242.3 83.5 %collective-permute-start.7 = (bf16[4,2,1,256,1024]{4,3,2,1,0:T(8,128)(2,1)S(1)}, bf16[4,2,1,256,1024]{4,3,2,1,0:T(8,128)(2,1)}, u32[]{:S(2)}, u32[]{:S(2)}) collective-permute-start(bf16[4,2,1,256,1024]{4,3,2,1,0:T(8,128)(2,1)S(1)} %maximum_select_fusion), channel_id=1, source_target_pairs={{0,16},{16,0},{1,17},{17,1},{2,18},{18,2},{3,19},{19,3},{4,20},{20... | collective-permute-start | bytes 12582920 | tf_op jit(solution)/shard_map/ppermute | solution.py:146
  243.5 59.7 %collective-permute-start.17 = (bf16[128,8192]{1,0:T(8,128)(2,1)}, bf16[128,8192]{1,0:T(8,128)(2,1)S(1)}, u32[]{:S(2)}, u32[]{:S(2)}) collective-permute-start(bf16[128,8192]{1,0:T(8,128)(2,1)} %collective-permute-done.16), channel_id=1, source_target_pairs={{4,0},{5,1},{6,2},{7,3},{20,16},{21,17},{22,18},{23,19}} | collective-permute-start | bytes 6291464 | tf_op jit(solution)/shard_map/ppermute | solution.py:43
  284.0 91.5 %collective-permute-start.37 = (bf16[128,8192]{1,0:T(8,128)(2,1)}, bf16[128,8192]{1,0:T(8,128)(2,1)}, u32[]{:S(2)}, u32[]{:S(2)}) collective-permute-start(bf16[128,8192]{1,0:T(8,128)(2,1)} %get-tuple-element.17), channel_id=1, source_target_pairs={{8,4},{9,5},{10,6},{11,7},{12,8},{13,9},{14,10},{15,11},{24,20},{2... | collective-permute-start | bytes 6291464 | tf_op jit(solution)/shard_map/ppermute | solution.py:43
  318.7 25.8 %collective-permute-start.39 = (bf16[128,1024]{1,0:T(8,128)(2,1)S(1)}, bf16[128,1024]{1,0:T(8,128)(2,1)S(1)}, u32[]{:S(2)}, u32[]{:S(2)}) collective-permute-start(bf16[128,1024]{1,0:T(8,128)(2,1)S(1)} %get-tuple-element.26), channel_id=1, source_target_pairs={{0,4},{1,5},{2,6},{3,7},{16,20},{17,21},{18,22},{19,23}} | collective-permute-start | bytes 786440 | tf_op jit(solution)/shard_map/ppermute | solution.py:43
  335.7 127.4 %collective-permute-start.8 = (bf16[4,2,2,256,1024]{4,3,2,1,0:T(8,128)(2,1)}, bf16[4,2,2,256,1024]{4,3,2,1,0:T(8,128)(2,1)}, u32[]{:S(2)}, u32[]{:S(2)}) collective-permute-start(bf16[4,2,2,256,1024]{4,3,2,1,0:T(8,128)(2,1)} %fusion.5), channel_id=1, source_target_pairs={{0,1},{1,0},{2,3},{3,2},{4,5},{5,4},{6,7},{7,6},{8,9},{9,8},{10,11... | collective-permute-start | bytes 25165832 | tf_op jit(solution)/shard_map/ppermute | solution.py:46
  343.2 10.4 %collective-permute-start.42 = (bf16[128,1024]{1,0:T(8,128)(2,1)S(1)}, bf16[128,1024]{1,0:T(8,128)(2,1)S(1)}, u32[]{:S(2)}, u32[]{:S(2)}) collective-permute-start(bf16[128,1024]{1,0:T(8,128)(2,1)S(1)} %get-tuple-element.27), channel_id=1, source_target_pairs={{12,8},{13,9},{14,10},{15,11},{28,24},{29,25},{30,26},{31,27}} | collective-permute-start | bytes 786440 | tf_op jit(solution)/shard_map/ppermute | solution.py:43
  344.6 10.4 %collective-permute-start.40 = (bf16[128,1024]{1,0:T(8,128)(2,1)S(1)}, bf16[128,1024]{1,0:T(8,128)(2,1)S(1)}, u32[]{:S(2)}, u32[]{:S(2)}) collective-permute-start(bf16[128,1024]{1,0:T(8,128)(2,1)S(1)} %fusion.44), channel_id=1, source_target_pairs={{0,4},{1,5},{2,6},{3,7},{4,8},{5,9},{6,10},{7,11},{16,20},{17,21},... | collective-permute-start | bytes 786440 | tf_op jit(solution)/shard_map/ppermute | solution.py:43
  346.6 17.0 %collective-permute-start.24 = (bf16[104,1024]{1,0:T(8,128)(2,1)S(1)}, bf16[104,1024]{1,0:T(8,128)(2,1)S(1)}, u32[]{:S(2)}, u32[]{:S(2)}) collective-permute-start(bf16[104,1024]{1,0:T(8,128)(2,1)S(1)} %get-tuple-element.31), channel_id=1, source_target_pairs={{0,1},{1,0},{2,3},{3,2},{4,5},{5,4},{6,7},{7,6},{8,9},{9,8},{10,11... | collective-permute-start | bytes 638984 | tf_op jit(solution)/shard_map/ppermute | solution.py:46
  355.2 10.0 %collective-permute-start.43 = (bf16[128,1024]{1,0:T(8,128)(2,1)S(1)}, bf16[128,1024]{1,0:T(8,128)(2,1)S(1)}, u32[]{:S(2)}, u32[]{:S(2)}) collective-permute-start(bf16[128,1024]{1,0:T(8,128)(2,1)S(1)} %get-tuple-element.25), channel_id=1, source_target_pairs={{8,4},{9,5},{10,6},{11,7},{12,8},{13,9},{14,10},{15,11},{24,20},{2... | collective-permute-start | bytes 786440 | tf_op jit(solution)/shard_map/ppermute | solution.py:43
  357.2 16.7 %collective-permute-start.41 = (bf16[128,1024]{1,0:T(8,128)(2,1)S(1)}, bf16[128,1024]{1,0:T(8,128)(2,1)S(1)}, u32[]{:S(2)}, u32[]{:S(2)}) collective-permute-start(bf16[128,1024]{1,0:T(8,128)(2,1)S(1)} %get-tuple-element.24), channel_id=1, source_target_pairs={{0,4},{1,5},{2,6},{3,7},{4,8},{5,9},{6,10},{7,11},{8,12},{9,13},{1... | collective-permute-start | bytes 786440 | tf_op jit(solution)/shard_map/ppermute | solution.py:43
  363.6 7.7 %collective-permute-start.25 = (bf16[104,1024]{1,0:T(8,128)(2,1)S(1)}, bf16[104,1024]{1,0:T(8,128)(2,1)S(1)}, u32[]{:S(2)}, u32[]{:S(2)}) collective-permute-start(bf16[104,1024]{1,0:T(8,128)(2,1)S(1)} %get-tuple-element.30), channel_id=1, source_target_pairs={{0,2},{1,3},{2,0},{3,1},{4,6},{5,7},{6,4},{7,5},{8,10},{9,11},{10,... | collective-permute-start | bytes 638984 | tf_op jit(solution)/shard_map/ppermute | solution.py:46
  365.2 8.2 %collective-permute-start.26 = (bf16[104,1024]{1,0:T(8,128)(2,1)S(1)}, bf16[104,1024]{1,0:T(8,128)(2,1)S(1)}, u32[]{:S(2)}, u32[]{:S(2)}) collective-permute-start(bf16[104,1024]{1,0:T(8,128)(2,1)S(1)} %get-tuple-element.29), channel_id=1, source_target_pairs={{0,3},{1,2},{2,1},{3,0},{4,7},{5,6},{6,5},{7,4},{8,11},{9,10},{10,... | collective-permute-start | bytes 638984 | tf_op jit(solution)/shard_map/ppermute | solution.py:46
  371.3 16.2 %collective-permute-start.30 = (bf16[104,8192]{1,0:T(8,128)(2,1)S(1)}, bf16[104,8192]{1,0:T(8,128)(2,1)S(1)}, u32[]{:S(2)}, u32[]{:S(2)}) collective-permute-start(bf16[104,8192]{1,0:T(8,128)(2,1)S(1)} %get-tuple-element.23), channel_id=1, source_target_pairs={{0,1},{1,0},{2,3},{3,2},{4,5},{5,4},{6,7},{7,6},{8,9},{9,8},{10,11... | collective-permute-start | bytes 5111816 | tf_op jit(solution)/shard_map/ppermute | solution.py:46
  373.4 40.4 %collective-permute-start.31 = (bf16[104,8192]{1,0:T(8,128)(2,1)}, bf16[104,8192]{1,0:T(8,128)(2,1)}, u32[]{:S(2)}, u32[]{:S(2)}) collective-permute-start(bf16[104,8192]{1,0:T(8,128)(2,1)} %get-tuple-element.22), channel_id=1, source_target_pairs={{0,2},{1,3},{2,0},{3,1},{4,6},{5,7},{6,4},{7,5},{8,10},{9,11},{10,... | collective-permute-start | bytes 5111816 | tf_op jit(solution)/shard_map/ppermute | solution.py:46
  373.9 76.0 %collective-permute-start.32 = (bf16[104,8192]{1,0:T(8,128)(2,1)}, bf16[104,8192]{1,0:T(8,128)(2,1)}, u32[]{:S(2)}, u32[]{:S(2)}) collective-permute-start(bf16[104,8192]{1,0:T(8,128)(2,1)} %get-tuple-element.21), channel_id=1, source_target_pairs={{0,3},{1,2},{2,1},{3,0},{4,7},{5,6},{6,5},{7,4},{8,11},{9,10},{10,... | collective-permute-start | bytes 5111816 | tf_op jit(solution)/shard_map/ppermute | solution.py:46
  375.5 10.1 %collective-permute-start.44 = (bf16[128,1024]{1,0:T(8,128)(2,1)S(1)}, bf16[128,1024]{1,0:T(8,128)(2,1)S(1)}, u32[]{:S(2)}, u32[]{:S(2)}) collective-permute-start(bf16[128,1024]{1,0:T(8,128)(2,1)S(1)} %fusion.43), channel_id=1, source_target_pairs={{4,0},{5,1},{6,2},{7,3},{8,4},{9,5},{10,6},{11,7},{12,8},{13,9},{1... | collective-permute-start | bytes 786440 | tf_op jit(solution)/shard_map/ppermute | solution.py:43
  385.6 71.3 %collective-permute-start.35 = (bf16[128,8192]{1,0:T(8,128)(2,1)S(1)}, bf16[128,8192]{1,0:T(8,128)(2,1)}, u32[]{:S(2)}, u32[]{:S(2)}) collective-permute-start(bf16[128,8192]{1,0:T(8,128)(2,1)S(1)} %copy-done.6), channel_id=1, source_target_pairs={{0,4},{1,5},{2,6},{3,7},{4,8},{5,9},{6,10},{7,11},{8,12},{9,13},{1... | collective-permute-start | bytes 6291464 | tf_op jit(solution)/shard_map/ppermute | solution.py:43
  388.8 68.1 %collective-permute-start.38 = (bf16[128,8192]{1,0:T(8,128)(2,1)}, bf16[128,8192]{1,0:T(8,128)(2,1)}, u32[]{:S(2)}, u32[]{:S(2)}) collective-permute-start(bf16[128,8192]{1,0:T(8,128)(2,1)} %fusion.18), channel_id=1, source_target_pairs={{4,0},{5,1},{6,2},{7,3},{8,4},{9,5},{10,6},{11,7},{12,8},{13,9},{1... | collective-permute-start | bytes 6291464 | tf_op jit(solution)/shard_map/ppermute | solution.py:43
  (28 other events, 600.1 us)

commit v2 on v1

v2 whole, which is shorter than its diff:
```python
import jax
import jax.numpy as jnp
from jax import lax
from jax.sharding import Mesh, PartitionSpec as P

adapter_scale = 0.25
bf16 = jnp.bfloat16
f32 = jnp.float32
CHAIN = 4
ORDER = ((3, 2, 1, 0), (3, 2, 0, 1), (0, 1, 3, 2), (0, 1, 2, 3))
RANK = tuple(tuple(row.index(k) for k in range(CHAIN)) for row in ORDER)


def dot(a, b, dims):
    return lax.dot_general(a, b, (dims, ((), ())), preferred_element_type=f32)


def gate(values, after):
    return lax.optimization_barrier((values, after))[0]


def shards(
    tokens,
    cotangent,
    frozen_key_matrix,
    adapter_down_weight,
    adapter_up_weight,
    token_adapter_index,
    adapter_storage_index,
):
    groups = lax.axis_size("groups")
    depth = lax.axis_size("chain")
    sides = lax.axis_size("side")
    plane = 2 * sides
    devices = depth * plane
    tok_count = tokens.shape[0]
    locals_, width, rank = adapter_down_weight.shape
    features = cotangent.shape[1]
    entries = adapter_storage_index.shape[0]
    capacity = max(2, 5 * tok_count // (3 * locals_ * devices))
    block = locals_ * rank
    half = width // 2
    rows = depth * locals_ * capacity
    z = lax.axis_index("chain")
    side = lax.axis_index("side")
    q = 2 * side + lax.axis_index("core")
    group = lax.axis_index("groups")
    edge = (z == 0) | (z == depth - 1)
    order = lax.dynamic_index_in_dim(jnp.array(ORDER, jnp.int32), z, 0, False)
    place = lax.dynamic_index_in_dim(jnp.array(RANK, jnp.int32), z, 0, False)

    def swap(values, bit):
        if bit == 1:
            return lax.ppermute(values, "core", [(0, 1), (1, 0)])
        return lax.ppermute(values, "side", [(i, i ^ (bit // 2)) for i in range(sides)])

    def turn(values, k):
        return lax.ppermute(values, "chain", [(i, (i + k) % depth) for i in range(depth)])

    def up(values):
        return lax.ppermute(values, "chain", [(i, i + 1) for i in range(depth - 1)])

    def down(values):
        return lax.ppermute(values, "chain", [(i + 1, i) for i in range(depth - 1)])

    bits = []
    while 2 ** len(bits) < plane:
        bits.append(2 ** len(bits))

    down_rows = jnp.transpose(adapter_down_weight, (0, 2, 1)).reshape(block, width)
    up_rows = adapter_up_weight.reshape(block, features)
    share = frozen_key_matrix.shape[0] // groups
    piece = lax.dynamic_slice_in_dim(frozen_key_matrix, group * share, share, 0)
    extra = share * features // block

    def pack(values):
        if share >= block:
            return jnp.concatenate([values[i : i + block] for i in range(0, share, block)], 1)
        return jnp.concatenate([values[:, i : i + extra] for i in range(0, features, extra)], 0)

    def unpack(values):
        if share >= block:
            return jnp.concatenate(
                [values[:, i : i + features] for i in range(0, extra, features)], 0
            )
        return jnp.concatenate([values[i : i + share] for i in range(0, block, share)], 1)

    flat_ids = token_adapter_index[:, 0]
    onehot = (flat_ids[:, None] == jnp.arange(entries, dtype=jnp.int32)[None, :]).astype(jnp.int32)
    within = jnp.sum(jnp.cumsum(onehot, axis=0) * onehot, axis=1) - 1
    position = jnp.sum(onehot * adapter_storage_index[None, :], axis=1)
    home, local = position // locals_, position % locals_
    far = home // plane
    chunk = jnp.sum(
        jnp.where(far[:, None] == jnp.arange(depth, dtype=jnp.int32)[None, :], place[None, :], 0),
        axis=1,
    )
    relative = (home % plane) ^ q
    slots = ((relative * depth + chunk) * locals_ + local) * capacity + within
    spread = (
        jnp.arange(plane * rows, dtype=jnp.int32)[:, None] == slots[None, :]
    ).astype(bf16)

    def dispatch(values):
        cut = spread.reshape(plane // 2, 2, rows, tok_count)
        first = [
            dot(cut[:, i].reshape(plane // 2 * rows, tok_count), values, ((1,), (0,))).astype(bf16)
            for i in range(2)
        ]
        sent = swap(first[1], 1)
        parts = [
            jnp.concatenate([v[m * rows : (m + 1) * rows] for v in (first[0], sent)], 0)
            for m in range(plane // 2)
        ]
        for bit in bits[1:]:
            got = swap(jnp.concatenate(parts[1::2], 0), bit)
            size = parts[0].shape[0]
            parts = [
                jnp.concatenate([v, got[i * size : (i + 1) * size]], 0)
                for i, v in enumerate(parts[::2])
            ]
        return parts[0]

    def give_back(values):
        parts = [values]
        for bit in bits[::-1]:
            size = parts[0].shape[0] // 2
            got = swap(jnp.concatenate([v[size:] for v in parts], 0), bit)
            parts = [v[:size] for v in parts] + [
                got[i * size : (i + 1) * size] for i in range(len(parts))
            ]
        index = [0]
        for bit in bits[::-1]:
            index = index + [m | bit for m in index]
        return jnp.concatenate([parts[index.index(m)] for m in range(plane)], 0)

    def join_sides(values):
        values = values[:, None]
        for bit in bits[1:]:
            other = swap(values, bit)
            low = (q & bit) == 0
            values = jnp.concatenate(
                [jnp.where(low, values, other), jnp.where(low, other, values)], 1
            )
        return values

    def join_rest(values):
        everything = lax.all_gather(values, ("groups", "core"), axis=0, tiled=False)
        everything = everything.reshape(groups, 2, *values.shape)
        everything = jnp.transpose(everything, (2, 3, 1, 0, 4, 5))
        return everything.reshape(values.shape[0], width // depth, features)

    row_adapter = (jnp.arange(plane * rows) % rows) // capacity
    col_adapter = jnp.arange(depth * block) // rank
    mask = row_adapter[:, None] == col_adapter[None, :]

    def masked(values):
        return jnp.where(mask, values, 0.0).astype(bf16)

    def grad(hid, values, *more):
        out = adapter_scale * dot(hid, values, ((0,), (0,)))
        for m in more:
            out = out + m.astype(f32)
        return out

    def widen(values, like):
        return jnp.pad(values, ((0, 0), (0, like.shape[1] - values.shape[1])))

    def near(u1, d1):
        return jnp.where((z == 0) | (z == 2), d1, u1)

    def middle(u1, d1, e2):
        return jnp.where(edge, e2, jnp.where(z == 1, d1, u1))

    turned = [turn(up_rows, k) for k in range(1, depth)]
    cot = dispatch(cotangent)

    a = [down_rows[:, :half], down_rows[:, half:]]
    tok = [tokens[:, :half], tokens[:, half:]]
    load = [jnp.concatenate([a[0], pack(piece)], 1), a[1]]
    load[0] = gate(load[0], turned)
    one, x = [None, None], [None, None]
    for h in range(2):
        one[h] = up(load[h]), down(load[h])
        x[h] = dispatch(gate(tok[h], cot) if h == 0 else gate(tok[h], x[0]))

    by_shift = jnp.stack([up_rows] + turned)
    up_all = jnp.concatenate(
        [
            lax.dynamic_index_in_dim(by_shift, (z - order[j] + depth) % depth, 0, False)
            for j in range(depth)
        ],
        axis=0,
    )
    hidden = masked(dot(cot, up_all, ((1,), (1,))))
    hid = [hidden[:, j * block : (j + 1) * block] for j in range(depth)]
    second = jnp.where(edge, hid[1], hid[0])
    third_up = jnp.where(z == 1, hid[1], hid[2])
    third_down = jnp.where(z == 2, hid[1], hid[2])

    def pair(p):
        cut = hidden.reshape(plane, 2, rows // 2, depth * block)[:, p]
        return cut.reshape(plane * rows // 2, depth * block)[
            :, p * 2 * block : (p + 1) * 2 * block
        ]

    def spread_pair(p):
        return spread.reshape(plane, 2, rows // 2, tok_count)[:, p].reshape(-1, tok_count)

    def lora(p, weights):
        return (adapter_scale * dot(pair(p), weights, ((1,), (0,)))).astype(bf16)

    def weight_part(values):
        return values[:, :half]

    def base_part(values):
        return unpack(values[:, half:])

    two = [None, None]
    for h in range(2):
        v = widen(grad(hid[0], x[h]).astype(bf16), load[h])
        two[h] = (
            up(jnp.where(z == 0, v, one[h][0])),
            down(jnp.where(z == depth - 1, v, one[h][1])),
        )
    base_32 = join_rest(join_sides(jnp.stack([base_part(near(*one[0])), piece])))
    near_a = jnp.concatenate([near(*map(weight_part, one[h])) for h in range(2)], 1)
    back_1 = give_back(lora(1, jnp.concatenate([near_a, down_rows], 0)))

    three, e2 = [None, None], [None, None]
    for h in range(2):
        uu, dd = two[h]
        e2[h] = jnp.where(z >= 2, uu, dd)
        r1 = jnp.where(edge, jnp.zeros_like(uu), jnp.where(z == 1, uu, dd))
        v = widen(grad(second, x[h], weight_part(r1)).astype(bf16), load[h])
        three[h] = up(jnp.where(z <= 1, v, e2[h])), down(jnp.where(z >= 2, v, e2[h]))
    base_1 = join_rest(join_sides(base_part(middle(*one[0], e2[0]))[None]))

    four, far_a, back_0 = [None, None], [None, None], [None, None]
    for h in range(2):
        uu, dd = map(weight_part, three[h])
        e3 = jnp.where(z == depth - 1, uu, dd)
        zero = jnp.zeros_like(uu)
        ru, rd = jnp.where(edge, zero, uu), jnp.where(edge, zero, dd)
        four[h] = (
            up(grad(third_up, x[h], ru).astype(bf16)),
            down(grad(third_down, x[h], rd).astype(bf16)),
        )
        far_a[h] = jnp.concatenate(
            [
                jnp.where(edge, e3, weight_part(e2[h])),
                middle(*map(weight_part, one[h]), weight_part(e2[h])),
            ],
            0,
        )
        back_0[h] = give_back(lora(0, far_a[h]))
    uu, dd = three[0]
    base_0 = join_rest(
        join_sides(
            base_part(jnp.where(edge, jnp.where(z == depth - 1, uu, dd), e2[0]))[None]
        )
    )

    down_all = jnp.concatenate([jnp.concatenate(far_a, 1), near_a, down_rows], 0)
    shrunk = masked(
        sum(
            dot(x[h], down_all[:, h * half : (h + 1) * half], ((1,), (1,))) for h in range(2)
        )
    )
    up_parts = adapter_scale * dot(shrunk, cot, ((0,), (0,)))
    up_own = up_parts[(depth - 1) * block :]
    up_parts = up_parts.astype(bf16).reshape(depth, block, features)
    up_sent = [
        turn(lax.dynamic_index_in_dim(up_parts, place[(z + k) % depth], 0, False), k)
        for k in range(1, depth)
    ]
    expanded = give_back((adapter_scale * dot(shrunk, up_all, ((1,), (0,)))).astype(bf16))

    whole = jnp.zeros((depth, width // depth, features), bf16)
    for j, f in ((3, base_32[1:]), (2, base_32[:1]), (1, base_1), (0, base_0)):
        whole = lax.dynamic_update_slice_in_dim(whole, f, order[j], 0)
    whole = whole.reshape(width, features)
    key_output = (
        dot(tokens, whole, ((1,), (0,))) + dot(spread, expanded, ((0,), (0,)))
    ).astype(bf16)
    token_grad = (
        dot(cotangent, whole, ((1,), (1,)))
        + dot(spread_pair(1), back_1, ((0,), (0,)))
        + dot(spread_pair(0), jnp.concatenate(back_0, 1), ((0,), (0,)))
    ).astype(bf16)
    down_grad = jnp.concatenate([grad(hid[3], x[h], *four[h]) for h in range(2)], axis=1)
    up_grad = up_own + sum(v.astype(f32) for v in up_sent)
    down_grad = jnp.transpose(down_grad.reshape(locals_, rank, width), (0, 2, 1))
    up_grad = up_grad.reshape(locals_, rank, features)
    return key_output, token_grad, down_grad, up_grad


def solution(mesh):
    groups, wide = mesh.devices.shape
    fine = Mesh(
        mesh.devices.reshape(groups, CHAIN, wide // CHAIN // 2, 2),
        ("groups", "chain", "side", "core"),
    )
    every = ("groups", "chain", "side", "core")
    return jax.shard_map(
        shards,
        mesh=fine,
        in_specs=(
            P(every, None),
            P(every, None),
            P(every[1:], None),
            P(every, None, None),
            P(every, None, None),
            P(every, None),
            P("groups"),
        ),
        out_specs=(
            P(every, None),
            P(every, None),
            P(every, None, None),
            P(every, None, None),
        ),
        check_vma=False,
    )
```

time: 525 us -> 529 us (level)
  the two profiles are of different devices: /device:TPU:18 before, /device:TPU:0 now
where the time goes in v2:
time: 529 us; the launch traced here: 519 us
  waiting for transfers between devices  187 us (35%)
  matrix products  93.4 us (18%)
  local copies, waits for them, and re-layouts  88.3 us (17%)
  starting transfers between devices  73.6 us (14%)
  other arithmetic  45.8 us (9%)
  between operations  31 us (6%)
    dot_general x29, matrix products, dot(): return lax.dot_general(a, b, (dims, ((), ())), preferred_element_type=f32)  93.4 us
    ppermute x10, waiting for transfers between devices, swap(): lax.ppermute(values, 'side', [(i, i ^ bit // 2) for i in range(sides)])  87.2 us
    ppermute x8, waiting for transfers between devices, down(): return lax.ppermute(values, 'chain', [(i + 1, i) for i in range(depth - 1)])  64.2 us
    ppermute x8, starting transfers between devices, up(): return lax.ppermute(values, 'chain', [(i, i + 1) for i in range(depth - 1)])  40.6 us
    ppermute x8, waiting for transfers between devices, up(): return lax.ppermute(values, 'chain', [(i, i + 1) for i in range(depth - 1)])  28.7 us
    unnamed x172, local copies, waits for them, and re-layouts  22.2 us
    ppermute x8, starting transfers between devices, down(): return lax.ppermute(values, 'chain', [(i + 1, i) for i in range(depth - 1)])  10.9 us
    ppermute x6, starting transfers between devices, turn(): lax.ppermute(values, 'chain', [(i, (i + k) % depth) for i in range(depth)])  10.8 us
  transfers between devices with their start and end apart: 42, of which 14 were waited for; matrix products, arithmetic and copies ran while one was open for 32% of the time, Pallas kernels for 0%

profile of v2, /device:TPU:0, one launch (start us, length us, event | category | flops | bytes accessed | tf_op | source)
XLA Modules:
  0.0 519.1 jit_solution(2551808287711667387)
XLA Ops:
  7.2 3.1 collective-permute-start
  10.3 2.6 collective-permute-start.1
  18.6 2.7 fusion.110
  40.0 2.7 collective-permute-start.4
  50.8 8.9 %collective-permute-done.7 = bf16[208,1024]{1,0:T(8,128)(2,1)S(1)} collective-permute-done((bf16[208,1024]{1,0:T(8,128)(2,1)S(1)}, bf16[208,1024]{1,0:T(8,128)(2,1)S(1)}, u32[]{:S(2)}, u32[]{:S(2)}) %collective-permute-start.7) | collective-permute-done | bytes 426016 | tf_op jit(solution)/shard_map/ppermute | solution.py:55
  65.0 31.2 %collective-permute-done.9 = bf16[208,4096]{1,0:T(8,128)(2,1)S(1)} collective-permute-done((bf16[208,4096]{1,0:T(8,128)(2,1)S(1)}, bf16[208,4096]{1,0:T(8,128)(2,1)S(1)}, u32[]{:S(2)}, u32[]{:S(2)}) %collective-permute-start.9) | collective-permute-done | bytes 1703968 | tf_op jit(solution)/shard_map/ppermute | solution.py:55
  97.4 2.7 pad_select_fusion.3
  101.4 6.4 %collective-permute-start.10 = (bf16[128,6144]{1,0:T(8,128)(2,1)}, bf16[128,6144]{1,0:T(8,128)(2,1)}, u32[]{:S(2)}, u32[]{:S(2)}) collective-permute-start(bf16[128,6144]{1,0:T(8,128)(2,1)} %get-tuple-element.88), channel_id=1, source_target_pairs={{0,4},{4,8},{8,12},{1,5},{5,9},{9,13},{2,6},{6,10},{10,14},{3,7},{... | collective-permute-start | bytes 4718600 | tf_op jit(solution)/shard_map/ppermute | solution.py:61
  109.1 5.6 %collective-permute-start.18 = (bf16[128,4096]{1,0:T(8,128)(2,1)}, bf16[128,4096]{1,0:T(8,128)(2,1)}, u32[]{:S(2)}, u32[]{:S(2)}) collective-permute-start(bf16[128,4096]{1,0:T(8,128)(2,1)} %get-tuple-element.50), channel_id=1, source_target_pairs={{0,4},{4,8},{8,12},{1,5},{5,9},{9,13},{2,6},{6,10},{10,14},{3,7},{... | collective-permute-start | bytes 3145736 | tf_op jit(solution)/shard_map/ppermute | solution.py:61
  114.6 45.3 %collective-permute-done.20 = bf16[128,4096]{1,0:T(8,128)(2,1)S(1)} collective-permute-done((bf16[128,4096]{1,0:T(8,128)(2,1)}, bf16[128,4096]{1,0:T(8,128)(2,1)S(1)}, u32[]{:S(2)}, u32[]{:S(2)}) %collective-permute-start.20) | collective-permute-done | bytes 1048608 | tf_op jit(solution)/shard_map/ppermute | solution.py:64
  161.2 4.2 broadcast_select_fusion.8
  165.5 4.8 collective-permute-start.19
  174.8 3.4 pad_select_fusion
  179.7 5.7 %collective-permute-start.13 = (bf16[128,6144]{1,0:T(8,128)(2,1)}, bf16[128,6144]{1,0:T(8,128)(2,1)}, u32[]{:S(2)}, u32[]{:S(2)}) collective-permute-start(bf16[128,6144]{1,0:T(8,128)(2,1)} %pad_select_fusion.1), channel_id=1, source_target_pairs={{0,4},{4,8},{8,12},{1,5},{5,9},{9,13},{2,6},{6,10},{10,14},{3,7},{... | collective-permute-start | bytes 4718600 | tf_op jit(solution)/shard_map/ppermute | solution.py:61
  187.3 6.8 %collective-permute-done.19 = bf16[128,4096]{1,0:T(8,128)(2,1)S(1)} collective-permute-done((bf16[128,4096]{1,0:T(8,128)(2,1)}, bf16[128,4096]{1,0:T(8,128)(2,1)S(1)}, u32[]{:S(2)}, u32[]{:S(2)}) %collective-permute-start.19) | collective-permute-done | bytes 1048608 | tf_op jit(solution)/shard_map/ppermute | solution.py:61
  195.1 3.5 collective-permute-done.21
  198.5 4.6 broadcast_select_fusion.4
  204.3 4.7 collective-permute-start.22
  210.4 17.3 %collective-permute-done.13 = bf16[128,6144]{1,0:T(8,128)(2,1)} collective-permute-done((bf16[128,6144]{1,0:T(8,128)(2,1)}, bf16[128,6144]{1,0:T(8,128)(2,1)}, u32[]{:S(2)}, u32[]{:S(2)}) %collective-permute-start.13) | collective-permute-done | bytes 1572896 | tf_op jit(solution)/shard_map/ppermute | solution.py:61
  227.8 4.5 collective-permute-done.14
  232.2 3.0 select_select_fusion.1
  265.4 3.2 select_select_fusion.2
  271.0 3.5 fusion.22
  275.7 3.4 fusion.21
  279.2 6.0 %collective-permute-start.34 = (bf16[128,4096]{1,0:T(8,128)(2,1)}, bf16[128,4096]{1,0:T(8,128)(2,1)}, u32[]{:S(2)}, u32[]{:S(2)}) collective-permute-start(bf16[128,4096]{1,0:T(8,128)(2,1)} %fusion.21), channel_id=1, source_target_pairs={{0,4},{4,8},{8,12},{1,5},{5,9},{9,13},{2,6},{6,10},{10,14},{3,7},{... | collective-permute-start | bytes 3145736 | tf_op jit(solution)/shard_map/ppermute | solution.py:61
  292.7 3.3 select_select_fusion.4
  296.0 31.4 %collective-permute-done.15 = bf16[1,1,256,1024]{3,2,1,0:T(8,128)(2,1)S(1)} collective-permute-done((bf16[1,1,256,1024]{3,2,1,0:T(8,128)(2,1)S(1)}, bf16[1,1,256,1024]{3,2,1,0:T(8,128)(2,1)S(1)}, u32[]{:S(2)}, u32[]{:S(2)}) %collective-permute-start.15) | collective-permute-done | bytes 524320 | tf_op jit(solution)/shard_map/ppermute | solution.py:55
  329.0 6.4 %pad_maximum_fusion = bf16[512,8192]{1,0:T(8,128)(2,1)S(1)} fusion(bf16[128,8192]{1,0:T(8,128)(2,1)S(1)} %bitcast.129, bf16[128,4096]{1,0:T(8,128)(2,1)} %get-tuple-element.49, bf16[128,4096]{1,0:T(8,128)(2,1)} %get-tuple-element.45, bf16[128,4096]{1,0:T(8,128)(2,1)} %copy-done.16, bf16[128,4096]{1,0:T(8,128)(2,1)} %copy-done.17, ...), kind=kLoop, calls=%fused_computation.6 | loop fusion | flops 58720256 | bytes 16777216 | tf_op jit(solution)/shard_map/concatenate | solution.py:264
  335.5 4.1 fusion.23
  343.8 8.1 %fusion.2 = bf16[208,8192]{1,0:T(8,128)(2,1)S(1)} fusion(bf16[128,8192]{1,0:T(8,128)(2,1)S(1)} %bitcast.130, bf16[128,4096]{1,0:T(8,128)(2,1)S(1)} %copy-done.15, bf16[128,4096]{1,0:T(8,128)(2,1)S(1)} %copy-done.20, bf16[208,512]{1,0:T(8,128)(2,1)S(1)} %copy-done.71), kind=kOutput, calls=%fused_computation.5 | convolution fusion | flops 888406016 | bytes 7708672 | tf_op jit(solution)/shard_map/dot_general | solution.py:15
  358.8 2.9 fusion.20
  362.0 2.4 collective-permute-start.37
  364.4 4.3 fusion.8
  374.0 3.1 fusion.19
  380.1 6.9 %collective-permute-done.37 = bf16[128,1024]{1,0:T(8,128)(2,1)} collective-permute-done((bf16[128,1024]{1,0:T(8,128)(2,1)}, bf16[128,1024]{1,0:T(8,128)(2,1)}, u32[]{:S(2)}, u32[]{:S(2)}) %collective-permute-start.37) | collective-permute-done | bytes 262176 | tf_op jit(solution)/shard_map/ppermute | solution.py:58
  391.4 4.7 collective-permute-start.32
  402.2 11.0 %collective-permute-done.33 = bf16[128,4096]{1,0:T(8,128)(2,1)S(1)} collective-permute-done((bf16[128,4096]{1,0:T(8,128)(2,1)S(1)}, bf16[128,4096]{1,0:T(8,128)(2,1)S(1)}, u32[]{:S(2)}, u32[]{:S(2)}) %collective-permute-start.33) | collective-permute-done | bytes 1048608 | tf_op jit(solution)/shard_map/ppermute | solution.py:64
  413.2 3.2 collective-permute-done.32
  420.7 14.2 %collective-permute-done.26 = bf16[104,8192]{1,0:T(8,128)(2,1)S(1)} collective-permute-done((bf16[104,8192]{1,0:T(8,128)(2,1)S(1)}, bf16[104,8192]{1,0:T(8,128)(2,1)S(1)}, u32[]{:S(2)}, u32[]{:S(2)}) %collective-permute-start.26) | collective-permute-done | bytes 1703968 | tf_op jit(solution)/shard_map/ppermute | solution.py:55
  436.3 10.6 %fusion.39 = f32[256,8192]{0,1:T(8,128)} fusion(pred[208,256]{1,0:T(8,128)(4,1)S(1)} %copy-done.76, bf16[52,4096]{1,0:T(8,128)(2,1)S(1)} %get-tuple-element.101, bf16[52,4096]{1,0:T(8,128)(2,1)S(1)} %copy-done.55, bf16[52,4096]{1,0:T(8,128)(2,1)S(1)} %get-tuple-element.100, bf16[52,4096]{1,0:T(8,128)(2,1)S(1)} %copy-done.54, ...), kind=kOutput, calls=%fused_computation.63 | convolution fusion | flops 899678208 | bytes 11849728 | tf_op jit(solution)/shard_map/dot_general | solution.py:15
  448.3 4.6 copy.45
  452.9 4.7 copy.46
  457.6 8.1 %copy.58 = bf16[2,2,2,2,256,1024]{5,4,0,1,3,2:T(8,128)(2,1)} copy(bf16[2,2,2,2,256,1024]{5,4,2,1,0,3:T(8,128)(2,1)} %bitcast.127) | data formatting | bytes 16777216 | tf_op jit(solution)/shard_map/reshape | solution.py:149
  465.7 3.9 fusion.109
  479.2 5.5 %convolution_bitcast_fusion.1 = f32[256,1024]{0,1:T(8,128)} fusion(bf16[8192,1024]{1,0:T(8,128)(2,1)S(1)} %bitcast.121, bf16[256,8192]{1,0:T(8,128)(2,1)S(1)} %copy-done.21), kind=kOutput, calls=%fused_computation.101 | convolution fusion | flops 4294967296 | bytes 22020096 | tf_op jit(solution)/shard_map/dot_general | solution.py:15
  484.7 7.5 %convolution_bitcast_fusion = f32[256,8192]{0,1:T(8,128)} fusion(bf16[8192,1024]{1,0:T(8,128)(2,1)S(1)} %bitcast.122, bf16[256,1024]{1,0:T(8,128)(2,1)S(1)} %copy-done), kind=kOutput, calls=%fused_computation.2 | convolution fusion | flops 4294967296 | bytes 25690112 | tf_op jit(solution)/shard_map/dot_general | solution.py:15
  495.7 10.1 %fusion.1 = bf16[256,8192]{0,1:T(8,128)(2,1)} fusion(f32[256,8192]{0,1:T(8,128)} %fusion.39, f32[256,8192]{0,1:T(8,128)} %convolution_bitcast_fusion, pred[208,256]{1,0:T(8,128)(4,1)S(1)} %reshape_squeeze.25, bf16[52,8192]{1,0:T(8,128)(2,1)} %get-tuple-element.55, bf16[52,8192]{1,0:T(8,128)(2,1)S(1)} %get-tuple-element.56, ...), kind=kOutput, calls=%fused_computation.4 | convolution fusion | flops 892338176 | bytes 24432640 | tf_op jit(solution)/shard_map/dot_general | solution.py:15
  505.8 6.3 %copy.51 = bf16[256,8192]{1,0:T(8,128)(2,1)} copy(bf16[256,8192]{0,1:T(8,128)(2,1)} %fusion.1) | data formatting | bytes 8388608
  (334 shorter events, 131.2 us)
Async XLA Ops:
  7.2 441.1 %all-gather.9.cloned.1.call-start = ((), (), s32[]{:S(2)}) async-start(), calls=%async_computation.1 | async-start | bytes 5242880 | tf_op jit(solution)/shard_map/all_gather | solution.py:148
  7.2 32.7 %collective-permute-start = (bf16[128,1024]{1,0:T(8,128)(2,1)}, bf16[128,1024]{1,0:T(8,128)(2,1)}, u32[]{:S(2)}, u32[]{:S(2)}) collective-permute-start(bf16[128,1024]{1,0:T(8,128)(2,1)} %bitcast.142), channel_id=1, source_target_pairs={{0,4},{4,8},{8,12},{12,0},{1,5},{5,9},{9,13},{13,1},{2,6},{6,10},{... | collective-permute-start | bytes 786440 | tf_op jit(solution)/shard_map/ppermute | solution.py:58
  10.3 29.7 %collective-permute-start.1 = (bf16[128,1024]{1,0:T(8,128)(2,1)}, bf16[128,1024]{1,0:T(8,128)(2,1)}, u32[]{:S(2)}, u32[]{:S(2)}) collective-permute-start(bf16[128,1024]{1,0:T(8,128)(2,1)} %bitcast.143), channel_id=1, source_target_pairs={{0,8},{4,12},{8,0},{12,4},{1,9},{5,13},{9,1},{13,5},{2,10},{6,14},... | collective-permute-start | bytes 786440 | tf_op jit(solution)/shard_map/ppermute | solution.py:58
  12.9 27.1 %collective-permute-start.2 = (bf16[128,1024]{1,0:T(8,128)(2,1)}, bf16[128,1024]{1,0:T(8,128)(2,1)}, u32[]{:S(2)}, u32[]{:S(2)}) collective-permute-start(bf16[128,1024]{1,0:T(8,128)(2,1)} %bitcast.144), channel_id=1, source_target_pairs={{0,12},{4,0},{8,4},{12,8},{1,13},{5,1},{9,5},{13,9},{2,14},{6,2},{... | collective-permute-start | bytes 786440 | tf_op jit(solution)/shard_map/ppermute | solution.py:58
  18.6 26.9 %collective-permute-start.6 = (bf16[208,1024]{1,0:T(8,128)(2,1)}, bf16[208,1024]{1,0:T(8,128)(2,1)}, u32[]{:S(2)}, u32[]{:S(2)}) collective-permute-start(bf16[208,1024]{1,0:T(8,128)(2,1)} %convolution_convert_fusion.4), channel_id=1, source_target_pairs={{0,1},{1,0},{2,3},{3,2},{4,5},{5,4},{6,7},{7,6},{8,9},{9,8},{10,11... | collective-permute-start | bytes 1277960 | tf_op jit(solution)/shard_map/ppermute | solution.py:54
  23.1 25.4 %collective-permute-start.8 = (bf16[208,4096]{1,0:T(8,128)(2,1)}, bf16[208,4096]{1,0:T(8,128)(2,1)}, u32[]{:S(2)}, u32[]{:S(2)}) collective-permute-start(bf16[208,4096]{1,0:T(8,128)(2,1)} %convolution_convert_fusion.2), channel_id=1, source_target_pairs={{0,1},{1,0},{2,3},{3,2},{4,5},{5,4},{6,7},{7,6},{8,9},{9,8},{10,11... | collective-permute-start | bytes 5111816 | tf_op jit(solution)/shard_map/ppermute | solution.py:54
  39.9 21.2 %collective-permute-start.16 = (bf16[208,4096]{1,0:T(8,128)(2,1)}, bf16[208,4096]{1,0:T(8,128)(2,1)S(1)}, u32[]{:S(2)}, u32[]{:S(2)}) collective-permute-start(bf16[208,4096]{1,0:T(8,128)(2,1)} %convolution_convert_fusion), channel_id=1, source_target_pairs={{0,1},{1,0},{2,3},{3,2},{4,5},{5,4},{6,7},{7,6},{8,9},{9,8},{10,11... | collective-permute-start | bytes 5111816 | tf_op jit(solution)/shard_map/ppermute | solution.py:54
  40.0 57.4 %collective-permute-start.4 = (bf16[128,6144]{1,0:T(8,128)(2,1)}, bf16[128,6144]{1,0:T(8,128)(2,1)S(1)}, u32[]{:S(2)}, u32[]{:S(2)}) collective-permute-start(bf16[128,6144]{1,0:T(8,128)(2,1)} %pad_maximum_fusion.8), channel_id=1, source_target_pairs={{0,4},{4,8},{8,12},{1,5},{5,9},{9,13},{2,6},{6,10},{10,14},{3,7},{... | collective-permute-start | bytes 4718600 | tf_op jit(solution)/shard_map/ppermute | solution.py:61
  42.7 54.7 %collective-permute-start.3 = (bf16[128,6144]{1,0:T(8,128)(2,1)}, bf16[128,6144]{1,0:T(8,128)(2,1)S(1)}, u32[]{:S(2)}, u32[]{:S(2)}) collective-permute-start(bf16[128,6144]{1,0:T(8,128)(2,1)} %pad_maximum_fusion.8), channel_id=1, source_target_pairs={{4,0},{8,4},{12,8},{5,1},{9,5},{13,9},{6,2},{10,6},{14,10},{7,3},{... | collective-permute-start | bytes 4718600 | tf_op jit(solution)/shard_map/ppermute | solution.py:64
  46.9 12.7 %collective-permute-start.7 = (bf16[208,1024]{1,0:T(8,128)(2,1)S(1)}, bf16[208,1024]{1,0:T(8,128)(2,1)S(1)}, u32[]{:S(2)}, u32[]{:S(2)}) collective-permute-start(bf16[208,1024]{1,0:T(8,128)(2,1)S(1)} %pad_maximum_fusion.16), channel_id=1, source_target_pairs={{0,2},{2,0},{1,3},{3,1},{4,6},{6,4},{5,7},{7,5},{8,10},{10,8},{9,1... | collective-permute-start | bytes 1277960 | tf_op jit(solution)/shard_map/ppermute | solution.py:55
  50.1 46.1 %copy-start.44 = (bf16[104,4096]{1,0:T(8,128)(2,1)}, bf16[104,4096]{1,0:T(8,128)(2,1)S(1)}, u32[]{:S(2)}) copy-start(bf16[104,4096]{1,0:T(8,128)(2,1)S(1)} %get-tuple-element.68) | copy-start | bytes 2555908
  50.2 45.9 %collective-permute-start.9 = (bf16[208,4096]{1,0:T(8,128)(2,1)S(1)}, bf16[208,4096]{1,0:T(8,128)(2,1)S(1)}, u32[]{:S(2)}, u32[]{:S(2)}) collective-permute-start(bf16[208,4096]{1,0:T(8,128)(2,1)S(1)} %pad_maximum_fusion.5), channel_id=1, source_target_pairs={{0,2},{2,0},{1,3},{3,1},{4,6},{6,4},{5,7},{7,5},{8,10},{10,8},{9,1... | collective-permute-start | bytes 5111816 | tf_op jit(solution)/shard_map/ppermute | solution.py:55
  61.1 35.1 %copy-start.58 = (bf16[416,512]{1,0:T(8,128)(2,1)}, bf16[416,512]{1,0:T(8,128)(2,1)S(1)}, u32[]{:S(2)}) copy-start(bf16[416,512]{1,0:T(8,128)(2,1)S(1)} %fusion.71) | copy-start | bytes 1277956
  61.1 35.1 %copy-start.38 = (bf16[104,4096]{1,0:T(8,128)(2,1)S(1)}, bf16[104,4096]{1,0:T(8,128)(2,1)}, u32[]{:S(2)}) copy-start(bf16[104,4096]{1,0:T(8,128)(2,1)} %get-tuple-element.66) | copy-start | bytes 2555908
  63.5 97.7 %collective-permute-start.17 = (bf16[208,4096]{1,0:T(8,128)(2,1)}, bf16[208,4096]{1,0:T(8,128)(2,1)}, u32[]{:S(2)}, u32[]{:S(2)}) collective-permute-start(bf16[208,4096]{1,0:T(8,128)(2,1)} %pad_maximum_fusion.6), channel_id=1, source_target_pairs={{0,2},{2,0},{1,3},{3,1},{4,6},{6,4},{5,7},{7,5},{8,10},{10,8},{9,1... | collective-permute-start | bytes 5111816 | tf_op jit(solution)/shard_map/ppermute | solution.py:55
  100.1 71.4 %collective-permute-start.11 = (bf16[128,6144]{1,0:T(8,128)(2,1)}, bf16[128,6144]{1,0:T(8,128)(2,1)S(1)}, u32[]{:S(2)}, u32[]{:S(2)}) collective-permute-start(bf16[128,6144]{1,0:T(8,128)(2,1)} %get-tuple-element.89), channel_id=1, source_target_pairs={{4,0},{8,4},{12,8},{5,1},{9,5},{13,9},{6,2},{10,6},{14,10},{7,3},{... | collective-permute-start | bytes 4718600 | tf_op jit(solution)/shard_map/ppermute | solution.py:64
  101.4 70.2 %collective-permute-start.10 = (bf16[128,6144]{1,0:T(8,128)(2,1)}, bf16[128,6144]{1,0:T(8,128)(2,1)}, u32[]{:S(2)}, u32[]{:S(2)}) collective-permute-start(bf16[128,6144]{1,0:T(8,128)(2,1)} %get-tuple-element.88), channel_id=1, source_target_pairs={{0,4},{4,8},{8,12},{1,5},{5,9},{9,13},{2,6},{6,10},{10,14},{3,7},{... | collective-permute-start | bytes 4718600 | tf_op jit(solution)/shard_map/ppermute | solution.py:61
  107.8 52.1 %collective-permute-start.20 = (bf16[128,4096]{1,0:T(8,128)(2,1)}, bf16[128,4096]{1,0:T(8,128)(2,1)S(1)}, u32[]{:S(2)}, u32[]{:S(2)}) collective-permute-start(bf16[128,4096]{1,0:T(8,128)(2,1)} %get-tuple-element.50), channel_id=1, source_target_pairs={{4,0},{8,4},{12,8},{5,1},{9,5},{13,9},{6,2},{10,6},{14,10},{7,3},{... | collective-permute-start | bytes 3145736 | tf_op jit(solution)/shard_map/ppermute | solution.py:64
  109.1 52.1 %collective-permute-start.18 = (bf16[128,4096]{1,0:T(8,128)(2,1)}, bf16[128,4096]{1,0:T(8,128)(2,1)}, u32[]{:S(2)}, u32[]{:S(2)}) collective-permute-start(bf16[128,4096]{1,0:T(8,128)(2,1)} %get-tuple-element.50), channel_id=1, source_target_pairs={{0,4},{4,8},{8,12},{1,5},{5,9},{9,13},{2,6},{6,10},{10,14},{3,7},{... | collective-permute-start | bytes 3145736 | tf_op jit(solution)/shard_map/ppermute | solution.py:61
  165.5 28.6 %collective-permute-start.19 = (bf16[128,4096]{1,0:T(8,128)(2,1)}, bf16[128,4096]{1,0:T(8,128)(2,1)S(1)}, u32[]{:S(2)}, u32[]{:S(2)}) collective-permute-start(bf16[128,4096]{1,0:T(8,128)(2,1)} %get-tuple-element.83), channel_id=1, source_target_pairs={{0,4},{4,8},{8,12},{1,5},{5,9},{9,13},{2,6},{6,10},{10,14},{3,7},{... | collective-permute-start | bytes 3145736 | tf_op jit(solution)/shard_map/ppermute | solution.py:61
  170.2 28.3 %collective-permute-start.21 = (bf16[128,4096]{1,0:T(8,128)(2,1)}, bf16[128,4096]{1,0:T(8,128)(2,1)}, u32[]{:S(2)}, u32[]{:S(2)}) collective-permute-start(bf16[128,4096]{1,0:T(8,128)(2,1)} %get-tuple-element.82), channel_id=1, source_target_pairs={{4,0},{8,4},{12,8},{5,1},{9,5},{13,9},{6,2},{10,6},{14,10},{7,3},{... | collective-permute-start | bytes 3145736 | tf_op jit(solution)/shard_map/ppermute | solution.py:64
  179.7 48.1 %collective-permute-start.13 = (bf16[128,6144]{1,0:T(8,128)(2,1)}, bf16[128,6144]{1,0:T(8,128)(2,1)}, u32[]{:S(2)}, u32[]{:S(2)}) collective-permute-start(bf16[128,6144]{1,0:T(8,128)(2,1)} %pad_select_fusion.1), channel_id=1, source_target_pairs={{0,4},{4,8},{8,12},{1,5},{5,9},{9,13},{2,6},{6,10},{10,14},{3,7},{... | collective-permute-start | bytes 4718600 | tf_op jit(solution)/shard_map/ppermute | solution.py:61
  185.4 46.8 %collective-permute-start.14 = (bf16[128,6144]{1,0:T(8,128)(2,1)}, bf16[128,6144]{1,0:T(8,128)(2,1)}, u32[]{:S(2)}, u32[]{:S(2)}) collective-permute-start(bf16[128,6144]{1,0:T(8,128)(2,1)} %get-tuple-element.34), channel_id=1, source_target_pairs={{4,0},{8,4},{12,8},{5,1},{9,5},{13,9},{6,2},{10,6},{14,10},{7,3},{... | collective-permute-start | bytes 4718600 | tf_op jit(solution)/shard_map/ppermute | solution.py:64
  203.2 29.1 %copy-start.7 = (bf16[128,6144]{1,0:T(8,128)(2,1)S(1)}, bf16[128,6144]{1,0:T(8,128)(2,1)}, u32[]{:S(2)}) copy-start(bf16[128,6144]{1,0:T(8,128)(2,1)} %copy-done.6) | copy-start | bytes 4718596
  204.3 61.1 %collective-permute-start.22 = (bf16[128,4096]{1,0:T(8,128)(2,1)}, bf16[128,4096]{1,0:T(8,128)(2,1)}, u32[]{:S(2)}, u32[]{:S(2)}) collective-permute-start(bf16[128,4096]{1,0:T(8,128)(2,1)} %broadcast_select_fusion.7), channel_id=1, source_target_pairs={{0,4},{4,8},{8,12},{1,5},{5,9},{9,13},{2,6},{6,10},{10,14},{3,7},{... | collective-permute-start | bytes 3145736 | tf_op jit(solution)/shard_map/ppermute | solution.py:61
  209.0 35.3 %copy-start.77 = (s32[4,4]{1,0:T(4,128)S(1)}, s32[4,4]{1,0:T(4,128)}, u32[]{:S(2)}) copy-start(s32[4,4]{1,0:T(4,128)} %constant.220.clone) | copy-start | bytes 196
  209.0 56.4 %collective-permute-start.23 = (bf16[128,4096]{1,0:T(8,128)(2,1)}, bf16[128,4096]{1,0:T(8,128)(2,1)}, u32[]{:S(2)}, u32[]{:S(2)}) collective-permute-start(bf16[128,4096]{1,0:T(8,128)(2,1)} %get-tuple-element.32), channel_id=1, source_target_pairs={{4,0},{8,4},{12,8},{5,1},{9,5},{13,9},{6,2},{10,6},{14,10},{7,3},{... | collective-permute-start | bytes 3145736 | tf_op jit(solution)/shard_map/ppermute | solution.py:64
  237.6 25.2 %collective-permute-start.12 = (bf16[1,1,256,1024]{3,2,1,0:T(8,128)(2,1)}, bf16[1,1,256,1024]{3,2,1,0:T(8,128)(2,1)}, u32[]{:S(2)}, u32[]{:S(2)}) collective-permute-start(bf16[1,1,256,1024]{3,2,1,0:T(8,128)(2,1)} %maximum_bitcast_fusion.2), channel_id=1, source_target_pairs={{0,2},{2,0},{1,3},{3,1},{4,6},{6,4},{5,7},{7,5},{8,10},{10,8},{9,1... | collective-permute-start | bytes 1572872 | tf_op jit(solution)/shard_map/ppermute | solution.py:55
  265.3 187.6 %all-gather.11.cloned.1.call-start = ((), (), s32[]{:S(2)}) async-start(), calls=%async_computation.2 | async-start | bytes 5242880 | tf_op jit(solution)/shard_map/all_gather | solution.py:148
  269.9 16.2 %collective-permute-start.30 = (bf16[104,4096]{1,0:T(8,128)(2,1)S(1)}, bf16[104,4096]{1,0:T(8,128)(2,1)S(1)}, u32[]{:S(2)}, u32[]{:S(2)}) collective-permute-start(bf16[104,4096]{1,0:T(8,128)(2,1)S(1)} %slice.435), channel_id=1, source_target_pairs={{0,2},{2,0},{1,3},{3,1},{4,6},{6,4},{5,7},{7,5},{8,10},{10,8},{9,1... | collective-permute-start | bytes 2555912 | tf_op jit(solution)/shard_map/ppermute | solution.py:55
  274.4 87.2 %collective-permute-start.35 = (bf16[128,4096]{1,0:T(8,128)(2,1)}, bf16[128,4096]{1,0:T(8,128)(2,1)}, u32[]{:S(2)}, u32[]{:S(2)}) collective-permute-start(bf16[128,4096]{1,0:T(8,128)(2,1)} %fusion.22), channel_id=1, source_target_pairs={{4,0},{8,4},{12,8},{5,1},{9,5},{13,9},{6,2},{10,6},{14,10},{7,3},{... | collective-permute-start | bytes 3145736 | tf_op jit(solution)/shard_map/ppermute | solution.py:64
  279.2 82.9 %collective-permute-start.34 = (bf16[128,4096]{1,0:T(8,128)(2,1)}, bf16[128,4096]{1,0:T(8,128)(2,1)}, u32[]{:S(2)}, u32[]{:S(2)}) collective-permute-start(bf16[128,4096]{1,0:T(8,128)(2,1)} %fusion.21), channel_id=1, source_target_pairs={{0,4},{4,8},{8,12},{1,5},{5,9},{9,13},{2,6},{6,10},{10,14},{3,7},{... | collective-permute-start | bytes 3145736 | tf_op jit(solution)/shard_map/ppermute | solution.py:61
  288.0 109.9 %collective-permute-start.31 = (bf16[104,4096]{1,0:T(8,128)(2,1)}, bf16[104,4096]{1,0:T(8,128)(2,1)}, u32[]{:S(2)}, u32[]{:S(2)}) collective-permute-start(bf16[104,4096]{1,0:T(8,128)(2,1)} %pad_maximum_fusion.15), channel_id=1, source_target_pairs={{0,1},{1,0},{2,3},{3,2},{4,5},{5,4},{6,7},{7,6},{8,9},{9,8},{10,11... | collective-permute-start | bytes 2555912 | tf_op jit(solution)/shard_map/ppermute | solution.py:54
  290.5 78.3 %collective-permute-start.5 = (bf16[2,1,256,1024]{3,2,0,1:T(8,128)(2,1)}, bf16[2,1,256,1024]{3,2,0,1:T(8,128)(2,1)}, u32[]{:S(2)}, u32[]{:S(2)}) collective-permute-start(bf16[2,1,256,1024]{3,2,0,1:T(8,128)(2,1)} %maximum_bitcast_fusion), channel_id=1, source_target_pairs={{0,2},{2,0},{1,3},{3,1},{4,6},{6,4},{5,7},{7,5},{8,10},{10,8},{9,1... | collective-permute-start | bytes 3145736 | tf_op jit(solution)/shard_map/ppermute | solution.py:55
  291.5 35.9 %collective-permute-start.15 = (bf16[1,1,256,1024]{3,2,1,0:T(8,128)(2,1)S(1)}, bf16[1,1,256,1024]{3,2,1,0:T(8,128)(2,1)S(1)}, u32[]{:S(2)}, u32[]{:S(2)}) collective-permute-start(bf16[1,1,256,1024]{3,2,1,0:T(8,128)(2,1)S(1)} %maximum_bitcast_fusion.3), channel_id=1, source_target_pairs={{0,2},{2,0},{1,3},{3,1},{4,6},{6,4},{5,7},{7,5},{8,10},{10,8},{9,1... | collective-permute-start | bytes 1572872 | tf_op jit(solution)/shard_map/ppermute | solution.py:55
  296.0 33.0 %copy-start.10 = (bf16[2,8192,64]{1,2,0:T(8,128)(2,1)S(1)}, bf16[2,8192,64]{1,2,0:T(8,128)(2,1)}, u32[]{:S(2)}) copy-start(bf16[2,8192,64]{1,2,0:T(8,128)(2,1)} %param.12) | copy-start | bytes 6291460
  328.8 128.8 %all-gather.7.cloned.1.call-start = ((), (), s32[]{:S(2)}) async-start(), calls=%async_computation | async-start | bytes 10485760 | tf_op jit(solution)/shard_map/all_gather | solution.py:148
  343.4 48.1 %collective-permute-start.24 = (bf16[208,1024]{1,0:T(8,128)(2,1)}, bf16[208,1024]{1,0:T(8,128)(2,1)}, u32[]{:S(2)}, u32[]{:S(2)}) collective-permute-start(bf16[208,1024]{1,0:T(8,128)(2,1)} %slice.408), channel_id=1, source_target_pairs={{0,2},{2,0},{1,3},{3,1},{4,6},{6,4},{5,7},{7,5},{8,10},{10,8},{9,1... | collective-permute-start | bytes 1277960 | tf_op jit(solution)/shard_map/ppermute | solution.py:55
  361.6 17.5 %collective-permute-start.38 = (bf16[128,1024]{1,0:T(8,128)(2,1)}, bf16[128,1024]{1,0:T(8,128)(2,1)}, u32[]{:S(2)}, u32[]{:S(2)}) collective-permute-start(bf16[128,1024]{1,0:T(8,128)(2,1)} %get-tuple-element.79), channel_id=1, source_target_pairs={{0,12},{4,0},{8,4},{12,8},{1,13},{5,1},{9,5},{13,9},{2,14},{6,2},{... | collective-permute-start | bytes 786440 | tf_op jit(solution)/shard_map/ppermute | solution.py:58
  362.0 25.0 %collective-permute-start.37 = (bf16[128,1024]{1,0:T(8,128)(2,1)}, bf16[128,1024]{1,0:T(8,128)(2,1)}, u32[]{:S(2)}, u32[]{:S(2)}) collective-permute-start(bf16[128,1024]{1,0:T(8,128)(2,1)} %get-tuple-element.80), channel_id=1, source_target_pairs={{0,8},{4,12},{8,0},{12,4},{1,9},{5,13},{9,1},{13,5},{2,10},{6,14},... | collective-permute-start | bytes 786440 | tf_op jit(solution)/shard_map/ppermute | solution.py:58
  368.8 19.3 %collective-permute-start.36 = (bf16[128,1024]{1,0:T(8,128)(2,1)}, bf16[128,1024]{1,0:T(8,128)(2,1)}, u32[]{:S(2)}, u32[]{:S(2)}) collective-permute-start(bf16[128,1024]{1,0:T(8,128)(2,1)} %get-tuple-element.78), channel_id=1, source_target_pairs={{0,4},{4,8},{8,12},{12,0},{1,5},{5,9},{9,13},{13,1},{2,6},{6,10},{... | collective-permute-start | bytes 786440 | tf_op jit(solution)/shard_map/ppermute | solution.py:58
  379.1 21.9 %collective-permute-start.28 = (bf16[104,4096]{1,0:T(8,128)(2,1)S(1)}, bf16[104,4096]{1,0:T(8,128)(2,1)S(1)}, u32[]{:S(2)}, u32[]{:S(2)}) collective-permute-start(bf16[104,4096]{1,0:T(8,128)(2,1)S(1)} %slice.428), channel_id=1, source_target_pairs={{0,2},{2,0},{1,3},{3,1},{4,6},{6,4},{5,7},{7,5},{8,10},{10,8},{9,1... | collective-permute-start | bytes 2555912 | tf_op jit(solution)/shard_map/ppermute | solution.py:55
  387.0 47.9 %collective-permute-start.26 = (bf16[104,8192]{1,0:T(8,128)(2,1)S(1)}, bf16[104,8192]{1,0:T(8,128)(2,1)S(1)}, u32[]{:S(2)}, u32[]{:S(2)}) collective-permute-start(bf16[104,8192]{1,0:T(8,128)(2,1)S(1)} %slice.418), channel_id=1, source_target_pairs={{0,2},{2,0},{1,3},{3,1},{4,6},{6,4},{5,7},{7,5},{8,10},{10,8},{9,1... | collective-permute-start | bytes 5111816 | tf_op jit(solution)/shard_map/ppermute | solution.py:55
  388.1 25.0 %collective-permute-start.33 = (bf16[128,4096]{1,0:T(8,128)(2,1)S(1)}, bf16[128,4096]{1,0:T(8,128)(2,1)S(1)}, u32[]{:S(2)}, u32[]{:S(2)}) collective-permute-start(bf16[128,4096]{1,0:T(8,128)(2,1)S(1)} %copy-done.82), channel_id=1, source_target_pairs={{4,0},{8,4},{12,8},{5,1},{9,5},{13,9},{6,2},{10,6},{14,10},{7,3},{... | collective-permute-start | bytes 3145736 | tf_op jit(solution)/shard_map/ppermute | solution.py:64
  391.4 24.9 %collective-permute-start.32 = (bf16[128,4096]{1,0:T(8,128)(2,1)S(1)}, bf16[128,4096]{1,0:T(8,128)(2,1)S(1)}, u32[]{:S(2)}, u32[]{:S(2)}) collective-permute-start(bf16[128,4096]{1,0:T(8,128)(2,1)S(1)} %fusion.19), channel_id=1, source_target_pairs={{0,4},{4,8},{8,12},{1,5},{5,9},{9,13},{2,6},{6,10},{10,14},{3,7},{... | collective-permute-start | bytes 3145736 | tf_op jit(solution)/shard_map/ppermute | solution.py:61
  398.0 3.4 collective-permute-start.25
  401.3 34.2 %collective-permute-start.29 = (bf16[104,4096]{1,0:T(8,128)(2,1)S(1)}, bf16[104,4096]{1,0:T(8,128)(2,1)S(1)}, u32[]{:S(2)}, u32[]{:S(2)}) collective-permute-start(bf16[104,4096]{1,0:T(8,128)(2,1)S(1)} %pad_maximum_fusion.14), channel_id=1, source_target_pairs={{0,1},{1,0},{2,3},{3,2},{4,5},{5,4},{6,7},{7,6},{8,9},{9,8},{10,11... | collective-permute-start | bytes 2555912 | tf_op jit(solution)/shard_map/ppermute | solution.py:54
  435.4 11.4 %collective-permute-start.27 = (bf16[104,8192]{1,0:T(8,128)(2,1)S(1)}, bf16[104,8192]{1,0:T(8,128)(2,1)S(1)}, u32[]{:S(2)}, u32[]{:S(2)}) collective-permute-start(bf16[104,8192]{1,0:T(8,128)(2,1)S(1)} %pad_maximum_fusion.7), channel_id=1, source_target_pairs={{0,1},{1,0},{2,3},{3,2},{4,5},{5,4},{6,7},{7,6},{8,9},{9,8},{10,11... | collective-permute-start | bytes 5111816 | tf_op jit(solution)/shard_map/ppermute | solution.py:54
  (79 other events, 439.9 us)
Sparse Core Ops, SparseCore 0:
  265.4 32.8 all-gather.8
  328.9 33.0 all-gather.10
  372.8 58.1 all-gather.6

commit v3 on v2

v3 whole, which is shorter than its diff:
```python
import jax
import jax.numpy as jnp
from jax import lax
from jax.experimental import pallas as pl
from jax.sharding import Mesh, PartitionSpec as P

adapter_scale = 0.25
bf16 = jnp.bfloat16
f32 = jnp.float32
CHAIN = 4
ORDER = ((3, 2, 1, 0), (3, 2, 0, 1), (0, 1, 3, 2), (0, 1, 2, 3))
RANK = tuple(tuple(row.index(k) for k in range(CHAIN)) for row in ORDER)


def dot(a, b, dims):
    return lax.dot_general(a, b, (dims, ((), ())), preferred_element_type=f32)


def tie(value, *after):
    def body(*refs):
        pass

    anywhere = pl.BlockSpec(memory_space=pl.ANY)
    return pl.pallas_call(
        body,
        out_shape=jax.ShapeDtypeStruct(value.shape, value.dtype),
        in_specs=[anywhere] * (1 + len(after)),
        out_specs=anywhere,
        input_output_aliases={0: 0},
        cost_estimate=pl.CostEstimate(flops=0, bytes_accessed=0, transcendentals=0),
    )(value, *after)


def shards(
    tokens,
    cotangent,
    frozen_key_matrix,
    adapter_down_weight,
    adapter_up_weight,
    token_adapter_index,
    adapter_storage_index,
):
    groups = lax.axis_size("groups")
    depth = lax.axis_size("chain")
    sides = lax.axis_size("side")
    plane = 2 * sides
    devices = depth * plane
    tok_count = tokens.shape[0]
    locals_, width, rank = adapter_down_weight.shape
    features = cotangent.shape[1]
    entries = adapter_storage_index.shape[0]
    capacity = max(2, 5 * tok_count // (3 * locals_ * devices))
    block = locals_ * rank
    half = width // 2
    rows = depth * locals_ * capacity
    z = lax.axis_index("chain")
    side = lax.axis_index("side")
    q = 2 * side + lax.axis_index("core")
    group = lax.axis_index("groups")
    edge = (z == 0) | (z == depth - 1)
    order = lax.dynamic_index_in_dim(jnp.array(ORDER, jnp.int32), z, 0, False)
    place = lax.dynamic_index_in_dim(jnp.array(RANK, jnp.int32), z, 0, False)

    def swap(values, bit):
        if bit == 1:
            return lax.ppermute(values, "core", [(0, 1), (1, 0)])
        return lax.ppermute(values, "side", [(i, i ^ (bit // 2)) for i in range(sides)])

    def turn(values, k):
        return lax.ppermute(values, "chain", [(i, (i + k) % depth) for i in range(depth)])

    def up(values):
        return lax.ppermute(values, "chain", [(i, i + 1) for i in range(depth - 1)])

    def down(values):
        return lax.ppermute(values, "chain", [(i + 1, i) for i in range(depth - 1)])

    bits = []
    while 2 ** len(bits) < plane:
        bits.append(2 ** len(bits))

    down_rows = jnp.transpose(adapter_down_weight, (0, 2, 1)).reshape(block, width)
    up_rows = adapter_up_weight.reshape(block, features)
    share = frozen_key_matrix.shape[0] // groups
    piece = lax.dynamic_slice_in_dim(frozen_key_matrix, group * share, share, 0)
    flat_ids = token_adapter_index[:, 0]
    onehot = (flat_ids[:, None] == jnp.arange(entries, dtype=jnp.int32)[None, :]).astype(jnp.int32)
    within = jnp.sum(jnp.cumsum(onehot, axis=0) * onehot, axis=1) - 1
    position = jnp.sum(onehot * adapter_storage_index[None, :], axis=1)
    home, local = position // locals_, position % locals_
    far = home // plane
    chunk = jnp.sum(
        jnp.where(far[:, None] == jnp.arange(depth, dtype=jnp.int32)[None, :], place[None, :], 0),
        axis=1,
    )
    relative = (home % plane) ^ q
    slots = ((relative * depth + chunk) * locals_ + local) * capacity + within
    spread = (
        jnp.arange(plane * rows, dtype=jnp.int32)[:, None] == slots[None, :]
    ).astype(bf16)

    def dispatch(spread, values, *after):
        rows = spread.shape[0] // plane
        cut = spread.reshape(plane // 2, 2, rows, tok_count)
        first = [
            dot(cut[:, i].reshape(plane // 2 * rows, tok_count), values, ((1,), (0,))).astype(bf16)
            for i in range(2)
        ]
        if after:
            first[1] = tie(first[1], *after)
        sent = swap(first[1], 1)
        parts = [
            jnp.concatenate([v[m * rows : (m + 1) * rows] for v in (first[0], sent)], 0)
            for m in range(plane // 2)
        ]
        for bit in bits[1:]:
            got = swap(jnp.concatenate(parts[1::2], 0), bit)
            size = parts[0].shape[0]
            parts = [
                jnp.concatenate([v, got[i * size : (i + 1) * size]], 0)
                for i, v in enumerate(parts[::2])
            ]
        return parts[0]

    def give_back(values):
        parts = [values]
        for bit in bits[::-1]:
            size = parts[0].shape[0] // 2
            got = swap(jnp.concatenate([v[size:] for v in parts], 0), bit)
            parts = [v[:size] for v in parts] + [
                got[i * size : (i + 1) * size] for i in range(len(parts))
            ]
        index = [0]
        for bit in bits[::-1]:
            index = index + [m | bit for m in index]
        return jnp.concatenate([parts[index.index(m)] for m in range(plane)], 0)

    row_adapter = (jnp.arange(plane * rows) % rows) // capacity
    col_adapter = jnp.arange(depth * block) // rank
    mask = row_adapter[:, None] == col_adapter[None, :]

    def masked(values):
        return jnp.where(mask, values, 0.0).astype(bf16)

    def grad(hid, values, *more):
        out = adapter_scale * dot(hid, values, ((0,), (0,)))
        for m in more:
            out = out + m.astype(f32)
        return out

    def near(u1, d1):
        return jnp.where((z == 0) | (z == 2), d1, u1)

    def middle(u1, d1, e2):
        return jnp.where(edge, e2, jnp.where(z == 1, d1, u1))

    def spread_pair(p):
        return spread.reshape(plane, 2, rows // 2, tok_count)[:, p].reshape(-1, tok_count)

    whole = lax.all_gather(piece, ("chain", "side", "core", "groups"), axis=0, tiled=True)

    turned = [turn(up_rows, k) for k in range(1, depth)]
    cot = dispatch(spread, cotangent)
    spreads = [spread_pair(p) for p in range(2)]

    a = [down_rows[:, :half], down_rows[:, half:]]
    a[1] = tie(a[1], cot)
    one = [(up(v), down(v)) for v in a]
    x0 = dispatch(spreads[0], tokens, cot)
    x1 = dispatch(spreads[1], tokens, x0, *one[0])

    by_shift = jnp.stack([up_rows] + turned)
    up_all = jnp.concatenate(
        [
            lax.dynamic_index_in_dim(by_shift, (z - order[j] + depth) % depth, 0, False)
            for j in range(depth)
        ],
        axis=0,
    )
    hidden = masked(dot(cot, up_all, ((1,), (1,))))

    def pair(p):
        cut = hidden.reshape(plane, 2, rows // 2, depth * block)[:, p]
        return cut.reshape(plane * rows // 2, depth * block)[
            :, p * 2 * block : (p + 1) * 2 * block
        ]

    pairs = [pair(p) for p in range(2)]
    hid = [pairs[j // 2][:, j % 2 * block : (j % 2 + 1) * block] for j in range(depth)]
    second = jnp.where(edge, hid[1], hid[0])

    def lora(p, weights):
        return (adapter_scale * dot(pairs[p], weights, ((1,), (0,)))).astype(bf16)

    def cols(values, h):
        return values[:, h * half : (h + 1) * half]

    two = [None, None]
    for h in range(2):
        v = grad(hid[0], cols(x0, h)).astype(bf16)
        two[h] = (
            up(jnp.where(z == 0, v, one[h][0])),
            down(jnp.where(z == depth - 1, v, one[h][1])),
        )
    near_a = jnp.concatenate([near(*one[h]) for h in range(2)], 1)
    back_1 = give_back(tie(lora(1, jnp.concatenate([near_a, down_rows], 0)), x1))

    three, e2 = [None, None], [None, None]
    for h in range(2):
        uu, dd = two[h]
        e2[h] = jnp.where(z >= 2, uu, dd)
        r1 = jnp.where(edge, jnp.zeros_like(uu), jnp.where(z == 1, uu, dd))
        v = grad(second, cols(x0, h), r1).astype(bf16)
        send_up, send_down = jnp.where(z <= 1, v, e2[h]), jnp.where(z >= 2, v, e2[h])
        if h == 1:
            send_up, send_down = tie(send_up, x1), tie(send_down, x1)
        three[h] = up(send_up), down(send_down)

    four, far_a, back_0 = [None, None], [None, None], [None, None]
    for h in range(2):
        uu, dd = three[h]
        e3 = jnp.where(z == depth - 1, uu, dd)
        zero = jnp.zeros_like(uu)
        ru, rd = jnp.where(edge, zero, uu), jnp.where(edge, zero, dd)
        far_a[h] = jnp.concatenate([jnp.where(edge, e3, e2[h]), middle(*one[h], e2[h])], 0)
        y0, y1 = cols(x0, h), cols(x1, h)
        third_up = grad(hid[2], y1, ru)
        third_down = grad(hid[2], y1, rd)
        inner = grad(hid[1], y0)
        third_up = jnp.where(z == 1, inner + ru.astype(f32), third_up)
        third_down = jnp.where(z == 2, inner + rd.astype(f32), third_down)
        third_up, third_down = third_up.astype(bf16), third_down.astype(bf16)
        if h == 1:
            third_up, third_down = tie(third_up, back_1), tie(third_down, back_1)
        four[h] = up(third_up), down(third_down)
        back_0[h] = give_back(tie(lora(0, far_a[h]), back_1 if h == 0 else back_0[0]))
    far_a = jnp.concatenate(far_a, 1)
    back_0 = jnp.concatenate(back_0, 1)

    down_all = jnp.concatenate([far_a, near_a, down_rows], 0)

    def cut(values, p):
        return values.reshape(plane, 2, rows // 2, -1)[:, p].reshape(plane * rows // 2, -1)

    cots = [cut(cot, p) for p in range(2)]
    masks = [
        cut(mask, p)[:, p * 2 * block : (p + 1) * 2 * block] for p in range(2)
    ]
    shrunk = [
        jnp.where(
            masks[p],
            dot(v, down_all[p * 2 * block : (p + 1) * 2 * block], ((1,), (1,))),
            0.0,
        ).astype(bf16)
        for p, v in enumerate((x0, x1))
    ]
    up_parts = jnp.concatenate(
        [adapter_scale * dot(shrunk[p], cots[p], ((0,), (0,))) for p in range(2)], 0
    )
    up_own = up_parts[(depth - 1) * block :]
    up_parts = up_parts.astype(bf16).reshape(depth, block, features)
    up_sent = [
        turn(lax.dynamic_index_in_dim(up_parts, place[(z + k) % depth], 0, False), k)
        for k in range(1, depth)
    ]
    expanded = jnp.concatenate(
        [
            (
                adapter_scale
                * dot(shrunk[p], up_all[p * 2 * block : (p + 1) * 2 * block], ((1,), (0,)))
            ).astype(bf16)
            for p in range(2)
        ],
        1,
    )
    frozen_out = dot(tokens, whole, ((1,), (0,)))
    frozen_grad = dot(cotangent, whole, ((1,), (1,)))
    expanded = give_back(tie(expanded, back_0, frozen_out, frozen_grad))

    key_output = (
        frozen_out
        + dot(spreads[0], expanded[:, :features], ((0,), (0,)))
        + dot(spreads[1], expanded[:, features:], ((0,), (0,)))
    ).astype(bf16)
    token_grad = (
        frozen_grad
        + dot(spreads[1], back_1, ((0,), (0,)))
        + dot(spreads[0], back_0, ((0,), (0,)))
    ).astype(bf16)
    down_grad = grad(hid[3], x1, *(jnp.concatenate(v, 1) for v in zip(*four)))
    up_grad = up_own + sum(v.astype(f32) for v in up_sent)
    down_grad = jnp.transpose(down_grad.reshape(locals_, rank, width), (0, 2, 1))
    up_grad = up_grad.reshape(locals_, rank, features)
    return key_output, token_grad, down_grad, up_grad


def solution(mesh):
    groups, wide = mesh.devices.shape
    fine = Mesh(
        mesh.devices.reshape(groups, CHAIN, wide // CHAIN // 2, 2),
        ("groups", "chain", "side", "core"),
    )
    every = ("groups", "chain", "side", "core")
    return jax.shard_map(
        shards,
        mesh=fine,
        in_specs=(
            P(every, None),
            P(every, None),
            P(every[1:], None),
            P(every, None, None),
            P(every, None, None),
            P(every, None),
            P("groups"),
        ),
        out_specs=(
            P(every, None),
            P(every, None),
            P(every, None, None),
            P(every, None, None),
        ),
        check_vma=False,
    )
```

time: 529 us -> 539 us (1.019); the launches traced: 519 us -> 535 us
  waiting for transfers between devices: 187 us -> 241 us
  local copies, waits for them, and re-layouts: 88.3 us -> 40.6 us
  starting transfers between devices: 73.6 us -> 96.7 us
  other arithmetic: 45.8 us -> 36.7 us
  between operations: 31 us -> 23.9 us
    ppermute x8, waiting for transfers between devices: 64.2 us -> 21.8 us  [down(): return lax.ppermute(values, 'chain', [(i + 1, i) for i in range(depth - 1)])]
    ppermute x8, waiting for transfers between devices: 28.7 us -> 65.5 us  [up(): return lax.ppermute(values, 'chain', [(i, i + 1) for i in range(depth - 1)])]
    ppermute x10 -> x7, waiting for transfers between devices: 87.2 us -> 118 us  [swap(): lax.ppermute(values, 'side', [(i, i ^ bit // 2) for i in range(sides)])]
    ppermute x6, waiting for transfers between devices: 6.93 us -> 33 us  [turn(): lax.ppermute(values, 'chain', [(i, (i + k) % depth) for i in range(depth)])]
    unnamed x172 -> x152, local copies, waits for them, and re-layouts: 22.2 us -> 4.63 us
    ppermute x6, starting transfers between devices: 10.8 us -> 23.6 us  [turn(): lax.ppermute(values, 'chain', [(i, (i + k) % depth) for i in range(depth)])]
    ppermute x8, starting transfers between devices: 40.6 us -> 51.4 us  [up(): return lax.ppermute(values, 'chain', [(i, i + 1) for i in range(depth - 1)])]
    transpose x2 -> x0, local copies, waits for them, and re-layouts: 9.31 us -> none  [join_rest(): everything = jnp.transpose(everything, (2, 3, 1, 0, 4, 5))]
  transfers between devices with their start and end apart: 42 -> 37, of which waited for: 14 -> 18; matrix products, arithmetic and copies ran while one was open for 32% -> 27% of each run, Pallas kernels for 0% -> 0%
where the time goes in v3:
time: 539 us; the launch traced here: 535 us
  waiting for transfers between devices  241 us (45%)
  starting transfers between devices  96.7 us (18%)
  matrix products  95.5 us (18%)
  local copies, waits for them, and re-layouts  40.6 us (8%)
  other arithmetic  36.7 us (7%)
  between operations  23.9 us (4%)
    ppermute x7, waiting for transfers between devices, swap(): lax.ppermute(values, 'side', [(i, i ^ bit // 2) for i in range(sides)])  118 us
    dot_general x31, matrix products, dot(): return lax.dot_general(a, b, (dims, ((), ())), preferred_element_type=f32)  95.5 us
    ppermute x8, waiting for transfers between devices, up(): return lax.ppermute(values, 'chain', [(i, i + 1) for i in range(depth - 1)])  65.5 us
    ppermute x8, starting transfers between devices, up(): return lax.ppermute(values, 'chain', [(i, i + 1) for i in range(depth - 1)])  51.4 us
    ppermute x6, waiting for transfers between devices, turn(): lax.ppermute(values, 'chain', [(i, (i + k) % depth) for i in range(depth)])  33 us
    ppermute x6, starting transfers between devices, turn(): lax.ppermute(values, 'chain', [(i, (i + k) % depth) for i in range(depth)])  23.6 us
    ppermute x8, waiting for transfers between devices, down(): return lax.ppermute(values, 'chain', [(i + 1, i) for i in range(depth - 1)])  21.8 us
    ppermute x7, starting transfers between devices, swap(): lax.ppermute(values, 'side', [(i, i ^ bit // 2) for i in range(sides)])  10.8 us
  transfers between devices with their start and end apart: 37, of which 18 were waited for; matrix products, arithmetic and copies ran while one was open for 27% of the time, Pallas kernels for 0%

profile of v3, /device:TPU:0, one launch (start us, length us, event | category | flops | bytes accessed | tf_op | source)
XLA Modules:
  0.0 534.8 jit_solution(11035956344376079293)
XLA Ops:
  7.2 5.1 collective-permute-start.6
  23.6 3.0 convolution_convert_fusion.1
  33.3 2.9 convolution_convert_fusion.3
  36.2 8.7 %collective-permute-done.1 = bf16[208,1024]{1,0:T(8,128)(2,1)} collective-permute-done((bf16[208,1024]{1,0:T(8,128)(2,1)}, bf16[208,1024]{1,0:T(8,128)(2,1)}, u32[]{:S(2)}, u32[]{:S(2)}) %collective-permute-start.1) | collective-permute-done | bytes 426016 | tf_op jit(solution)/shard_map/ppermute | solution.py:67
  44.8 2.1 pad_maximum_fusion.16.refs_1_
  48.1 2.7 collective-permute-done.2
  58.8 4.6 collective-permute-start.7
  66.9 5.6 %collective-permute-start.13 = (bf16[128,4096]{1,0:T(8,128)(2,1)}, bf16[128,4096]{1,0:T(8,128)(2,1)}, u32[]{:S(2)}, u32[]{:S(2)}) collective-permute-start(bf16[128,4096]{1,0:T(8,128)(2,1)} %shard_map.121), channel_id=1, source_target_pairs={{0,4},{4,8},{8,12},{1,5},{5,9},{9,13},{2,6},{6,10},{10,14},{3,7},{... | collective-permute-start | bytes 3145736 | tf_op jit(solution)/shard_map/ppermute | solution.py:73
  75.8 23.3 %collective-permute-done.3 = bf16[104,8192]{1,0:T(8,128)(2,1)} collective-permute-done((bf16[104,8192]{1,0:T(8,128)(2,1)S(1)}, bf16[104,8192]{1,0:T(8,128)(2,1)}, u32[]{:S(2)}, u32[]{:S(2)}) %collective-permute-start.3) | collective-permute-done | bytes 1703968 | tf_op jit(solution)/shard_map/ppermute | solution.py:67
  99.1 2.2 pad_maximum_fusion.1.refs_1_
  101.3 4.5 collective-permute-done.7.refs_2_
  105.8 3.1 broadcast_select_fusion.11
  110.2 6.3 %collective-permute-start.8 = (bf16[128,4096]{1,0:T(8,128)(2,1)}, bf16[128,4096]{1,0:T(8,128)(2,1)}, u32[]{:S(2)}, u32[]{:S(2)}) collective-permute-start(bf16[128,4096]{1,0:T(8,128)(2,1)} %get-tuple-element.45), channel_id=1, source_target_pairs={{0,4},{4,8},{8,12},{1,5},{5,9},{9,13},{2,6},{6,10},{10,14},{3,7},{... | collective-permute-start | bytes 3145736 | tf_op jit(solution)/shard_map/ppermute | solution.py:73
  127.8 4.2 convolution_convert_fusion.refs_0_
  134.7 12.3 %collective-permute-done.13 = bf16[128,4096]{1,0:T(8,128)(2,1)} collective-permute-done((bf16[128,4096]{1,0:T(8,128)(2,1)}, bf16[128,4096]{1,0:T(8,128)(2,1)}, u32[]{:S(2)}, u32[]{:S(2)}) %collective-permute-start.13) | collective-permute-done | bytes 1048608 | tf_op jit(solution)/shard_map/ppermute | solution.py:73
  150.1 15.0 %collective-permute-start.14 = (bf16[128,4096]{1,0:T(8,128)(2,1)S(1)}, bf16[128,4096]{1,0:T(8,128)(2,1)S(1)}, u32[]{:S(2)}, u32[]{:S(2)}) collective-permute-start(bf16[128,4096]{1,0:T(8,128)(2,1)S(1)} %get-tuple-element.48), channel_id=1, source_target_pairs={{0,4},{4,8},{8,12},{1,5},{5,9},{9,13},{2,6},{6,10},{10,14},{3,7},{... | collective-permute-start | bytes 3145736 | tf_op jit(solution)/shard_map/ppermute | solution.py:73
  165.0 16.1 %collective-permute-done.10 = bf16[128,4096]{1,0:T(8,128)(2,1)} collective-permute-done((bf16[128,4096]{1,0:T(8,128)(2,1)}, bf16[128,4096]{1,0:T(8,128)(2,1)}, u32[]{:S(2)}, u32[]{:S(2)}) %collective-permute-start.10) | collective-permute-done | bytes 1048608 | tf_op jit(solution)/shard_map/ppermute | solution.py:76
  181.1 10.8 %collective-permute-done.8 = bf16[128,4096]{1,0:T(8,128)(2,1)} collective-permute-done((bf16[128,4096]{1,0:T(8,128)(2,1)}, bf16[128,4096]{1,0:T(8,128)(2,1)}, u32[]{:S(2)}, u32[]{:S(2)}) %collective-permute-start.8) | collective-permute-done | bytes 1048608 | tf_op jit(solution)/shard_map/ppermute | solution.py:73
  191.9 2.2 broadcast_select_fusion.4
  194.3 6.3 %collective-permute-start.11 = (bf16[128,4096]{1,0:T(8,128)(2,1)S(1)}, bf16[128,4096]{1,0:T(8,128)(2,1)S(1)}, u32[]{:S(2)}, u32[]{:S(2)}) collective-permute-start(bf16[128,4096]{1,0:T(8,128)(2,1)S(1)} %broadcast_select_fusion.9), channel_id=1, source_target_pairs={{0,4},{4,8},{8,12},{1,5},{5,9},{9,13},{2,6},{6,10},{10,14},{3,7},{... | collective-permute-start | bytes 3145736 | tf_op jit(solution)/shard_map/ppermute | solution.py:73
  203.5 14.7 %collective-permute-done.14 = bf16[128,4096]{1,0:T(8,128)(2,1)S(1)} collective-permute-done((bf16[128,4096]{1,0:T(8,128)(2,1)S(1)}, bf16[128,4096]{1,0:T(8,128)(2,1)S(1)}, u32[]{:S(2)}, u32[]{:S(2)}) %collective-permute-start.14) | collective-permute-done | bytes 1048608 | tf_op jit(solution)/shard_map/ppermute | solution.py:73
  224.6 15.6 %collective-permute-done.11 = bf16[128,4096]{1,0:T(8,128)(2,1)S(1)} collective-permute-done((bf16[128,4096]{1,0:T(8,128)(2,1)S(1)}, bf16[128,4096]{1,0:T(8,128)(2,1)S(1)}, u32[]{:S(2)}, u32[]{:S(2)}) %collective-permute-start.11) | collective-permute-done | bytes 1048608 | tf_op jit(solution)/shard_map/ppermute | solution.py:73
  240.2 3.5 select_select_fusion.2
  245.6 14.6 %collective-permute-done.18 = bf16[104,8192]{1,0:T(8,128)(2,1)S(1)} collective-permute-done((bf16[104,8192]{1,0:T(8,128)(2,1)S(1)}, bf16[104,8192]{1,0:T(8,128)(2,1)S(1)}, u32[]{:S(2)}, u32[]{:S(2)}) %collective-permute-start.18) | collective-permute-done | bytes 1703968 | tf_op jit(solution)/shard_map/ppermute | solution.py:67
  262.2 4.7 collective-permute-start.19
  269.6 3.4 fusion.26
  274.4 6.9 %collective-permute-start.29 = (bf16[128,4096]{1,0:T(8,128)(2,1)}, bf16[128,4096]{1,0:T(8,128)(2,1)}, u32[]{:S(2)}, u32[]{:S(2)}) collective-permute-start(bf16[128,4096]{1,0:T(8,128)(2,1)} %get-tuple-element.13), channel_id=1, source_target_pairs={{0,4},{4,8},{8,12},{1,5},{5,9},{9,13},{2,6},{6,10},{10,14},{3,7},{... | collective-permute-start | bytes 3145736 | tf_op jit(solution)/shard_map/ppermute | solution.py:73
  283.1 7.7 %collective-permute-done.19 = bf16[128,4096]{1,0:T(8,128)(2,1)S(1)} collective-permute-done((bf16[128,4096]{1,0:T(8,128)(2,1)}, bf16[128,4096]{1,0:T(8,128)(2,1)S(1)}, u32[]{:S(2)}, u32[]{:S(2)}) %collective-permute-start.19) | collective-permute-done | bytes 1048608 | tf_op jit(solution)/shard_map/ppermute | solution.py:73
  290.8 4.4 collective-permute-done.20
  295.2 2.2 select_select_fusion
  298.5 9.2 %fusion.2.refs_0_ = bf16[208,8192]{1,0:T(8,128)(2,1)} fusion(bf16[128,8192]{1,0:T(8,128)(2,1)S(1)} %bitcast.103, bf16[128,4096]{1,0:T(8,128)(2,1)S(1)} %get-tuple-element.21, bf16[128,4096]{1,0:T(8,128)(2,1)S(1)} %copy-done.43, bf16[208,512]{1,0:T(8,128)(2,1)S(1)} %copy-done.58), kind=kOutput, calls=%fused_computation.5 | convolution fusion | flops 888406016 | bytes 7708672 | tf_op jit(solution)/shard_map/dot_general | solution.py:16
  311.2 2.9 fusion.52
  314.4 29.2 %collective-permute-done.21 = bf16[104,8192]{1,0:T(8,128)(2,1)S(1)} collective-permute-done((bf16[104,8192]{1,0:T(8,128)(2,1)S(1)}, bf16[104,8192]{1,0:T(8,128)(2,1)S(1)}, u32[]{:S(2)}, u32[]{:S(2)}) %collective-permute-start.21) | collective-permute-done | bytes 1703968 | tf_op jit(solution)/shard_map/ppermute | solution.py:67
  351.0 2.2 pad_maximum_fusion.3.refs_1_
  358.4 17.5 %collective-permute-done.23 = bf16[104,4096]{1,0:T(8,128)(2,1)S(1)} collective-permute-done((bf16[104,4096]{1,0:T(8,128)(2,1)S(1)}, bf16[104,4096]{1,0:T(8,128)(2,1)S(1)}, u32[]{:S(2)}, u32[]{:S(2)}) %collective-permute-start.23) | collective-permute-done | bytes 852000 | tf_op jit(solution)/shard_map/ppermute | solution.py:67
  380.7 13.4 %collective-permute-start.35 = (bf16[128,1024]{1,0:T(8,128)(2,1)}, bf16[128,1024]{1,0:T(8,128)(2,1)}, u32[]{:S(2)}, u32[]{:S(2)}) collective-permute-start(bf16[128,1024]{1,0:T(8,128)(2,1)} %get-tuple-element.41), channel_id=1, source_target_pairs={{0,12},{4,0},{8,4},{12,8},{1,13},{5,1},{9,5},{13,9},{2,14},{6,2},{... | collective-permute-start | bytes 786440 | tf_op jit(solution)/shard_map/ppermute | solution.py:70
  396.0 2.5 fusion.28
  400.8 2.6 pad_maximum_fusion.9.refs_1_
  410.0 15.7 %collective-permute-done.25 = bf16[104,4096]{1,0:T(8,128)(2,1)S(1)} collective-permute-done((bf16[104,4096]{1,0:T(8,128)(2,1)S(1)}, bf16[104,4096]{1,0:T(8,128)(2,1)S(1)}, u32[]{:S(2)}, u32[]{:S(2)}) %collective-permute-start.25) | collective-permute-done | bytes 852000 | tf_op jit(solution)/shard_map/ppermute | solution.py:67
  427.1 2.2 collective-permute-start.34
  429.4 33.0 %collective-permute-done.34 = bf16[128,1024]{1,0:T(8,128)(2,1)S(1)} collective-permute-done((bf16[128,1024]{1,0:T(8,128)(2,1)S(1)}, bf16[128,1024]{1,0:T(8,128)(2,1)S(1)}, u32[]{:S(2)}, u32[]{:S(2)}) %collective-permute-start.34) | collective-permute-done | bytes 262176 | tf_op jit(solution)/shard_map/ppermute | solution.py:70
  465.4 5.0 fusion.4
  470.6 6.8 %maximum_maximum_fusion.refs_1_ = bf16[208,8192]{1,0:T(8,128)(2,1)S(1)} fusion(bf16[52,4096]{1,0:T(8,128)(2,1)S(1)} %get-tuple-element.58, bf16[52,4096]{1,0:T(8,128)(2,1)S(1)} %get-tuple-element.59, bf16[52,4096]{1,0:T(8,128)(2,1)S(1)} %get-tuple-element.57, bf16[52,4096]{1,0:T(8,128)(2,1)S(1)} %get-tuple-element.24, bf16[52,4096]{1,0:T(8,128)(2,1)S(1)} %copy-done.22, ...), kind=kLoop, calls=%fused_computation.43 | loop fusion | flops 27262976 | bytes 6815744 | tf_op jit(solution)/shard_map/concatenate | solution.py:238
  477.4 4.7 fusion.133
  482.1 12.6 %convolution_bitcast_fusion.1.refs_2_ = f32[256,1024]{1,0:T(8,128)} fusion(bf16[256,8192]{1,0:T(8,128)(2,1)} %param.9, bf16[8192,1024]{1,0:T(8,128)(2,1)} %all-gather.2.cloned.1.call-done), kind=kOutput, calls=%fused_computation.73 | convolution fusion | flops 4294967296 | bytes 22020096 | tf_op jit(solution)/shard_map/dot_general | solution.py:16
  494.7 6.8 %convolution_bitcast_fusion.refs_3_ = f32[256,8192]{1,0:T(8,128)} fusion(bf16[8192,1024]{1,0:T(8,128)(2,1)S(1)} %copy-done.75, bf16[256,1024]{1,0:T(8,128)(2,1)S(1)} %copy-done.32), kind=kOutput, calls=%fused_computation.2 | convolution fusion | flops 4294967296 | bytes 25690112 | tf_op jit(solution)/shard_map/dot_general | solution.py:16
  505.6 9.4 %collective-permute-done.27 = bf16[104,2048]{1,0:T(8,128)(2,1)S(1)} collective-permute-done((bf16[104,2048]{1,0:T(8,128)(2,1)S(1)}, bf16[104,2048]{1,0:T(8,128)(2,1)S(1)}, u32[]{:S(2)}, u32[]{:S(2)}) %collective-permute-start.27) | collective-permute-done | bytes 426016 | tf_op jit(solution)/shard_map/ppermute | solution.py:67
  515.2 9.8 %fusion.1 = bf16[256,8192]{1,0:T(8,128)(2,1)} fusion(f32[256,8192]{1,0:T(8,128)} %fusion.133, f32[256,8192]{1,0:T(8,128)} %convolution_bitcast_fusion.refs_3_, pred[208,256]{1,0:T(8,128)(4,1)S(1)} %copy-done.59, bf16[208,8192]{1,0:T(8,128)(2,1)S(1)} %copy-done.4), kind=kOutput, calls=%fused_computation.4 | convolution fusion | flops 878706688 | bytes 24432640 | tf_op jit(solution)/shard_map/dot_general | solution.py:16
  (311 shorter events, 106.8 us)
Async XLA Ops:
  7.2 474.9 %all-gather.2.cloned.1.call-start = ((), (), s32[]{:S(2)}) async-start(), calls=%async_computation | async-start | bytes 17301504 | tf_op jit(solution)/shard_map/all_gather | solution.py:160
  7.2 51.6 %collective-permute-start.6 = (bf16[128,1024]{1,0:T(8,128)(2,1)}, bf16[128,1024]{1,0:T(8,128)(2,1)}, u32[]{:S(2)}, u32[]{:S(2)}) collective-permute-start(bf16[128,1024]{1,0:T(8,128)(2,1)} %bitcast.108), channel_id=1, source_target_pairs={{0,12},{4,0},{8,4},{12,8},{1,13},{5,1},{9,5},{13,9},{2,14},{6,2},{... | collective-permute-start | bytes 786440 | tf_op jit(solution)/shard_map/ppermute | solution.py:70
  12.3 51.1 %collective-permute-start.5 = (bf16[128,1024]{1,0:T(8,128)(2,1)}, bf16[128,1024]{1,0:T(8,128)(2,1)}, u32[]{:S(2)}, u32[]{:S(2)}) collective-permute-start(bf16[128,1024]{1,0:T(8,128)(2,1)} %bitcast.109), channel_id=1, source_target_pairs={{0,8},{4,12},{8,0},{12,4},{1,9},{5,13},{9,1},{13,5},{2,10},{6,14},... | collective-permute-start | bytes 786440 | tf_op jit(solution)/shard_map/ppermute | solution.py:70
  12.3 51.1 %collective-permute-start.4 = (bf16[128,1024]{1,0:T(8,128)(2,1)}, bf16[128,1024]{1,0:T(8,128)(2,1)}, u32[]{:S(2)}, u32[]{:S(2)}) collective-permute-start(bf16[128,1024]{1,0:T(8,128)(2,1)} %bitcast.110), channel_id=1, source_target_pairs={{0,4},{4,8},{8,12},{12,0},{1,5},{5,9},{9,13},{13,1},{2,6},{6,10},{... | collective-permute-start | bytes 786440 | tf_op jit(solution)/shard_map/ppermute | solution.py:70
  18.7 7.9 %collective-permute-start = (bf16[208,1024]{1,0:T(8,128)(2,1)}, bf16[208,1024]{1,0:T(8,128)(2,1)}, u32[]{:S(2)}, u32[]{:S(2)}) collective-permute-start(bf16[208,1024]{1,0:T(8,128)(2,1)} %convolution_convert_fusion.4), channel_id=1, source_target_pairs={{0,1},{1,0},{2,3},{3,2},{4,5},{5,4},{6,7},{7,6},{8,9},{9,8},{10,11... | collective-permute-start | bytes 1277960 | tf_op jit(solution)/shard_map/ppermute | solution.py:66
  21.0 80.3 %collective-permute-start.9 = (bf16[128,4096]{1,0:T(8,128)(2,1)}, bf16[128,4096]{1,0:T(8,128)(2,1)}, u32[]{:S(2)}, u32[]{:S(2)}) collective-permute-start(bf16[128,4096]{1,0:T(8,128)(2,1)} %get-tuple-element.23), channel_id=1, source_target_pairs={{4,0},{8,4},{12,8},{5,1},{9,5},{13,9},{6,2},{10,6},{14,10},{7,3},{... | collective-permute-start | bytes 3145736 | tf_op jit(solution)/shard_map/ppermute | solution.py:76
  29.2 15.7 %collective-permute-start.1 = (bf16[208,1024]{1,0:T(8,128)(2,1)}, bf16[208,1024]{1,0:T(8,128)(2,1)}, u32[]{:S(2)}, u32[]{:S(2)}) collective-permute-start(bf16[208,1024]{1,0:T(8,128)(2,1)} %pad_maximum_fusion.21), channel_id=1, source_target_pairs={{0,2},{2,0},{1,3},{3,1},{4,6},{6,4},{5,7},{7,5},{8,10},{10,8},{9,1... | collective-permute-start | bytes 1277960 | tf_op jit(solution)/shard_map/ppermute | solution.py:67
  46.9 3.8 collective-permute-start.2
  52.1 46.9 %collective-permute-start.3 = (bf16[104,8192]{1,0:T(8,128)(2,1)S(1)}, bf16[104,8192]{1,0:T(8,128)(2,1)}, u32[]{:S(2)}, u32[]{:S(2)}) collective-permute-start(bf16[104,8192]{1,0:T(8,128)(2,1)S(1)} %pad_maximum_fusion.6), channel_id=1, source_target_pairs={{0,2},{2,0},{1,3},{3,1},{4,6},{6,4},{5,7},{7,5},{8,10},{10,8},{9,1... | collective-permute-start | bytes 5111816 | tf_op jit(solution)/shard_map/ppermute | solution.py:67
  58.8 47.0 %collective-permute-start.7 = (bf16[128,4096]{1,0:T(8,128)(2,1)}, bf16[128,4096]{1,0:T(8,128)(2,1)}, u32[]{:S(2)}, u32[]{:S(2)}) collective-permute-start(bf16[128,4096]{1,0:T(8,128)(2,1)} %get-tuple-element.23), channel_id=1, source_target_pairs={{0,4},{4,8},{8,12},{1,5},{5,9},{9,13},{2,6},{6,10},{10,14},{3,7},{... | collective-permute-start | bytes 3145736 | tf_op jit(solution)/shard_map/ppermute | solution.py:73
  65.6 69.0 %collective-permute-start.15 = (bf16[128,4096]{1,0:T(8,128)(2,1)}, bf16[128,4096]{1,0:T(8,128)(2,1)}, u32[]{:S(2)}, u32[]{:S(2)}) collective-permute-start(bf16[128,4096]{1,0:T(8,128)(2,1)} %shard_map.121), channel_id=1, source_target_pairs={{4,0},{8,4},{12,8},{5,1},{9,5},{13,9},{6,2},{10,6},{14,10},{7,3},{... | collective-permute-start | bytes 3145736 | tf_op jit(solution)/shard_map/ppermute | solution.py:76
  66.9 80.0 %collective-permute-start.13 = (bf16[128,4096]{1,0:T(8,128)(2,1)}, bf16[128,4096]{1,0:T(8,128)(2,1)}, u32[]{:S(2)}, u32[]{:S(2)}) collective-permute-start(bf16[128,4096]{1,0:T(8,128)(2,1)} %shard_map.121), channel_id=1, source_target_pairs={{0,4},{4,8},{8,12},{1,5},{5,9},{9,13},{2,6},{6,10},{10,14},{3,7},{... | collective-permute-start | bytes 3145736 | tf_op jit(solution)/shard_map/ppermute | solution.py:73
  108.9 72.2 %collective-permute-start.10 = (bf16[128,4096]{1,0:T(8,128)(2,1)}, bf16[128,4096]{1,0:T(8,128)(2,1)}, u32[]{:S(2)}, u32[]{:S(2)}) collective-permute-start(bf16[128,4096]{1,0:T(8,128)(2,1)} %get-tuple-element.44), channel_id=1, source_target_pairs={{4,0},{8,4},{12,8},{5,1},{9,5},{13,9},{6,2},{10,6},{14,10},{7,3},{... | collective-permute-start | bytes 3145736 | tf_op jit(solution)/shard_map/ppermute | solution.py:76
  110.2 81.7 %collective-permute-start.8 = (bf16[128,4096]{1,0:T(8,128)(2,1)}, bf16[128,4096]{1,0:T(8,128)(2,1)}, u32[]{:S(2)}, u32[]{:S(2)}) collective-permute-start(bf16[128,4096]{1,0:T(8,128)(2,1)} %get-tuple-element.45), channel_id=1, source_target_pairs={{0,4},{4,8},{8,12},{1,5},{5,9},{9,13},{2,6},{6,10},{10,14},{3,7},{... | collective-permute-start | bytes 3145736 | tf_op jit(solution)/shard_map/ppermute | solution.py:73
  134.7 57.2 %copy-start.60 = (bf16[208,512]{1,0:T(8,128)(2,1)S(1)}, bf16[208,512]{1,0:T(8,128)(2,1)}, u32[]{:S(2)}) copy-start(bf16[208,512]{1,0:T(8,128)(2,1)} %reshape_squeeze.48) | copy-start | bytes 638980
  134.7 85.2 %collective-permute-start.17 = (bf16[104,8192]{1,0:T(8,128)(2,1)}, bf16[104,8192]{1,0:T(8,128)(2,1)S(1)}, u32[]{:S(2)}, u32[]{:S(2)}) collective-permute-start(bf16[104,8192]{1,0:T(8,128)(2,1)} %shard_map.122), channel_id=1, source_target_pairs={{0,1},{1,0},{2,3},{3,2},{4,5},{5,4},{6,7},{7,6},{8,9},{9,8},{10,11... | collective-permute-start | bytes 5111816 | tf_op jit(solution)/shard_map/ppermute | solution.py:66
  148.8 54.7 %collective-permute-start.16 = (bf16[128,4096]{1,0:T(8,128)(2,1)S(1)}, bf16[128,4096]{1,0:T(8,128)(2,1)S(1)}, u32[]{:S(2)}, u32[]{:S(2)}) collective-permute-start(bf16[128,4096]{1,0:T(8,128)(2,1)S(1)} %get-tuple-element.47), channel_id=1, source_target_pairs={{4,0},{8,4},{12,8},{5,1},{9,5},{13,9},{6,2},{10,6},{14,10},{7,3},{... | collective-permute-start | bytes 3145736 | tf_op jit(solution)/shard_map/ppermute | solution.py:76
  150.1 68.0 %collective-permute-start.14 = (bf16[128,4096]{1,0:T(8,128)(2,1)S(1)}, bf16[128,4096]{1,0:T(8,128)(2,1)S(1)}, u32[]{:S(2)}, u32[]{:S(2)}) collective-permute-start(bf16[128,4096]{1,0:T(8,128)(2,1)S(1)} %get-tuple-element.48), channel_id=1, source_target_pairs={{0,4},{4,8},{8,12},{1,5},{5,9},{9,13},{2,6},{6,10},{10,14},{3,7},{... | collective-permute-start | bytes 3145736 | tf_op jit(solution)/shard_map/ppermute | solution.py:73
  194.3 46.0 %collective-permute-start.11 = (bf16[128,4096]{1,0:T(8,128)(2,1)S(1)}, bf16[128,4096]{1,0:T(8,128)(2,1)S(1)}, u32[]{:S(2)}, u32[]{:S(2)}) collective-permute-start(bf16[128,4096]{1,0:T(8,128)(2,1)S(1)} %broadcast_select_fusion.9), channel_id=1, source_target_pairs={{0,4},{4,8},{8,12},{1,5},{5,9},{9,13},{2,6},{6,10},{10,14},{3,7},{... | collective-permute-start | bytes 3145736 | tf_op jit(solution)/shard_map/ppermute | solution.py:73
  200.6 39.7 %collective-permute-start.12 = (bf16[128,4096]{1,0:T(8,128)(2,1)S(1)}, bf16[128,4096]{1,0:T(8,128)(2,1)S(1)}, u32[]{:S(2)}, u32[]{:S(2)}) collective-permute-start(bf16[128,4096]{1,0:T(8,128)(2,1)S(1)} %get-tuple-element.6), channel_id=1, source_target_pairs={{4,0},{8,4},{12,8},{5,1},{9,5},{13,9},{6,2},{10,6},{14,10},{7,3},{... | collective-permute-start | bytes 3145736 | tf_op jit(solution)/shard_map/ppermute | solution.py:76
  221.6 38.6 %collective-permute-start.18 = (bf16[104,8192]{1,0:T(8,128)(2,1)S(1)}, bf16[104,8192]{1,0:T(8,128)(2,1)S(1)}, u32[]{:S(2)}, u32[]{:S(2)}) collective-permute-start(bf16[104,8192]{1,0:T(8,128)(2,1)S(1)} %pad_maximum_fusion.7), channel_id=1, source_target_pairs={{0,2},{2,0},{1,3},{3,1},{4,6},{6,4},{5,7},{7,5},{8,10},{10,8},{9,1... | collective-permute-start | bytes 5111816 | tf_op jit(solution)/shard_map/ppermute | solution.py:67
  262.2 28.6 %collective-permute-start.19 = (bf16[128,4096]{1,0:T(8,128)(2,1)}, bf16[128,4096]{1,0:T(8,128)(2,1)S(1)}, u32[]{:S(2)}, u32[]{:S(2)}) collective-permute-start(bf16[128,4096]{1,0:T(8,128)(2,1)} %shard_map.123), channel_id=1, source_target_pairs={{0,4},{4,8},{8,12},{1,5},{5,9},{9,13},{2,6},{6,10},{10,14},{3,7},{... | collective-permute-start | bytes 3145736 | tf_op jit(solution)/shard_map/ppermute | solution.py:73
  267.0 28.2 %collective-permute-start.20 = (bf16[128,4096]{1,0:T(8,128)(2,1)}, bf16[128,4096]{1,0:T(8,128)(2,1)S(1)}, u32[]{:S(2)}, u32[]{:S(2)}) collective-permute-start(bf16[128,4096]{1,0:T(8,128)(2,1)} %shard_map.124), channel_id=1, source_target_pairs={{4,0},{8,4},{12,8},{5,1},{9,5},{13,9},{6,2},{10,6},{14,10},{7,3},{... | collective-permute-start | bytes 3145736 | tf_op jit(solution)/shard_map/ppermute | solution.py:76
  273.0 192.4 %collective-permute-start.31 = (bf16[128,4096]{1,0:T(8,128)(2,1)}, bf16[128,4096]{1,0:T(8,128)(2,1)}, u32[]{:S(2)}, u32[]{:S(2)}) collective-permute-start(bf16[128,4096]{1,0:T(8,128)(2,1)} %get-tuple-element.12), channel_id=1, source_target_pairs={{4,0},{8,4},{12,8},{5,1},{9,5},{13,9},{6,2},{10,6},{14,10},{7,3},{... | collective-permute-start | bytes 3145736 | tf_op jit(solution)/shard_map/ppermute | solution.py:76
  274.4 191.0 %collective-permute-start.29 = (bf16[128,4096]{1,0:T(8,128)(2,1)}, bf16[128,4096]{1,0:T(8,128)(2,1)}, u32[]{:S(2)}, u32[]{:S(2)}) collective-permute-start(bf16[128,4096]{1,0:T(8,128)(2,1)} %get-tuple-element.13), channel_id=1, source_target_pairs={{0,4},{4,8},{8,12},{1,5},{5,9},{9,13},{2,6},{6,10},{10,14},{3,7},{... | collective-permute-start | bytes 3145736 | tf_op jit(solution)/shard_map/ppermute | solution.py:73
  309.4 34.2 %collective-permute-start.21 = (bf16[104,8192]{1,0:T(8,128)(2,1)S(1)}, bf16[104,8192]{1,0:T(8,128)(2,1)S(1)}, u32[]{:S(2)}, u32[]{:S(2)}) collective-permute-start(bf16[104,8192]{1,0:T(8,128)(2,1)S(1)} %slice.373), channel_id=1, source_target_pairs={{0,2},{2,0},{1,3},{3,1},{4,6},{6,4},{5,7},{7,5},{8,10},{10,8},{9,1... | collective-permute-start | bytes 5111816 | tf_op jit(solution)/shard_map/ppermute | solution.py:67
  314.3 30.2 %copy-start.3 = (bf16[208,8192]{1,0:T(8,128)(2,1)S(1)}, bf16[208,8192]{1,0:T(8,128)(2,1)}, u32[]{:S(2)}) copy-start(bf16[208,8192]{1,0:T(8,128)(2,1)} %pad_maximum_fusion.2.refs_1_) | copy-start | bytes 10223620
  314.3 30.2 %copy-start.29 = (bf16[2,8192,64]{1,2,0:T(8,128)(2,1)S(1)}, bf16[2,8192,64]{1,2,0:T(8,128)(2,1)}, u32[]{:S(2)}) copy-start(bf16[2,8192,64]{1,2,0:T(8,128)(2,1)} %param.12) | copy-start | bytes 6291460
  314.4 30.2 %copy-start.44 = (bf16[128,4096]{1,0:T(8,128)(2,1)S(1)}, bf16[128,4096]{1,0:T(8,128)(2,1)}, u32[]{:S(2)}) copy-start(bf16[128,4096]{1,0:T(8,128)(2,1)} %get-tuple-element.19) | copy-start | bytes 3145732
  314.4 30.2 %copy-start.51 = (bf16[128,4096]{1,0:T(8,128)(2,1)S(1)}, bf16[128,4096]{1,0:T(8,128)(2,1)}, u32[]{:S(2)}) copy-start(bf16[128,4096]{1,0:T(8,128)(2,1)} %copy-done.50) | copy-start | bytes 3145732
  344.1 6.7 %collective-permute-start.22 = (bf16[104,8192]{1,0:T(8,128)(2,1)S(1)}, bf16[104,8192]{1,0:T(8,128)(2,1)S(1)}, u32[]{:S(2)}, u32[]{:S(2)}) collective-permute-start(bf16[104,8192]{1,0:T(8,128)(2,1)S(1)} %pad_maximum_fusion.8), channel_id=1, source_target_pairs={{0,1},{1,0},{2,3},{3,2},{4,5},{5,4},{6,7},{7,6},{8,9},{9,8},{10,11... | collective-permute-start | bytes 5111816 | tf_op jit(solution)/shard_map/ppermute | solution.py:66
  354.5 39.6 %copy-start.40 = (bf16[128,4096]{1,0:T(8,128)(2,1)S(1)}, bf16[128,4096]{1,0:T(8,128)(2,1)}, u32[]{:S(2)}) copy-start(bf16[128,4096]{1,0:T(8,128)(2,1)} %copy-done.39) | copy-start | bytes 3145732
  354.5 39.6 %copy-start.42 = (bf16[128,4096]{1,0:T(8,128)(2,1)S(1)}, bf16[128,4096]{1,0:T(8,128)(2,1)}, u32[]{:S(2)}) copy-start(bf16[128,4096]{1,0:T(8,128)(2,1)} %copy-done.41) | copy-start | bytes 3145732
  354.5 39.5 %copy-start.61 = (bf16[208,512]{1,0:T(8,128)(2,1)S(1)}, bf16[208,512]{1,0:T(8,128)(2,1)}, u32[]{:S(2)}) copy-start(bf16[208,512]{1,0:T(8,128)(2,1)} %reshape_squeeze.48) | copy-start | bytes 638980
  354.6 21.4 %collective-permute-start.23 = (bf16[104,4096]{1,0:T(8,128)(2,1)S(1)}, bf16[104,4096]{1,0:T(8,128)(2,1)S(1)}, u32[]{:S(2)}, u32[]{:S(2)}) collective-permute-start(bf16[104,4096]{1,0:T(8,128)(2,1)S(1)} %slice.380), channel_id=1, source_target_pairs={{0,2},{2,0},{1,3},{3,1},{4,6},{6,4},{5,7},{7,5},{8,10},{10,8},{9,1... | collective-permute-start | bytes 2555912 | tf_op jit(solution)/shard_map/ppermute | solution.py:67
  377.9 20.6 %collective-permute-start.24 = (bf16[104,4096]{1,0:T(8,128)(2,1)}, bf16[104,4096]{1,0:T(8,128)(2,1)}, u32[]{:S(2)}, u32[]{:S(2)}) collective-permute-start(bf16[104,4096]{1,0:T(8,128)(2,1)} %pad_maximum_fusion.18), channel_id=1, source_target_pairs={{0,1},{1,0},{2,3},{3,2},{4,5},{5,4},{6,7},{7,6},{8,9},{9,8},{10,11... | collective-permute-start | bytes 2555912 | tf_op jit(solution)/shard_map/ppermute | solution.py:66
  378.8 29.1 %collective-permute-start.33 = (bf16[128,1024]{1,0:T(8,128)(2,1)}, bf16[128,1024]{1,0:T(8,128)(2,1)}, u32[]{:S(2)}, u32[]{:S(2)}) collective-permute-start(bf16[128,1024]{1,0:T(8,128)(2,1)} %get-tuple-element.40), channel_id=1, source_target_pairs={{0,4},{4,8},{8,12},{12,0},{1,5},{5,9},{9,13},{13,1},{2,6},{6,10},{... | collective-permute-start | bytes 786440 | tf_op jit(solution)/shard_map/ppermute | solution.py:70
  380.7 46.4 %collective-permute-start.35 = (bf16[128,1024]{1,0:T(8,128)(2,1)}, bf16[128,1024]{1,0:T(8,128)(2,1)}, u32[]{:S(2)}, u32[]{:S(2)}) collective-permute-start(bf16[128,1024]{1,0:T(8,128)(2,1)} %get-tuple-element.41), channel_id=1, source_target_pairs={{0,12},{4,0},{8,4},{12,8},{1,13},{5,1},{9,5},{13,9},{2,14},{6,2},{... | collective-permute-start | bytes 786440 | tf_op jit(solution)/shard_map/ppermute | solution.py:70
  403.4 59.0 %copy-start.62 = (bf16[208,1024]{1,0:T(8,128)(2,1)S(1)}, bf16[208,1024]{1,0:T(8,128)(2,1)}, u32[]{:S(2)}) copy-start(bf16[208,1024]{1,0:T(8,128)(2,1)} %fusion.47) | copy-start | bytes 1277956
  403.4 59.0 %copy-start.63 = (bf16[208,1024]{1,0:T(8,128)(2,1)S(1)}, bf16[208,1024]{1,0:T(8,128)(2,1)}, u32[]{:S(2)}) copy-start(bf16[208,1024]{1,0:T(8,128)(2,1)} %fusion.48) | copy-start | bytes 1277956
  404.8 58.6 %copy-start.26 = (f32[256,1024]{1,0:T(8,128)S(1)}, f32[256,1024]{1,0:T(8,128)}, u32[]{:S(2)}) copy-start(f32[256,1024]{1,0:T(8,128)} %get-tuple-element.95) | copy-start | bytes 3145732
  404.8 20.9 %collective-permute-start.25 = (bf16[104,4096]{1,0:T(8,128)(2,1)S(1)}, bf16[104,4096]{1,0:T(8,128)(2,1)S(1)}, u32[]{:S(2)}, u32[]{:S(2)}) collective-permute-start(bf16[104,4096]{1,0:T(8,128)(2,1)S(1)} %slice.387), channel_id=1, source_target_pairs={{0,2},{2,0},{1,3},{3,1},{4,6},{6,4},{5,7},{7,5},{8,10},{10,8},{9,1... | collective-permute-start | bytes 2555912 | tf_op jit(solution)/shard_map/ppermute | solution.py:67
  407.9 57.5 %collective-permute-start.30 = (bf16[128,4096]{1,0:T(8,128)(2,1)S(1)}, bf16[128,4096]{1,0:T(8,128)(2,1)S(1)}, u32[]{:S(2)}, u32[]{:S(2)}) collective-permute-start(bf16[128,4096]{1,0:T(8,128)(2,1)S(1)} %copy-done.52), channel_id=1, source_target_pairs={{0,4},{4,8},{8,12},{1,5},{5,9},{9,13},{2,6},{6,10},{10,14},{3,7},{... | collective-permute-start | bytes 3145736 | tf_op jit(solution)/shard_map/ppermute | solution.py:73
  425.7 39.8 %collective-permute-start.32 = (bf16[128,4096]{1,0:T(8,128)(2,1)S(1)}, bf16[128,4096]{1,0:T(8,128)(2,1)S(1)}, u32[]{:S(2)}, u32[]{:S(2)}) collective-permute-start(bf16[128,4096]{1,0:T(8,128)(2,1)S(1)} %copy-done.53), channel_id=1, source_target_pairs={{4,0},{8,4},{12,8},{5,1},{9,5},{13,9},{6,2},{10,6},{14,10},{7,3},{... | collective-permute-start | bytes 3145736 | tf_op jit(solution)/shard_map/ppermute | solution.py:76
  427.1 35.4 %collective-permute-start.34 = (bf16[128,1024]{1,0:T(8,128)(2,1)S(1)}, bf16[128,1024]{1,0:T(8,128)(2,1)S(1)}, u32[]{:S(2)}, u32[]{:S(2)}) collective-permute-start(bf16[128,1024]{1,0:T(8,128)(2,1)S(1)} %copy-done.71), channel_id=1, source_target_pairs={{0,8},{4,12},{8,0},{12,4},{1,9},{5,13},{9,1},{13,5},{2,10},{6,14},... | collective-permute-start | bytes 786440 | tf_op jit(solution)/shard_map/ppermute | solution.py:70
  462.4 8.0 %collective-permute-start.26 = (bf16[104,4096]{1,0:T(8,128)(2,1)S(1)}, bf16[104,4096]{1,0:T(8,128)(2,1)S(1)}, u32[]{:S(2)}, u32[]{:S(2)}) collective-permute-start(bf16[104,4096]{1,0:T(8,128)(2,1)S(1)} %pad_maximum_fusion.19), channel_id=1, source_target_pairs={{0,1},{1,0},{2,3},{3,2},{4,5},{5,4},{6,7},{7,6},{8,9},{9,8},{10,11... | collective-permute-start | bytes 2555912 | tf_op jit(solution)/shard_map/ppermute | solution.py:66
  502.7 12.3 %collective-permute-start.27 = (bf16[104,2048]{1,0:T(8,128)(2,1)S(1)}, bf16[104,2048]{1,0:T(8,128)(2,1)S(1)}, u32[]{:S(2)}, u32[]{:S(2)}) collective-permute-start(bf16[104,2048]{1,0:T(8,128)(2,1)S(1)} %slice.394), channel_id=1, source_target_pairs={{0,2},{2,0},{1,3},{3,1},{4,6},{6,4},{5,7},{7,5},{8,10},{10,8},{9,1... | collective-permute-start | bytes 1277960 | tf_op jit(solution)/shard_map/ppermute | solution.py:67
  515.1 9.9 %collective-permute-start.28 = (bf16[104,2048]{1,0:T(8,128)(2,1)S(1)}, bf16[104,2048]{1,0:T(8,128)(2,1)S(1)}, u32[]{:S(2)}, u32[]{:S(2)}) collective-permute-start(bf16[104,2048]{1,0:T(8,128)(2,1)S(1)} %pad_maximum_fusion.22), channel_id=1, source_target_pairs={{0,1},{1,0},{2,3},{3,2},{4,5},{5,4},{6,7},{7,6},{8,9},{9,8},{10,11... | collective-permute-start | bytes 1277960 | tf_op jit(solution)/shard_map/ppermute | solution.py:66
  (65 other events, 656.8 us)
Sparse Core Ops, SparseCore 0:
  19.7 179.9 all-gather.1

commit v4 on v3

v4 whole, which is shorter than its diff:
```python
import jax
import jax.numpy as jnp
from jax import lax
from jax.sharding import Mesh, PartitionSpec as P

adapter_scale = 0.25
bf16 = jnp.bfloat16
f32 = jnp.float32
CHAIN = 4
ORDER = ((3, 2, 1, 0), (3, 2, 0, 1), (0, 1, 3, 2), (0, 1, 2, 3))
RANK = tuple(tuple(row.index(k) for k in range(CHAIN)) for row in ORDER)


def dot(a, b, dims):
    return lax.dot_general(a, b, (dims, ((), ())), preferred_element_type=f32)


def tie(value, *after):
    odd = False
    for v in after:
        first = v[(0,) * v.ndim]
        odd = odd | (first != first)
    return jnp.where(odd, jnp.zeros_like(value), value)


def shards(
    tokens,
    cotangent,
    frozen_key_matrix,
    adapter_down_weight,
    adapter_up_weight,
    token_adapter_index,
    adapter_storage_index,
):
    groups = lax.axis_size("groups")
    depth = lax.axis_size("chain")
    sides = lax.axis_size("side")
    plane = 2 * sides
    devices = depth * plane
    tok_count = tokens.shape[0]
    locals_, width, rank = adapter_down_weight.shape
    features = cotangent.shape[1]
    entries = adapter_storage_index.shape[0]
    capacity = max(2, 5 * tok_count // (3 * locals_ * devices))
    block = locals_ * rank
    half = width // 2
    used = depth // 2 * locals_ * capacity
    rows = -(-used // 8) * 8
    across = ("side", "core")
    z = lax.axis_index("chain")
    side = lax.axis_index("side")
    q = 2 * side + lax.axis_index("core")
    group = lax.axis_index("groups")
    edge = (z == 0) | (z == depth - 1)
    order = lax.dynamic_index_in_dim(jnp.array(ORDER, jnp.int32), z, 0, False)
    place = lax.dynamic_index_in_dim(jnp.array(RANK, jnp.int32), z, 0, False)

    def turn(values, k):
        return lax.ppermute(values, "chain", [(i, (i + k) % depth) for i in range(depth)])

    def up(values):
        return lax.ppermute(values, "chain", [(i, i + 1) for i in range(depth - 1)])

    def down(values):
        return lax.ppermute(values, "chain", [(i + 1, i) for i in range(depth - 1)])

    down_rows = jnp.transpose(adapter_down_weight, (0, 2, 1)).reshape(block, width)
    up_rows = adapter_up_weight.reshape(block, features)
    share = frozen_key_matrix.shape[0] // groups
    piece = lax.dynamic_slice_in_dim(frozen_key_matrix, group * share, share, 0)
    flat_ids = token_adapter_index[:, 0]
    onehot = (flat_ids[:, None] == jnp.arange(entries, dtype=jnp.int32)[None, :]).astype(jnp.int32)
    within = jnp.sum(jnp.cumsum(onehot, axis=0) * onehot, axis=1) - 1
    position = jnp.sum(onehot * adapter_storage_index[None, :], axis=1)
    home, local = position // locals_, position % locals_
    far = home // plane
    chunk = jnp.sum(
        jnp.where(far[:, None] == jnp.arange(depth, dtype=jnp.int32)[None, :], place[None, :], 0),
        axis=1,
    )
    slots = (home % plane) * rows + (chunk % 2 * locals_ + local) * capacity + within
    numbers = jnp.arange(plane * rows, dtype=jnp.int32)[:, None]
    spreads = [
        ((numbers == slots[None, :]) & (chunk // 2 == p)[None, :]).astype(bf16)
        for p in range(2)
    ]

    def exchange(values):
        return lax.all_to_all(values, across, split_axis=0, concat_axis=0, tiled=True)

    def spread_out(p, values):
        return dot(spreads[p], values, ((1,), (0,))).astype(bf16)

    row_adapter = (jnp.arange(plane * rows) % rows) // capacity
    col_adapter = jnp.arange(2 * block) // rank
    mask = row_adapter[:, None] == col_adapter[None, :]

    def masked(values):
        return jnp.where(mask, values, 0.0).astype(bf16)

    def grad(hid, values, *more):
        out = adapter_scale * dot(hid, values, ((0,), (0,)))
        for m in more:
            out = out + m.astype(f32)
        return out

    def near(u1, d1):
        return jnp.where((z == 0) | (z == 2), d1, u1)

    def middle(u1, d1, e2):
        return jnp.where(edge, e2, jnp.where(z == 1, d1, u1))

    ups = lax.all_gather(up_rows, "chain", axis=0, tiled=False)
    up_all = jnp.concatenate(
        [lax.dynamic_index_in_dim(ups, order[j], 0, False) for j in range(depth)], axis=0
    )
    piece = tie(piece, ups)
    whole = lax.all_gather(piece, ("chain", "side", "core", "groups"), axis=0, tiled=True)

    a = [down_rows[:, :half], down_rows[:, half:]]
    one = [(up(v), down(v)) for v in a]
    cots = exchange(jnp.concatenate([spread_out(p, cotangent) for p in range(2)], 1))
    cots = [cots[:, :features], cots[:, features:]]
    x0 = exchange(spread_out(0, tokens))
    x1 = exchange(tie(spread_out(1, tokens), x0))

    def up_pair(p):
        return up_all[p * 2 * block : (p + 1) * 2 * block]

    pairs = [masked(dot(cots[p], up_pair(p), ((1,), (1,)))) for p in range(2)]
    hid = [pairs[j // 2][:, j % 2 * block : (j % 2 + 1) * block] for j in range(depth)]
    second = jnp.where(edge, hid[1], hid[0])

    def lora(p, weights):
        return (adapter_scale * dot(pairs[p], weights, ((1,), (0,)))).astype(bf16)

    def cols(values, h):
        return values[:, h * half : (h + 1) * half]

    two = [None, None]
    for h in range(2):
        v = grad(hid[0], cols(x0, h)).astype(bf16)
        two[h] = (
            up(jnp.where(z == 0, v, one[h][0])),
            down(jnp.where(z == depth - 1, v, one[h][1])),
        )
    near_a = jnp.concatenate([near(*one[h]) for h in range(2)], 1)
    back_1 = exchange(tie(lora(1, jnp.concatenate([near_a, down_rows], 0)), x1))

    three, e2 = [None, None], [None, None]
    for h in range(2):
        uu, dd = two[h]
        e2[h] = jnp.where(z >= 2, uu, dd)
        r1 = jnp.where(edge, jnp.zeros_like(uu), jnp.where(z == 1, uu, dd))
        v = grad(second, cols(x0, h), r1).astype(bf16)
        send_up, send_down = jnp.where(z <= 1, v, e2[h]), jnp.where(z >= 2, v, e2[h])
        if h == 1:
            send_up, send_down = tie(send_up, x1), tie(send_down, x1)
        three[h] = up(send_up), down(send_down)

    frozen_out = dot(tokens, whole, ((1,), (0,)))
    frozen_grad = dot(cotangent, whole, ((1,), (1,)))
    four, far_a, back_0 = [None, None], [None, None], [None, None]
    for h in range(2):
        uu, dd = three[h]
        e3 = jnp.where(z == depth - 1, uu, dd)
        zero = jnp.zeros_like(uu)
        ru, rd = jnp.where(edge, zero, uu), jnp.where(edge, zero, dd)
        far_a[h] = jnp.concatenate([jnp.where(edge, e3, e2[h]), middle(*one[h], e2[h])], 0)
        y0, y1 = cols(x0, h), cols(x1, h)
        third_up = grad(hid[2], y1, ru)
        third_down = grad(hid[2], y1, rd)
        inner = grad(hid[1], y0)
        third_up = jnp.where(z == 1, inner + ru.astype(f32), third_up)
        third_down = jnp.where(z == 2, inner + rd.astype(f32), third_down)
        third_up, third_down = third_up.astype(bf16), third_down.astype(bf16)
        done = (back_1,) if h == 0 else (frozen_out, frozen_grad)
        third_up, third_down = tie(third_up, *done), tie(third_down, *done)
        four[h] = up(third_up), down(third_down)
        back_0[h] = exchange(tie(lora(0, far_a[h]), back_1 if h == 0 else back_0[0]))
    far_a = jnp.concatenate(far_a, 1)
    back_0 = jnp.concatenate(back_0, 1)

    down_all = jnp.concatenate([far_a, near_a, down_rows], 0)

    shrunk = [
        masked(dot(v, down_all[p * 2 * block : (p + 1) * 2 * block], ((1,), (1,))))
        for p, v in enumerate((x0, x1))
    ]
    up_parts = jnp.concatenate(
        [adapter_scale * dot(shrunk[p], cots[p], ((0,), (0,))) for p in range(2)], 0
    )
    up_own = up_parts[(depth - 1) * block :]
    up_parts = up_parts.astype(bf16).reshape(depth, block, features)
    up_sent = [
        turn(lax.dynamic_index_in_dim(up_parts, place[(z + k) % depth], 0, False), k)
        for k in range(1, depth)
    ]
    expanded = jnp.concatenate(
        [
            (
                adapter_scale
                * dot(shrunk[p], up_pair(p), ((1,), (0,)))
            ).astype(bf16)
            for p in range(2)
        ],
        1,
    )
    expanded = exchange(tie(expanded, back_0))

    key_output = (
        frozen_out
        + dot(spreads[0], expanded[:, :features], ((0,), (0,)))
        + dot(spreads[1], expanded[:, features:], ((0,), (0,)))
    ).astype(bf16)
    token_grad = (
        frozen_grad
        + dot(spreads[1], back_1, ((0,), (0,)))
        + dot(spreads[0], back_0, ((0,), (0,)))
    ).astype(bf16)
    down_grad = grad(hid[3], x1, *(jnp.concatenate(v, 1) for v in zip(*four)))
    up_grad = up_own + sum(v.astype(f32) for v in up_sent)
    down_grad = jnp.transpose(down_grad.reshape(locals_, rank, width), (0, 2, 1))
    up_grad = up_grad.reshape(locals_, rank, features)
    return key_output, token_grad, down_grad, up_grad


def solution(mesh):
    groups, wide = mesh.devices.shape
    fine = Mesh(
        mesh.devices.reshape(groups, CHAIN, wide // CHAIN // 2, 2),
        ("groups", "chain", "side", "core"),
    )
    every = ("groups", "chain", "side", "core")
    return jax.shard_map(
        shards,
        mesh=fine,
        in_specs=(
            P(every, None),
            P(every, None),
            P(every[1:], None),
            P(every, None, None),
            P(every, None, None),
            P(every, None),
            P("groups"),
        ),
        out_specs=(
            P(every, None),
            P(every, None),
            P(every, None, None),
            P(every, None, None),
        ),
        check_vma=False,
    )
```

time: 539 us -> 459 us (0.85)
  waiting for transfers between devices: 241 us -> 176 us
  local copies, waits for them, and re-layouts: 40.6 us -> 24.1 us
  other arithmetic: 36.7 us -> 21.2 us
  matrix products: 95.5 us -> 109 us
  between operations: 23.9 us -> 36.9 us
  starting transfers between devices: 96.7 us -> 86.2 us
    ppermute x14 -> x0, waiting for transfers between devices: 121 us -> none  [the longest x7 118 us: swap(): lax.ppermute(values, 'side', [(i, i ^ bit // 2) for i in range(sides)])]
    all_to_all x0 -> x7, waiting for transfers between devices: none -> 62.8 us  [exchange(): lax.all_to_all(values, across, split_axis=0, concat_axis=0, tiled=True)]
    ppermute x8, waiting for transfers between devices: 65.5 us -> 13.3 us  [up(): return lax.ppermute(values, 'chain', [(i, i + 1) for i in range(depth - 1)])]
    ppermute x8, waiting for transfers between devices: 21.8 us -> 58.5 us  [down(): return lax.ppermute(values, 'chain', [(i + 1, i) for i in range(depth - 1)])]
    all_gather x0 -> x1, waiting for transfers between devices: none -> 32.3 us  [shards(): ups = lax.all_gather(up_rows, 'chain', axis=0, tiled=False)]
    all_to_all x0 -> x7, starting transfers between devices: none -> 30.3 us  [exchange(): lax.all_to_all(values, across, split_axis=0, concat_axis=0, tiled=True)]
    ppermute x6 -> x3, waiting for transfers between devices: 33 us -> 8.05 us  [turn(): lax.ppermute(values, 'chain', [(i, (i + k) % depth) for i in range(depth)])]
    concatenate x15 -> x1, other arithmetic: 21.9 us -> 1 us  [shards(): jnp.concatenate([spread_out(p, cotangent) for p in range(2)], 1)]
  transfers between devices with their start and end apart: 37 -> 28, of which waited for: 18 -> 12; matrix products, arithmetic and copies ran while one was open for 27% -> 26% of each run, Pallas kernels for 0% -> 0%
where the time goes in v4:
time: 459 us; the launch traced here: 453 us
  waiting for transfers between devices  176 us (38%)
  matrix products  109 us (24%)
  starting transfers between devices  86.2 us (19%)
  between operations  36.9 us (8%)
  local copies, waits for them, and re-layouts  24.1 us (5%)
  other arithmetic  21.2 us (5%)
    dot_general x30, matrix products, dot(): return lax.dot_general(a, b, (dims, ((), ())), preferred_element_type=f32)  109 us
    all_to_all x7, waiting for transfers between devices, exchange(): lax.all_to_all(values, across, split_axis=0, concat_axis=0, tiled=True)  62.8 us
    ppermute x8, waiting for transfers between devices, down(): return lax.ppermute(values, 'chain', [(i + 1, i) for i in range(depth - 1)])  58.5 us
    ppermute x8, starting transfers between devices, up(): return lax.ppermute(values, 'chain', [(i, i + 1) for i in range(depth - 1)])  40.1 us
    all_gather x1, waiting for transfers between devices, shards(): ups = lax.all_gather(up_rows, 'chain', axis=0, tiled=False)  32.3 us
    all_to_all x7, starting transfers between devices, exchange(): lax.all_to_all(values, across, split_axis=0, concat_axis=0, tiled=True)  30.3 us
    select_n x5, other arithmetic, tie(): return jnp.where(odd, jnp.zeros_like(value), value)  14.2 us
    ppermute x8, waiting for transfers between devices, up(): return lax.ppermute(values, 'chain', [(i, i + 1) for i in range(depth - 1)])  13.3 us
  transfers between devices with their start and end apart: 28, of which 12 were waited for; matrix products, arithmetic and copies ran while one was open for 26% of the time, Pallas kernels for 0%

profile of v4, /device:TPU:0, one launch (start us, length us, event | category | flops | bytes accessed | tf_op | source)
XLA Modules:
  0.0 453.3 jit_solution(8130838733958052034)
XLA Ops:
  8.0 32.3 %all-gather.3.cloned.1.call-done = bf16[4,128,1024]{2,1,0:T(8,128)(2,1)} async-done(((bf16[1,128,1024]{2,1,0:T(8,128)(2,1)}), bf16[4,128,1024]{2,1,0:T(8,128)(2,1)}) %all-gather.3.cloned.1.call-update) | async-done | bytes 1048592 | tf_op jit(solution)/shard_map/all_gather | solution.py:113
  49.4 3.5 all-to-all-start.2
  53.0 5.3 %convolution_convert_fusion.1 = bf16[224,8192]{1,0:T(8,128)(2,1)} fusion(bf16[256,8192]{1,0:T(8,128)(2,1)} %param.9, s32[256]{0:T(256)S(1)} %fusion.110, pred[256]{0:T(512)(128)(4,1)S(1)} %broadcast_compare_fusion.1), kind=kOutput, calls=%fused_computation.7 | convolution fusion | flops 941473792 | bytes 7865600 | tf_op jit(solution)/shard_map/dot_general | solution.py:15
  58.3 11.1 %all-to-all-done.2 = bf16[4,56,2048]{2,1,0:T(8,128)(2,1)S(1)} async-done(((bf16[4,56,2048]{2,1,0:T(8,128)(2,1)}), bf16[4,56,2048]{2,1,0:T(8,128)(2,1)S(1)}, u32[]{:S(2)}, u32[]{:S(2)}) %all-to-all-start.2) | async-done | bytes 917536 | tf_op jit(solution)/shard_map/all_to_all | solution.py:89
  69.4 5.0 %all-to-all-start = ((bf16[4,56,8192]{2,1,0:T(8,128)(2,1)}), bf16[4,56,8192]{2,1,0:T(8,128)(2,1)}, u32[]{:S(2)}, u32[]{:S(2)}) async-start(bf16[4,56,8192]{2,1,0:T(8,128)(2,1)} %bitcast.93), calls=%async_computation | async-start | bytes 7340032 | tf_op jit(solution)/shard_map/all_to_all | solution.py:89
  75.9 3.4 collective-permute-start.1
  80.7 5.5 %collective-permute-start.3 = (bf16[128,4096]{1,0:T(8,128)(2,1)}, bf16[128,4096]{1,0:T(8,128)(2,1)}, u32[]{:S(2)}, u32[]{:S(2)}) collective-permute-start(bf16[128,4096]{1,0:T(8,128)(2,1)} %get-tuple-element.41), channel_id=1, source_target_pairs={{0,4},{4,8},{8,12},{1,5},{5,9},{9,13},{2,6},{6,10},{10,14},{3,7},{... | collective-permute-start | bytes 3145736 | tf_op jit(solution)/shard_map/ppermute | solution.py:62
  96.0 2.1 dynamic-slice_bitcast_fusion.4
  99.9 24.7 %all-to-all-done = bf16[4,56,8192]{2,1,0:T(8,128)(2,1)} async-done(((bf16[4,56,8192]{2,1,0:T(8,128)(2,1)}), bf16[4,56,8192]{2,1,0:T(8,128)(2,1)}, u32[]{:S(2)}, u32[]{:S(2)}) %all-to-all-start) | async-done | bytes 3670048 | tf_op jit(solution)/shard_map/all_to_all | solution.py:89
  127.1 5.1 %fusion.2 = bf16[224,8192]{1,0:T(8,128)(2,1)} fusion(bf16[256,8192]{1,0:T(8,128)(2,1)} %param.9, pred[]{:T(512)} %bitcast.9, s32[256]{0:T(256)S(1)} %fusion.110, pred[256]{0:T(512)(128)(4,1)S(1)} %get-tuple-element.26), kind=kOutput, calls=%fused_computation.9 | convolution fusion | flops 943308800 | bytes 7865601 | tf_op jit(solution)/shard_map/dot_general | solution.py:15
  132.2 4.8 %all-to-all-start.1 = ((bf16[4,56,8192]{2,1,0:T(8,128)(2,1)}), bf16[4,56,8192]{2,1,0:T(8,128)(2,1)}, u32[]{:S(2)}, u32[]{:S(2)}) async-start(bf16[4,56,8192]{2,1,0:T(8,128)(2,1)} %bitcast.98), calls=%async_computation.1 | async-start | bytes 7340032 | tf_op jit(solution)/shard_map/all_to_all | solution.py:89
  137.1 4.1 broadcast_select_fusion.7
  142.5 5.5 %collective-permute-start.4 = (bf16[128,4096]{1,0:T(8,128)(2,1)}, bf16[128,4096]{1,0:T(8,128)(2,1)}, u32[]{:S(2)}, u32[]{:S(2)}) collective-permute-start(bf16[128,4096]{1,0:T(8,128)(2,1)} %get-tuple-element.49), channel_id=1, source_target_pairs={{0,4},{4,8},{8,12},{1,5},{5,9},{9,13},{2,6},{6,10},{10,14},{3,7},{... | collective-permute-start | bytes 3145736 | tf_op jit(solution)/shard_map/ppermute | solution.py:62
  150.1 13.3 %collective-permute-done.3 = bf16[128,4096]{1,0:T(8,128)(2,1)} collective-permute-done((bf16[128,4096]{1,0:T(8,128)(2,1)}, bf16[128,4096]{1,0:T(8,128)(2,1)}, u32[]{:S(2)}, u32[]{:S(2)}) %collective-permute-start.3) | collective-permute-done | bytes 1048608 | tf_op jit(solution)/shard_map/ppermute | solution.py:62
  163.4 13.3 %collective-permute-done.2 = bf16[128,4096]{1,0:T(8,128)(2,1)} collective-permute-done((bf16[128,4096]{1,0:T(8,128)(2,1)}, bf16[128,4096]{1,0:T(8,128)(2,1)}, u32[]{:S(2)}, u32[]{:S(2)}) %collective-permute-start.2) | collective-permute-done | bytes 1048608 | tf_op jit(solution)/shard_map/ppermute | solution.py:65
  176.7 3.6 broadcast_select_fusion.6
  181.6 5.5 %collective-permute-start.8 = (bf16[128,4096]{1,0:T(8,128)(2,1)}, bf16[128,4096]{1,0:T(8,128)(2,1)}, u32[]{:S(2)}, u32[]{:S(2)}) collective-permute-start(bf16[128,4096]{1,0:T(8,128)(2,1)} %get-tuple-element.51), channel_id=1, source_target_pairs={{0,4},{4,8},{8,12},{1,5},{5,9},{9,13},{2,6},{6,10},{10,14},{3,7},{... | collective-permute-start | bytes 3145736 | tf_op jit(solution)/shard_map/ppermute | solution.py:62
  189.1 24.7 %collective-permute-done.5 = bf16[128,4096]{1,0:T(8,128)(2,1)} collective-permute-done((bf16[128,4096]{1,0:T(8,128)(2,1)}, bf16[128,4096]{1,0:T(8,128)(2,1)}, u32[]{:S(2)}, u32[]{:S(2)}) %collective-permute-start.5) | collective-permute-done | bytes 1048608 | tf_op jit(solution)/shard_map/ppermute | solution.py:65
  213.8 3.8 broadcast_select_fusion.1
  222.8 13.3 %collective-permute-done.9 = bf16[128,4096]{1,0:T(8,128)(2,1)} collective-permute-done((bf16[128,4096]{1,0:T(8,128)(2,1)}, bf16[128,4096]{1,0:T(8,128)(2,1)}, u32[]{:S(2)}, u32[]{:S(2)}) %collective-permute-start.9) | collective-permute-done | bytes 1048608 | tf_op jit(solution)/shard_map/ppermute | solution.py:65
  236.1 3.9 select_select_fusion.2
  242.0 4.4 collective-permute-start.10
  247.9 3.3 convolution_multiply_fusion.4
  251.2 9.5 %convolution_bitcast_fusion.1 = f32[256,1024]{0,1:T(8,128)S(1)} fusion(bf16[8192,1024]{1,0:T(8,128)(2,1)} %all-gather.5.cloned.1.call-done, bf16[256,8192]{1,0:T(8,128)(2,1)} %param.9), kind=kOutput, calls=%fused_computation.77 | convolution fusion | flops 4294967296 | bytes 22020096 | tf_op jit(solution)/shard_map/dot_general | solution.py:15
  263.1 8.3 %convolution_bitcast_fusion = f32[256,8192]{0,1:T(8,128)S(1)} fusion(bf16[8192,1024]{1,0:T(8,128)(2,1)} %all-gather.5.cloned.1.call-done, bf16[256,1024]{1,0:T(8,128)(2,1)S(1)} %copy-done), kind=kOutput, calls=%fused_computation.2 | convolution fusion | flops 4294967296 | bytes 25690112 | tf_op jit(solution)/shard_map/dot_general | solution.py:15
  273.4 5.4 %fusion.58 = (bf16[128,4096]{1,0:T(8,128)(2,1)}, bf16[128,4096]{1,0:T(8,128)(2,1)}, bf16[128,4096]{1,0:T(8,128)(2,1)}, bf16[128,4096]{1,0:T(8,128)(2,1)S(1)}, bf16[128,4096]{1,0:T(8,128)(2,1)}) fusion(f32[128,4096]{1,0:T(8,128)S(1)} %copy-done.3, f32[128,4096]{1,0:T(8,128)S(1)} %convolution_multiply_fusion.5, bf16[128,4096]{1,0:T(8,128)(2,1)} %collective-permute-done.11, ...), kind=kLoop, calls=%fused_computation.94 | loop fusion | flops 9961472 | bytes 14680070 | tf_op jit(solution)/shard_map/jit(_where)/select_n | solution.py:23
  278.9 9.4 %fusion.3 = bf16[224,8192]{1,0:T(8,128)(2,1)} fusion(bf16[224,256]{1,0:T(8,128)(2,1)S(1)} %copy-done.36, pred[]{:T(512)} %bitcast.12, bf16[128,8192]{1,0:T(8,128)(2,1)S(1)} %bitcast.103, bf16[128,4096]{1,0:T(8,128)(2,1)S(1)} %get-tuple-element.42, bf16[128,4096]{1,0:T(8,128)(2,1)S(1)} %copy-done.20), kind=kOutput, calls=%fused_computation.10 | convolution fusion | flops 957612032 | bytes 7979009 | tf_op jit(solution)/shard_map/dot_general | solution.py:15
  288.3 5.0 %all-to-all-start.3 = ((bf16[4,56,8192]{2,1,0:T(8,128)(2,1)}), bf16[4,56,8192]{2,1,0:T(8,128)(2,1)}, u32[]{:S(2)}, u32[]{:S(2)}) async-start(bf16[4,56,8192]{2,1,0:T(8,128)(2,1)} %bitcast.97), calls=%async_computation.3 | async-start | bytes 7340032 | tf_op jit(solution)/shard_map/all_to_all | solution.py:89
  299.7 5.7 %collective-permute-start.6 = (bf16[128,4096]{1,0:T(8,128)(2,1)}, bf16[128,4096]{1,0:T(8,128)(2,1)}, u32[]{:S(2)}, u32[]{:S(2)}) collective-permute-start(bf16[128,4096]{1,0:T(8,128)(2,1)} %get-tuple-element.47), channel_id=1, source_target_pairs={{0,4},{4,8},{8,12},{1,5},{5,9},{9,13},{2,6},{6,10},{10,14},{3,7},{... | collective-permute-start | bytes 3145736 | tf_op jit(solution)/shard_map/ppermute | solution.py:62
  308.9 3.3 convolution_multiply_fusion.6
  313.5 6.2 %collective-permute-start.13 = (bf16[128,4096]{1,0:T(8,128)(2,1)}, bf16[128,4096]{1,0:T(8,128)(2,1)}, u32[]{:S(2)}, u32[]{:S(2)}) collective-permute-start(bf16[128,4096]{1,0:T(8,128)(2,1)} %get-tuple-element.33), channel_id=1, source_target_pairs={{0,4},{4,8},{8,12},{1,5},{5,9},{9,13},{2,6},{6,10},{10,14},{3,7},{... | collective-permute-start | bytes 3145736 | tf_op jit(solution)/shard_map/ppermute | solution.py:62
  319.7 4.3 fusion.57
  324.0 11.9 %all-to-all-done.3 = bf16[4,56,8192]{2,1,0:T(8,128)(2,1)} async-done(((bf16[4,56,8192]{2,1,0:T(8,128)(2,1)}), bf16[4,56,8192]{2,1,0:T(8,128)(2,1)}, u32[]{:S(2)}, u32[]{:S(2)}) %all-to-all-start.3) | async-done | bytes 3670048 | tf_op jit(solution)/shard_map/all_to_all | solution.py:89
  338.4 4.7 %fusion.59 = (bf16[128,4096]{1,0:T(8,128)(2,1)}, bf16[128,4096]{1,0:T(8,128)(2,1)}, bf16[128,4096]{1,0:T(8,128)(2,1)S(1)}) fusion(f32[128,4096]{1,0:T(8,128)} %convolution_multiply_fusion.6, f32[128,4096]{1,0:T(8,128)S(1)} %convolution_multiply_fusion.7, bf16[128,4096]{1,0:T(8,128)(2,1)} %collective-permute-done.7, pred[]{:T(512)S(6)} %eq.162, pred[]{:T(512)} %bitcast.24, ...), kind=kLoop, calls=%fused_computation.95 | loop fusion | flops 8388608 | bytes 10485765 | tf_op jit(solution)/shard_map/jit(_where)/select_n | solution.py:23
  345.0 3.7 all-to-all-start.4
  351.4 4.7 %fusion.53 = bf16[224,256]{1,0:T(8,128)(2,1)S(1)} fusion(bf16[224,8192]{1,0:T(8,128)(2,1)} %bitcast.8, bf16[128,4096]{1,0:T(8,128)(2,1)} %get-tuple-element.43, bf16[128,4096]{1,0:T(8,128)(2,1)} %get-tuple-element.34, bf16[128,4096]{1,0:T(8,128)(2,1)} %get-tuple-element.36, bf16[128,4096]{1,0:T(8,128)(2,1)} %copy-done.16, s32[256]{0:T(256)} %copy-done.40, ...), kind=kOutput, calls=%fused_computation.91 | convolution fusion | flops 956473344 | bytes 7980928 | tf_op jit(solution)/shard_map/dot_general | solution.py:15
  356.5 15.1 %all-to-all-done.4 = bf16[4,56,4096]{2,1,0:T(8,128)(2,1)S(1)} async-done(((bf16[4,56,4096]{2,1,0:T(8,128)(2,1)}), bf16[4,56,4096]{2,1,0:T(8,128)(2,1)S(1)}, u32[]{:S(2)}, u32[]{:S(2)}) %all-to-all-start.4) | async-done | bytes 1835040 | tf_op jit(solution)/shard_map/all_to_all | solution.py:89
  374.5 3.6 all-to-all-start.5
  379.8 3.0 collective-permute-start.16
  386.7 4.1 collective-permute-done.16
  392.1 4.0 collective-permute-done.18
  396.7 3.9 collective-permute-start.12
  400.6 4.7 %all-to-all-start.6 = ((bf16[4,56,4096]{2,1,0:T(8,128)(2,1)}), bf16[4,56,4096]{2,1,0:T(8,128)(2,1)}, u32[]{:S(2)}, u32[]{:S(2)}) async-start(bf16[4,56,4096]{2,1,0:T(8,128)(2,1)} %bitcast.109), calls=%async_computation.6 | async-start | bytes 3670016 | tf_op jit(solution)/shard_map/all_to_all | solution.py:89
  405.3 9.6 %convolution_add_fusion.1 = f32[256,8192]{0,1:T(8,128)} fusion(f32[256,8192]{0,1:T(8,128)} %copy-done.2, bf16[224,8192]{1,0:T(8,128)(2,1)} %bitcast.23, s32[256]{0:T(256)S(1)} %fusion.110, pred[256]{0:T(512)(128)(4,1)S(1)} %get-tuple-element.26), kind=kOutput, calls=%fused_computation.1 | convolution fusion | flops 941735936 | bytes 20448512 | tf_op jit(solution)/shard_map/dot_general | solution.py:15
  416.8 7.3 %collective-permute-done.14 = bf16[128,4096]{1,0:T(8,128)(2,1)} collective-permute-done((bf16[128,4096]{1,0:T(8,128)(2,1)}, bf16[128,4096]{1,0:T(8,128)(2,1)}, u32[]{:S(2)}, u32[]{:S(2)}) %collective-permute-start.14) | collective-permute-done | bytes 1048608 | tf_op jit(solution)/shard_map/ppermute | solution.py:65
  424.1 6.6 %convert_add_fusion = f32[128,8192]{1,0:T(8,128)} fusion(bf16[128,4096]{1,0:T(8,128)(2,1)} %collective-permute-done.13, bf16[128,4096]{1,0:T(8,128)(2,1)} %collective-permute-done.12, bf16[128,4096]{1,0:T(8,128)(2,1)} %collective-permute-done.15, bf16[128,4096]{1,0:T(8,128)(2,1)} %collective-permute-done.14, bf16[224,8192]{1,0:T(8,128)(2,1)} %bitcast.11, ...), kind=kOutput, calls=%fused_computation.36 | convolution fusion | flops 481296384 | bytes 12115968 | tf_op jit(solution)/shard_map/dot_general | solution.py:15
  432.4 7.7 %fusion = bf16[256,8192]{0,1:T(8,128)(2,1)} fusion(f32[256,8192]{0,1:T(8,128)} %convolution_add_fusion.1, bf16[224,4096]{1,0:T(8,128)(2,1)} %bitcast.37, bf16[224,4096]{1,0:T(8,128)(2,1)S(1)} %bitcast.95, s32[256]{0:T(256)S(1)} %fusion.110, pred[256]{0:T(512)(128)(4,1)S(1)} %broadcast_compare_fusion.1), kind=kOutput, calls=%fused_computation.4 | convolution fusion | flops 951173120 | bytes 16254208 | tf_op jit(solution)/shard_map/dot_general | solution.py:15
  440.1 6.3 %copy.39 = bf16[256,8192]{1,0:T(8,128)(2,1)} copy(bf16[256,8192]{0,1:T(8,128)(2,1)} %fusion) | data formatting | bytes 8388608
  (162 shorter events, 56.9 us)
Async XLA Ops:
  7.2 40.7 %copy-start = (bf16[256,1024]{1,0:T(8,128)(2,1)S(1)}, bf16[256,1024]{1,0:T(8,128)(2,1)}, u32[]{:S(2)}) copy-start(bf16[256,1024]{1,0:T(8,128)(2,1)} %param.10) | copy-start | bytes 1572868
  7.2 33.1 %all-gather.3.cloned.1.call-start = ((), (), s32[]{:S(2)}) async-start(), calls=%async_computation.7 | async-start | bytes 1310720 | tf_op jit(solution)/shard_map/all_gather | solution.py:113
  7.9 243.2 %all-gather.5.cloned.1.call-start = ((), (), s32[]{:S(2)}) async-start(), calls=%async_computation.8 | async-start | bytes 17301504 | tf_op jit(solution)/shard_map/all_gather | solution.py:118
  49.4 20.0 %all-to-all-start.2 = ((bf16[4,56,2048]{2,1,0:T(8,128)(2,1)}), bf16[4,56,2048]{2,1,0:T(8,128)(2,1)S(1)}, u32[]{:S(2)}, u32[]{:S(2)}) async-start(bf16[4,56,2048]{2,1,0:T(8,128)(2,1)} %bitcast.13), calls=%async_computation.2 | async-start | bytes 1835008 | tf_op jit(solution)/shard_map/all_to_all | solution.py:89
  69.4 279.3 %copy-start.15 = (bf16[4,56,2048]{2,1,0:T(8,128)(2,1)}, bf16[4,56,2048]{2,1,0:T(8,128)(2,1)S(1)}, u32[]{:S(2)}) copy-start(bf16[4,56,2048]{2,1,0:T(8,128)(2,1)S(1)} %all-to-all-done.2) | copy-start | bytes 2752516
  69.4 55.1 %all-to-all-start = ((bf16[4,56,8192]{2,1,0:T(8,128)(2,1)}), bf16[4,56,8192]{2,1,0:T(8,128)(2,1)}, u32[]{:S(2)}, u32[]{:S(2)}) async-start(bf16[4,56,8192]{2,1,0:T(8,128)(2,1)} %bitcast.93), calls=%async_computation | async-start | bytes 7340032 | tf_op jit(solution)/shard_map/all_to_all | solution.py:89
  75.9 61.1 %collective-permute-start.1 = (bf16[128,4096]{1,0:T(8,128)(2,1)}, bf16[128,4096]{1,0:T(8,128)(2,1)S(1)}, u32[]{:S(2)}, u32[]{:S(2)}) collective-permute-start(bf16[128,4096]{1,0:T(8,128)(2,1)} %get-tuple-element.40), channel_id=1, source_target_pairs={{0,4},{4,8},{8,12},{1,5},{5,9},{9,13},{2,6},{6,10},{10,14},{3,7},{... | collective-permute-start | bytes 3145736 | tf_op jit(solution)/shard_map/ppermute | solution.py:62
  79.4 57.7 %collective-permute-start = (bf16[128,4096]{1,0:T(8,128)(2,1)}, bf16[128,4096]{1,0:T(8,128)(2,1)S(1)}, u32[]{:S(2)}, u32[]{:S(2)}) collective-permute-start(bf16[128,4096]{1,0:T(8,128)(2,1)} %get-tuple-element.40), channel_id=1, source_target_pairs={{4,0},{8,4},{12,8},{5,1},{9,5},{13,9},{6,2},{10,6},{14,10},{7,3},{... | collective-permute-start | bytes 3145736 | tf_op jit(solution)/shard_map/ppermute | solution.py:65
  80.7 82.7 %collective-permute-start.3 = (bf16[128,4096]{1,0:T(8,128)(2,1)}, bf16[128,4096]{1,0:T(8,128)(2,1)}, u32[]{:S(2)}, u32[]{:S(2)}) collective-permute-start(bf16[128,4096]{1,0:T(8,128)(2,1)} %get-tuple-element.41), channel_id=1, source_target_pairs={{0,4},{4,8},{8,12},{1,5},{5,9},{9,13},{2,6},{6,10},{10,14},{3,7},{... | collective-permute-start | bytes 3145736 | tf_op jit(solution)/shard_map/ppermute | solution.py:62
  86.2 90.5 %collective-permute-start.2 = (bf16[128,4096]{1,0:T(8,128)(2,1)}, bf16[128,4096]{1,0:T(8,128)(2,1)}, u32[]{:S(2)}, u32[]{:S(2)}) collective-permute-start(bf16[128,4096]{1,0:T(8,128)(2,1)} %get-tuple-element.41), channel_id=1, source_target_pairs={{4,0},{8,4},{12,8},{5,1},{9,5},{13,9},{6,2},{10,6},{14,10},{7,3},{... | collective-permute-start | bytes 3145736 | tf_op jit(solution)/shard_map/ppermute | solution.py:65
  132.2 88.2 %all-to-all-start.1 = ((bf16[4,56,8192]{2,1,0:T(8,128)(2,1)}), bf16[4,56,8192]{2,1,0:T(8,128)(2,1)}, u32[]{:S(2)}, u32[]{:S(2)}) async-start(bf16[4,56,8192]{2,1,0:T(8,128)(2,1)} %bitcast.98), calls=%async_computation.1 | async-start | bytes 7340032 | tf_op jit(solution)/shard_map/all_to_all | solution.py:89
  137.0 13.0 %copy-start.5 = (bf16[128,4096]{1,0:T(8,128)(2,1)}, bf16[128,4096]{1,0:T(8,128)(2,1)S(1)}, u32[]{:S(2)}) copy-start(bf16[128,4096]{1,0:T(8,128)(2,1)S(1)} %collective-permute-done.1) | copy-start | bytes 3145732
  137.1 13.0 %copy-start.7 = (bf16[128,4096]{1,0:T(8,128)(2,1)}, bf16[128,4096]{1,0:T(8,128)(2,1)S(1)}, u32[]{:S(2)}) copy-start(bf16[128,4096]{1,0:T(8,128)(2,1)S(1)} %collective-permute-done) | copy-start | bytes 3145732
  141.2 72.6 %collective-permute-start.5 = (bf16[128,4096]{1,0:T(8,128)(2,1)}, bf16[128,4096]{1,0:T(8,128)(2,1)}, u32[]{:S(2)}, u32[]{:S(2)}) collective-permute-start(bf16[128,4096]{1,0:T(8,128)(2,1)} %get-tuple-element.48), channel_id=1, source_target_pairs={{4,0},{8,4},{12,8},{5,1},{9,5},{13,9},{6,2},{10,6},{14,10},{7,3},{... | collective-permute-start | bytes 3145736 | tf_op jit(solution)/shard_map/ppermute | solution.py:65
  142.5 71.3 %collective-permute-start.4 = (bf16[128,4096]{1,0:T(8,128)(2,1)}, bf16[128,4096]{1,0:T(8,128)(2,1)}, u32[]{:S(2)}, u32[]{:S(2)}) collective-permute-start(bf16[128,4096]{1,0:T(8,128)(2,1)} %get-tuple-element.49), channel_id=1, source_target_pairs={{0,4},{4,8},{8,12},{1,5},{5,9},{9,13},{2,6},{6,10},{10,14},{3,7},{... | collective-permute-start | bytes 3145736 | tf_op jit(solution)/shard_map/ppermute | solution.py:62
  148.0 39.1 %copy-start.26 = (bf16[224,256]{1,0:T(8,128)(2,1)S(1)}, bf16[224,256]{1,0:T(8,128)(2,1)}, u32[]{:S(2)}) copy-start(bf16[224,256]{1,0:T(8,128)(2,1)} %fusion.49) | copy-start | bytes 344068
  180.3 55.8 %collective-permute-start.9 = (bf16[128,4096]{1,0:T(8,128)(2,1)}, bf16[128,4096]{1,0:T(8,128)(2,1)}, u32[]{:S(2)}, u32[]{:S(2)}) collective-permute-start(bf16[128,4096]{1,0:T(8,128)(2,1)} %get-tuple-element.50), channel_id=1, source_target_pairs={{4,0},{8,4},{12,8},{5,1},{9,5},{13,9},{6,2},{10,6},{14,10},{7,3},{... | collective-permute-start | bytes 3145736 | tf_op jit(solution)/shard_map/ppermute | solution.py:65
  181.6 54.5 %collective-permute-start.8 = (bf16[128,4096]{1,0:T(8,128)(2,1)}, bf16[128,4096]{1,0:T(8,128)(2,1)}, u32[]{:S(2)}, u32[]{:S(2)}) collective-permute-start(bf16[128,4096]{1,0:T(8,128)(2,1)} %get-tuple-element.51), channel_id=1, source_target_pairs={{0,4},{4,8},{8,12},{1,5},{5,9},{9,13},{2,6},{6,10},{10,14},{3,7},{... | collective-permute-start | bytes 3145736 | tf_op jit(solution)/shard_map/ppermute | solution.py:62
  189.1 29.5 %copy-start.6 = (bf16[128,4096]{1,0:T(8,128)(2,1)S(1)}, bf16[128,4096]{1,0:T(8,128)(2,1)}, u32[]{:S(2)}) copy-start(bf16[128,4096]{1,0:T(8,128)(2,1)} %copy-done.5) | copy-start | bytes 3145732
  189.1 29.5 %copy-start.8 = (bf16[128,4096]{1,0:T(8,128)(2,1)S(1)}, bf16[128,4096]{1,0:T(8,128)(2,1)}, u32[]{:S(2)}) copy-start(bf16[128,4096]{1,0:T(8,128)(2,1)} %copy-done.7) | copy-start | bytes 3145732
  236.1 11.8 %copy-start.35 = (bf16[224,256]{1,0:T(8,128)(2,1)S(1)}, bf16[224,256]{1,0:T(8,128)(2,1)}, u32[]{:S(2)}) copy-start(bf16[224,256]{1,0:T(8,128)(2,1)} %fusion.48) | copy-start | bytes 344068
  242.0 31.3 %collective-permute-start.10 = (bf16[128,4096]{1,0:T(8,128)(2,1)}, bf16[128,4096]{1,0:T(8,128)(2,1)}, u32[]{:S(2)}, u32[]{:S(2)}) collective-permute-start(bf16[128,4096]{1,0:T(8,128)(2,1)} %select_select_fusion.3), channel_id=1, source_target_pairs={{0,4},{4,8},{8,12},{1,5},{5,9},{9,13},{2,6},{6,10},{10,14},{3,7},{... | collective-permute-start | bytes 3145736 | tf_op jit(solution)/shard_map/ppermute | solution.py:62
  246.4 27.0 %collective-permute-start.11 = (bf16[128,4096]{1,0:T(8,128)(2,1)}, bf16[128,4096]{1,0:T(8,128)(2,1)}, u32[]{:S(2)}, u32[]{:S(2)}) collective-permute-start(bf16[128,4096]{1,0:T(8,128)(2,1)} %get-tuple-element.24), channel_id=1, source_target_pairs={{4,0},{8,4},{12,8},{5,1},{9,5},{13,9},{6,2},{10,6},{14,10},{7,3},{... | collective-permute-start | bytes 3145736 | tf_op jit(solution)/shard_map/ppermute | solution.py:65
  263.0 10.3 %copy-start.3 = (f32[128,4096]{1,0:T(8,128)S(1)}, f32[128,4096]{1,0:T(8,128)}, u32[]{:S(2)}) copy-start(f32[128,4096]{1,0:T(8,128)} %convolution_multiply_fusion.4) | copy-start | bytes 6291460
  263.0 10.3 %copy-start.10 = (bf16[128,4096]{1,0:T(8,128)(2,1)S(1)}, bf16[128,4096]{1,0:T(8,128)(2,1)}, u32[]{:S(2)}) copy-start(bf16[128,4096]{1,0:T(8,128)(2,1)} %copy-done.9) | copy-start | bytes 3145732
  288.3 18.7 %copy-start.27 = (bf16[224,256]{1,0:T(8,128)(2,1)S(1)}, bf16[224,256]{1,0:T(8,128)(2,1)}, u32[]{:S(2)}) copy-start(bf16[224,256]{1,0:T(8,128)(2,1)} %fusion.49) | copy-start | bytes 344068
  288.3 47.6 %all-to-all-start.3 = ((bf16[4,56,8192]{2,1,0:T(8,128)(2,1)}), bf16[4,56,8192]{2,1,0:T(8,128)(2,1)}, u32[]{:S(2)}, u32[]{:S(2)}) async-start(bf16[4,56,8192]{2,1,0:T(8,128)(2,1)} %bitcast.97), calls=%async_computation.3 | async-start | bytes 7340032 | tf_op jit(solution)/shard_map/all_to_all | solution.py:89
  299.7 38.6 %collective-permute-start.6 = (bf16[128,4096]{1,0:T(8,128)(2,1)}, bf16[128,4096]{1,0:T(8,128)(2,1)}, u32[]{:S(2)}, u32[]{:S(2)}) collective-permute-start(bf16[128,4096]{1,0:T(8,128)(2,1)} %get-tuple-element.47), channel_id=1, source_target_pairs={{0,4},{4,8},{8,12},{1,5},{5,9},{9,13},{2,6},{6,10},{10,14},{3,7},{... | collective-permute-start | bytes 3145736 | tf_op jit(solution)/shard_map/ppermute | solution.py:62
  305.4 14.3 %copy-start.14 = (bf16[2,8192,64]{1,2,0:T(8,128)(2,1)S(1)}, bf16[2,8192,64]{1,2,0:T(8,128)(2,1)}, u32[]{:S(2)}) copy-start(bf16[2,8192,64]{1,2,0:T(8,128)(2,1)} %param.12) | copy-start | bytes 6291460
  305.4 14.3 %copy-start.21 = (bf16[128,4096]{1,0:T(8,128)(2,1)S(1)}, bf16[128,4096]{1,0:T(8,128)(2,1)}, u32[]{:S(2)}) copy-start(bf16[128,4096]{1,0:T(8,128)(2,1)} %get-tuple-element.37) | copy-start | bytes 3145732
  305.4 14.3 %copy-start.25 = (bf16[128,4096]{1,0:T(8,128)(2,1)S(1)}, bf16[128,4096]{1,0:T(8,128)(2,1)}, u32[]{:S(2)}) copy-start(bf16[128,4096]{1,0:T(8,128)(2,1)} %copy-done.24) | copy-start | bytes 3145732
  305.4 14.3 %copy-start.41 = (s32[256]{0:T(256)S(1)}, s32[256]{0:T(256)}, u32[]{:S(2)}) copy-start(s32[256]{0:T(256)} %copy-done.40) | copy-start | bytes 3076
  305.4 33.0 %collective-permute-start.7 = (bf16[128,4096]{1,0:T(8,128)(2,1)}, bf16[128,4096]{1,0:T(8,128)(2,1)}, u32[]{:S(2)}, u32[]{:S(2)}) collective-permute-start(bf16[128,4096]{1,0:T(8,128)(2,1)} %get-tuple-element.22), channel_id=1, source_target_pairs={{4,0},{8,4},{12,8},{5,1},{9,5},{13,9},{6,2},{10,6},{14,10},{7,3},{... | collective-permute-start | bytes 3145736 | tf_op jit(solution)/shard_map/ppermute | solution.py:65
  312.2 104.6 %collective-permute-start.15 = (bf16[128,4096]{1,0:T(8,128)(2,1)}, bf16[128,4096]{1,0:T(8,128)(2,1)}, u32[]{:S(2)}, u32[]{:S(2)}) collective-permute-start(bf16[128,4096]{1,0:T(8,128)(2,1)} %get-tuple-element.32), channel_id=1, source_target_pairs={{4,0},{8,4},{12,8},{5,1},{9,5},{13,9},{6,2},{10,6},{14,10},{7,3},{... | collective-permute-start | bytes 3145736 | tf_op jit(solution)/shard_map/ppermute | solution.py:65
  313.5 103.4 %collective-permute-start.13 = (bf16[128,4096]{1,0:T(8,128)(2,1)}, bf16[128,4096]{1,0:T(8,128)(2,1)}, u32[]{:S(2)}, u32[]{:S(2)}) collective-permute-start(bf16[128,4096]{1,0:T(8,128)(2,1)} %get-tuple-element.33), channel_id=1, source_target_pairs={{0,4},{4,8},{8,12},{1,5},{5,9},{9,13},{2,6},{6,10},{10,14},{3,7},{... | collective-permute-start | bytes 3145736 | tf_op jit(solution)/shard_map/ppermute | solution.py:62
  345.0 26.6 %all-to-all-start.4 = ((bf16[4,56,4096]{2,1,0:T(8,128)(2,1)}), bf16[4,56,4096]{2,1,0:T(8,128)(2,1)S(1)}, u32[]{:S(2)}, u32[]{:S(2)}) async-start(bf16[4,56,4096]{2,1,0:T(8,128)(2,1)} %bitcast.110), calls=%async_computation.4 | async-start | bytes 3670016 | tf_op jit(solution)/shard_map/all_to_all | solution.py:89
  374.5 10.3 %copy-start.28 = (bf16[224,256]{1,0:T(8,128)(2,1)S(1)}, bf16[224,256]{1,0:T(8,128)(2,1)}, u32[]{:S(2)}) copy-start(bf16[224,256]{1,0:T(8,128)(2,1)} %fusion.49) | copy-start | bytes 344068
  374.5 26.1 %all-to-all-start.5 = ((bf16[4,56,2048]{2,1,0:T(8,128)(2,1)}), bf16[4,56,2048]{2,1,0:T(8,128)(2,1)S(1)}, u32[]{:S(2)}, u32[]{:S(2)}) async-start(bf16[4,56,2048]{2,1,0:T(8,128)(2,1)} %maximum_select_fusion), calls=%async_computation.5 | async-start | bytes 1835008 | tf_op jit(solution)/shard_map/all_to_all | solution.py:89
  379.8 11.0 %collective-permute-start.16 = (bf16[128,1024]{1,0:T(8,128)(2,1)S(1)}, bf16[128,1024]{1,0:T(8,128)(2,1)S(1)}, u32[]{:S(2)}, u32[]{:S(2)}) collective-permute-start(bf16[128,1024]{1,0:T(8,128)(2,1)S(1)} %get-tuple-element.44), channel_id=1, source_target_pairs={{0,4},{4,8},{8,12},{12,0},{1,5},{5,9},{9,13},{13,1},{2,6},{6,10},{... | collective-permute-start | bytes 786440 | tf_op jit(solution)/shard_map/ppermute | solution.py:59
  382.8 13.2 %collective-permute-start.18 = (bf16[128,1024]{1,0:T(8,128)(2,1)S(1)}, bf16[128,1024]{1,0:T(8,128)(2,1)S(1)}, u32[]{:S(2)}, u32[]{:S(2)}) collective-permute-start(bf16[128,1024]{1,0:T(8,128)(2,1)S(1)} %get-tuple-element.45), channel_id=1, source_target_pairs={{0,12},{4,0},{8,4},{12,8},{1,13},{5,1},{9,5},{13,9},{2,14},{6,2},{... | collective-permute-start | bytes 786440 | tf_op jit(solution)/shard_map/ppermute | solution.py:59
  383.7 31.3 %collective-permute-start.17 = (bf16[128,1024]{1,0:T(8,128)(2,1)S(1)}, bf16[128,1024]{1,0:T(8,128)(2,1)}, u32[]{:S(2)}, u32[]{:S(2)}) collective-permute-start(bf16[128,1024]{1,0:T(8,128)(2,1)S(1)} %get-tuple-element.46), channel_id=1, source_target_pairs={{0,8},{4,12},{8,0},{12,4},{1,9},{5,13},{9,1},{13,5},{2,10},{6,14},... | collective-permute-start | bytes 786440 | tf_op jit(solution)/shard_map/ppermute | solution.py:59
  390.8 33.3 %collective-permute-start.14 = (bf16[128,4096]{1,0:T(8,128)(2,1)}, bf16[128,4096]{1,0:T(8,128)(2,1)}, u32[]{:S(2)}, u32[]{:S(2)}) collective-permute-start(bf16[128,4096]{1,0:T(8,128)(2,1)} %get-tuple-element.30), channel_id=1, source_target_pairs={{4,0},{8,4},{12,8},{5,1},{9,5},{13,9},{6,2},{10,6},{14,10},{7,3},{... | collective-permute-start | bytes 3145736 | tf_op jit(solution)/shard_map/ppermute | solution.py:65
  396.7 27.4 %collective-permute-start.12 = (bf16[128,4096]{1,0:T(8,128)(2,1)}, bf16[128,4096]{1,0:T(8,128)(2,1)}, u32[]{:S(2)}, u32[]{:S(2)}) collective-permute-start(bf16[128,4096]{1,0:T(8,128)(2,1)} %get-tuple-element.31), channel_id=1, source_target_pairs={{0,4},{4,8},{8,12},{1,5},{5,9},{9,13},{2,6},{6,10},{10,14},{3,7},{... | collective-permute-start | bytes 3145736 | tf_op jit(solution)/shard_map/ppermute | solution.py:62
  400.6 31.8 %all-to-all-start.6 = ((bf16[4,56,4096]{2,1,0:T(8,128)(2,1)}), bf16[4,56,4096]{2,1,0:T(8,128)(2,1)}, u32[]{:S(2)}, u32[]{:S(2)}) async-start(bf16[4,56,4096]{2,1,0:T(8,128)(2,1)} %bitcast.109), calls=%async_computation.6 | async-start | bytes 3670016 | tf_op jit(solution)/shard_map/all_to_all | solution.py:89
  405.3 9.7 %copy-start.11 = (f32[256,1024]{1,0:T(8,128)S(1)}, f32[256,1024]{1,0:T(8,128)}, u32[]{:S(2)}) copy-start(f32[256,1024]{1,0:T(8,128)} %get-tuple-element.66) | copy-start | bytes 3145732
  405.3 18.8 %copy-start.37 = (bf16[224,256]{1,0:T(8,128)(2,1)S(1)}, bf16[224,256]{1,0:T(8,128)(2,1)}, u32[]{:S(2)}) copy-start(bf16[224,256]{1,0:T(8,128)(2,1)} %fusion.48) | copy-start | bytes 344068
  416.8 13.8 %copy-start.18 = (f32[256,1024]{0,1:T(8,128)S(1)}, f32[256,1024]{0,1:T(8,128)}, u32[]{:S(2)}) copy-start(f32[256,1024]{0,1:T(8,128)} %copy-done.17) | copy-start | bytes 3145732
  432.4 14.1 %copy-start.1 = (bf16[256,1024]{1,0:T(8,128)(2,1)S(1)}, bf16[256,1024]{1,0:T(8,128)(2,1)}, u32[]{:S(2)}) copy-start(bf16[256,1024]{1,0:T(8,128)(2,1)} %param.10) | copy-start | bytes 1572868
  (22 other events, 93.4 us)
Sparse Core Ops, SparseCore 0:
  9.6 30.6 all-gather.2
  44.8 170.0 all-gather.4

commit v5 on v4

--- a/solution.py
+++ b/solution.py
@@ -114,12 +114,12 @@
     up_all = jnp.concatenate(
         [lax.dynamic_index_in_dim(ups, order[j], 0, False) for j in range(depth)], axis=0
     )
-    piece = tie(piece, ups)
-    whole = lax.all_gather(piece, ("chain", "side", "core", "groups"), axis=0, tiled=True)
 
     a = [down_rows[:, :half], down_rows[:, half:]]
     one = [(up(v), down(v)) for v in a]
     cots = exchange(jnp.concatenate([spread_out(p, cotangent) for p in range(2)], 1))
+    piece = tie(piece, cots)
+    whole = lax.all_gather(piece, ("chain", "side", "core", "groups"), axis=0, tiled=True)
     cots = [cots[:, :features], cots[:, features:]]
     x0 = exchange(spread_out(0, tokens))
     x1 = exchange(tie(spread_out(1, tokens), x0))
@@ -154,8 +154,7 @@
         r1 = jnp.where(edge, jnp.zeros_like(uu), jnp.where(z == 1, uu, dd))
         v = grad(second, cols(x0, h), r1).astype(bf16)
         send_up, send_down = jnp.where(z <= 1, v, e2[h]), jnp.where(z >= 2, v, e2[h])
-        if h == 1:
-            send_up, send_down = tie(send_up, x1), tie(send_down, x1)
+        send_up, send_down = tie(send_up, x1), tie(send_down, x1)
         three[h] = up(send_up), down(send_down)
 
     frozen_out = dot(tokens, whole, ((1,), (0,)))
@@ -174,8 +173,7 @@
         third_up = jnp.where(z == 1, inner + ru.astype(f32), third_up)
         third_down = jnp.where(z == 2, inner + rd.astype(f32), third_down)
         third_up, third_down = third_up.astype(bf16), third_down.astype(bf16)
-        done = (back_1,) if h == 0 else (frozen_out, frozen_grad)
-        third_up, third_down = tie(third_up, *done), tie(third_down, *done)
+        third_up, third_down = tie(third_up, back_1), tie(third_down, back_1)
         four[h] = up(third_up), down(third_down)
         back_0[h] = exchange(tie(lora(0, far_a[h]), back_1 if h == 0 else back_0[0]))
     far_a = jnp.concatenate(far_a, 1)
@@ -206,7 +204,7 @@
         ],
         1,
     )
-    expanded = exchange(tie(expanded, back_0))
+    expanded = exchange(tie(expanded, back_0, frozen_out, frozen_grad))
 
     key_output = (
         frozen_out

time: 459 us -> 495 us (1.078)
  blocking collectives: 0 us -> 56.6 us
  starting transfers between devices: 86.2 us -> 78.1 us
  matrix products: 109 us -> 102 us
  waiting for transfers between devices: 176 us -> 171 us
    all_to_all x0 -> x1, blocking collectives: none -> 56.6 us  [exchange(): lax.all_to_all(values, across, split_axis=0, concat_axis=0, tiled=True)]
    ppermute x8, waiting for transfers between devices: 13.3 us -> 59.6 us  [up(): return lax.ppermute(values, 'chain', [(i, i + 1) for i in range(depth - 1)])]
    all_to_all x7 -> x6, waiting for transfers between devices: 62.8 us -> 20.4 us  [exchange(): lax.all_to_all(values, across, split_axis=0, concat_axis=0, tiled=True)]
    ppermute x3, waiting for transfers between devices: 8.05 us -> 46.9 us  [turn(): lax.ppermute(values, 'chain', [(i, (i + k) % depth) for i in range(depth)])]
    all_gather x1, waiting for transfers between devices: 32.3 us -> 0.01 us  [shards(): ups = lax.all_gather(up_rows, 'chain', axis=0, tiled=False)]
    ppermute x8, waiting for transfers between devices: 58.5 us -> 43.8 us  [down(): return lax.ppermute(values, 'chain', [(i + 1, i) for i in range(depth - 1)])]
    dot_general x30, matrix products: 109 us -> 102 us  [dot(): return lax.dot_general(a, b, (dims, ((), ())), preferred_element_type=f32)]
    all_to_all x7 -> x6, starting transfers between devices: 30.3 us -> 26 us  [exchange(): lax.all_to_all(values, across, split_axis=0, concat_axis=0, tiled=True)]
  transfers between devices with their start and end apart: 28 -> 27, of which waited for: 12 -> 13; matrix products, arithmetic and copies ran while one was open for 26% -> 29% of each run, Pallas kernels for 0% -> 0%
where the time goes in v5:
time: 495 us; the launch traced here: 492 us
  waiting for transfers between devices  171 us (35%)
  matrix products  102 us (21%)
  starting transfers between devices  78.1 us (16%)
  blocking collectives  56.6 us (11%)
  between operations  37 us (7%)
  other arithmetic  23.8 us (5%)
  local copies, waits for them, and re-layouts  23.6 us (5%)
    dot_general x30, matrix products, dot(): return lax.dot_general(a, b, (dims, ((), ())), preferred_element_type=f32)  102 us
    ppermute x8, waiting for transfers between devices, up(): return lax.ppermute(values, 'chain', [(i, i + 1) for i in range(depth - 1)])  59.6 us
    all_to_all x1, blocking collectives, exchange(): lax.all_to_all(values, across, split_axis=0, concat_axis=0, tiled=True)  56.6 us
    ppermute x3, waiting for transfers between devices, turn(): lax.ppermute(values, 'chain', [(i, (i + k) % depth) for i in range(depth)])  46.9 us
    ppermute x8, waiting for transfers between devices, down(): return lax.ppermute(values, 'chain', [(i + 1, i) for i in range(depth - 1)])  43.8 us
    ppermute x8, starting transfers between devices, up(): return lax.ppermute(values, 'chain', [(i, i + 1) for i in range(depth - 1)])  38.6 us
    all_to_all x6, starting transfers between devices, exchange(): lax.all_to_all(values, across, split_axis=0, concat_axis=0, tiled=True)  26 us
    all_to_all x6, waiting for transfers between devices, exchange(): lax.all_to_all(values, across, split_axis=0, concat_axis=0, tiled=True)  20.4 us
  transfers between devices with their start and end apart: 27, of which 13 were waited for; matrix products, arithmetic and copies ran while one was open for 29% of the time, Pallas kernels for 0%

profile of v5, /device:TPU:0, one launch (start us, length us, event | category | flops | bytes accessed | tf_op | source)
XLA Modules:
  0.0 492.5 jit_solution(14469244028023099115)
XLA Ops:
  12.7 4.2 all-to-all-start
  16.9 13.1 %all-to-all-done = bf16[4,56,2048]{2,1,0:T(8,128)(2,1)S(1)} async-done(((bf16[4,56,2048]{2,1,0:T(8,128)(2,1)}), bf16[4,56,2048]{2,1,0:T(8,128)(2,1)S(1)}, u32[]{:S(2)}, u32[]{:S(2)}) %all-to-all-start) | async-done | bytes 917536 | tf_op jit(solution)/shard_map/all_to_all | solution.py:89
  32.7 3.3 convolution_convert_fusion.1
  36.1 56.6 %all_to_all.81 = bf16[4,56,8192]{2,1,0:T(8,128)(2,1)S(1)} all-to-all(bf16[4,56,8192]{2,1,0:T(8,128)(2,1)S(1)} %bitcast.102), channel_id=1, replica_groups=mesh['groups'=2,'chain'=4,'side'=2,'core'=2] {'side','core'}, dimensions={0} | all-to-all | bytes 7340032 | tf_op jit(solution)/shard_map/all_to_all | solution.py:89
  96.4 3.0 fusion.2
  99.3 4.9 %all-to-all-start.2 = ((bf16[4,56,8192]{2,1,0:T(8,128)(2,1)}), bf16[4,56,8192]{2,1,0:T(8,128)(2,1)}, u32[]{:S(2)}, u32[]{:S(2)}) async-start(bf16[4,56,8192]{2,1,0:T(8,128)(2,1)} %bitcast.107), calls=%async_computation.2 | async-start | bytes 7340032 | tf_op jit(solution)/shard_map/all_to_all | solution.py:89
  105.7 4.2 collective-permute-start.1
  111.3 4.6 collective-permute-start.3
  129.8 26.1 %collective-permute-done.1 = bf16[128,4096]{1,0:T(8,128)(2,1)S(1)} collective-permute-done((bf16[128,4096]{1,0:T(8,128)(2,1)}, bf16[128,4096]{1,0:T(8,128)(2,1)S(1)}, u32[]{:S(2)}, u32[]{:S(2)}) %collective-permute-start.1) | collective-permute-done | bytes 1048608 | tf_op jit(solution)/shard_map/ppermute | solution.py:62
  155.9 7.2 %collective-permute-done = bf16[128,4096]{1,0:T(8,128)(2,1)} collective-permute-done((bf16[128,4096]{1,0:T(8,128)(2,1)}, bf16[128,4096]{1,0:T(8,128)(2,1)}, u32[]{:S(2)}, u32[]{:S(2)}) %collective-permute-start) | collective-permute-done | bytes 1048608 | tf_op jit(solution)/shard_map/ppermute | solution.py:65
  163.1 3.1 broadcast_select_fusion.5
  167.5 5.5 %collective-permute-start.4 = (bf16[128,4096]{1,0:T(8,128)(2,1)}, bf16[128,4096]{1,0:T(8,128)(2,1)}, u32[]{:S(2)}, u32[]{:S(2)}) collective-permute-start(bf16[128,4096]{1,0:T(8,128)(2,1)} %get-tuple-element.47), channel_id=1, source_target_pairs={{0,4},{4,8},{8,12},{1,5},{5,9},{9,13},{2,6},{6,10},{10,14},{3,7},{... | collective-permute-start | bytes 3145736 | tf_op jit(solution)/shard_map/ppermute | solution.py:62
  173.0 24.1 %collective-permute-done.3 = bf16[128,4096]{1,0:T(8,128)(2,1)S(1)} collective-permute-done((bf16[128,4096]{1,0:T(8,128)(2,1)}, bf16[128,4096]{1,0:T(8,128)(2,1)S(1)}, u32[]{:S(2)}, u32[]{:S(2)}) %collective-permute-start.3) | collective-permute-done | bytes 1048608 | tf_op jit(solution)/shard_map/ppermute | solution.py:62
  197.2 5.2 %collective-permute-done.2 = bf16[128,4096]{1,0:T(8,128)(2,1)} collective-permute-done((bf16[128,4096]{1,0:T(8,128)(2,1)}, bf16[128,4096]{1,0:T(8,128)(2,1)}, u32[]{:S(2)}, u32[]{:S(2)}) %collective-permute-start.2) | collective-permute-done | bytes 1048608 | tf_op jit(solution)/shard_map/ppermute | solution.py:65
  202.4 3.1 broadcast_select_fusion.4
  206.8 5.5 %collective-permute-start.8 = (bf16[128,4096]{1,0:T(8,128)(2,1)}, bf16[128,4096]{1,0:T(8,128)(2,1)}, u32[]{:S(2)}, u32[]{:S(2)}) collective-permute-start(bf16[128,4096]{1,0:T(8,128)(2,1)} %get-tuple-element.50), channel_id=1, source_target_pairs={{0,4},{4,8},{8,12},{1,5},{5,9},{9,13},{2,6},{6,10},{10,14},{3,7},{... | collective-permute-start | bytes 3145736 | tf_op jit(solution)/shard_map/ppermute | solution.py:62
  216.9 8.0 %collective-permute-done.5 = bf16[128,4096]{1,0:T(8,128)(2,1)} collective-permute-done((bf16[128,4096]{1,0:T(8,128)(2,1)}, bf16[128,4096]{1,0:T(8,128)(2,1)}, u32[]{:S(2)}, u32[]{:S(2)}) %collective-permute-start.5) | collective-permute-done | bytes 1048608 | tf_op jit(solution)/shard_map/ppermute | solution.py:65
  224.9 4.0 select_select_fusion.6
  228.9 18.2 %collective-permute-done.9 = bf16[128,4096]{1,0:T(8,128)(2,1)} collective-permute-done((bf16[128,4096]{1,0:T(8,128)(2,1)}, bf16[128,4096]{1,0:T(8,128)(2,1)}, u32[]{:S(2)}, u32[]{:S(2)}) %collective-permute-start.9) | collective-permute-done | bytes 1048608 | tf_op jit(solution)/shard_map/ppermute | solution.py:65
  247.1 3.3 select_select_fusion.2
  250.4 3.2 select_select_fusion.4
  253.6 3.3 select_select_fusion
  256.9 9.4 %fusion.3 = bf16[224,8192]{1,0:T(8,128)(2,1)} fusion(bf16[224,256]{1,0:T(8,128)(2,1)S(1)} %copy-done.37, pred[]{:T(512)} %bitcast.13, bf16[128,8192]{1,0:T(8,128)(2,1)S(1)} %bitcast.112, bf16[128,4096]{1,0:T(8,128)(2,1)S(1)} %get-tuple-element.39, bf16[128,4096]{1,0:T(8,128)(2,1)S(1)} %get-tuple-element.37), kind=kOutput, calls=%fused_computation.10 | convolution fusion | flops 957612032 | bytes 7979009 | tf_op jit(solution)/shard_map/dot_general | solution.py:15
  266.3 4.9 all-to-all-start.3
  282.0 4.4 collective-permute-start.10
  287.8 3.6 fusion.57
  291.5 5.5 %collective-permute-start.6 = (bf16[128,4096]{1,0:T(8,128)(2,1)}, bf16[128,4096]{1,0:T(8,128)(2,1)}, u32[]{:S(2)}, u32[]{:S(2)}) collective-permute-start(bf16[128,4096]{1,0:T(8,128)(2,1)} %get-tuple-element.45), channel_id=1, source_target_pairs={{0,4},{4,8},{8,12},{1,5},{5,9},{9,13},{2,6},{6,10},{10,14},{3,7},{... | collective-permute-start | bytes 3145736 | tf_op jit(solution)/shard_map/ppermute | solution.py:62
  299.8 3.3 convolution_multiply_fusion.4
  303.1 3.3 convolution_multiply_fusion.6
  306.4 7.3 %all-to-all-done.3 = bf16[4,56,8192]{2,1,0:T(8,128)(2,1)} async-done(((bf16[4,56,8192]{2,1,0:T(8,128)(2,1)}), bf16[4,56,8192]{2,1,0:T(8,128)(2,1)}, u32[]{:S(2)}, u32[]{:S(2)}) %all-to-all-start.3) | async-done | bytes 3670048 | tf_op jit(solution)/shard_map/all_to_all | solution.py:89
  316.3 5.5 %fusion.58 = (bf16[128,4096]{1,0:T(8,128)(2,1)}, bf16[128,4096]{1,0:T(8,128)(2,1)}, bf16[128,4096]{1,0:T(8,128)(2,1)S(1)}) fusion(f32[128,4096]{1,0:T(8,128)} %convolution_multiply_fusion.4, f32[128,4096]{1,0:T(8,128)} %convolution_multiply_fusion.5, bf16[128,4096]{1,0:T(8,128)(2,1)} %collective-permute-done.11, pred[]{:T(512)S(6)} %eq.162, pred[]{:T(512)} %bitcast.24, ...), kind=kLoop, calls=%fused_computation.94 | loop fusion | flops 8388608 | bytes 10485765 | tf_op jit(solution)/shard_map/jit(_where)/select_n | solution.py:23
  321.8 9.3 %collective-permute-done.6 = bf16[128,4096]{1,0:T(8,128)(2,1)} collective-permute-done((bf16[128,4096]{1,0:T(8,128)(2,1)}, bf16[128,4096]{1,0:T(8,128)(2,1)}, u32[]{:S(2)}, u32[]{:S(2)}) %collective-permute-start.6) | collective-permute-done | bytes 1048608 | tf_op jit(solution)/shard_map/ppermute | solution.py:62
  331.1 5.2 %collective-permute-done.7 = bf16[128,4096]{1,0:T(8,128)(2,1)} collective-permute-done((bf16[128,4096]{1,0:T(8,128)(2,1)}, bf16[128,4096]{1,0:T(8,128)(2,1)}, u32[]{:S(2)}, u32[]{:S(2)}) %collective-permute-start.7) | collective-permute-done | bytes 1048608 | tf_op jit(solution)/shard_map/ppermute | solution.py:65
  336.3 4.0 fusion.59
  344.9 5.5 %collective-permute-start.13 = (bf16[128,4096]{1,0:T(8,128)(2,1)}, bf16[128,4096]{1,0:T(8,128)(2,1)}, u32[]{:S(2)}, u32[]{:S(2)}) collective-permute-start(bf16[128,4096]{1,0:T(8,128)(2,1)} %get-tuple-element.33), channel_id=1, source_target_pairs={{0,4},{4,8},{8,12},{1,5},{5,9},{9,13},{2,6},{6,10},{10,14},{3,7},{... | collective-permute-start | bytes 3145736 | tf_op jit(solution)/shard_map/ppermute | solution.py:62
  354.1 3.2 collective-permute-start.12
  359.2 3.7 all-to-all-start.4
  363.0 17.7 %collective-permute-done.18 = bf16[128,1024]{1,0:T(8,128)(2,1)} collective-permute-done((bf16[128,1024]{1,0:T(8,128)(2,1)}, bf16[128,1024]{1,0:T(8,128)(2,1)}, u32[]{:S(2)}, u32[]{:S(2)}) %collective-permute-start.18) | collective-permute-done | bytes 262176 | tf_op jit(solution)/shard_map/ppermute | solution.py:59
  387.2 26.9 %collective-permute-done.17 = bf16[128,1024]{1,0:T(8,128)(2,1)S(1)} collective-permute-done((bf16[128,1024]{1,0:T(8,128)(2,1)}, bf16[128,1024]{1,0:T(8,128)(2,1)S(1)}, u32[]{:S(2)}, u32[]{:S(2)}) %collective-permute-start.17) | collective-permute-done | bytes 262176 | tf_op jit(solution)/shard_map/ppermute | solution.py:59
  416.1 6.6 %convert_add_fusion = f32[128,8192]{1,0:T(8,128)} fusion(bf16[128,4096]{1,0:T(8,128)(2,1)} %collective-permute-done.13, bf16[128,4096]{1,0:T(8,128)(2,1)} %collective-permute-done.12, bf16[128,4096]{1,0:T(8,128)(2,1)} %collective-permute-done.15, bf16[128,4096]{1,0:T(8,128)(2,1)} %collective-permute-done.14, bf16[224,8192]{1,0:T(8,128)(2,1)} %bitcast.12, ...), kind=kOutput, calls=%fused_computation.36 | convolution fusion | flops 481296384 | bytes 12115968 | tf_op jit(solution)/shard_map/dot_general | solution.py:15
  424.5 3.1 fusion.6
  427.7 4.7 all-to-all-start.6
  432.4 9.4 %convolution_bitcast_fusion.1 = f32[256,1024]{0,1:T(8,128)S(1)} fusion(bf16[8192,1024]{1,0:T(8,128)(2,1)} %all-gather.3.cloned.1.call-done, bf16[256,8192]{1,0:T(8,128)(2,1)} %param.9), kind=kOutput, calls=%fused_computation.77 | convolution fusion | flops 4294967296 | bytes 22020096 | tf_op jit(solution)/shard_map/dot_general | solution.py:15
  441.8 8.6 %convolution_bitcast_fusion = f32[256,8192]{0,1:T(8,128)S(1)} fusion(bf16[8192,1024]{1,0:T(8,128)(2,1)} %all-gather.3.cloned.1.call-done, bf16[256,1024]{1,0:T(8,128)(2,1)S(1)} %copy-done), kind=kOutput, calls=%fused_computation.2 | convolution fusion | flops 4294967296 | bytes 25690112 | tf_op jit(solution)/shard_map/dot_general | solution.py:15
  456.8 9.5 %convolution_add_fusion.1 = f32[256,8192]{0,1:T(8,128)} fusion(f32[256,8192]{0,1:T(8,128)} %copy-done.6, bf16[224,8192]{1,0:T(8,128)(2,1)} %bitcast.23, s32[256]{0:T(256)S(1)} %fusion.110, pred[256]{0:T(512)(128)(4,1)S(1)} %broadcast_compare_fusion.7), kind=kOutput, calls=%fused_computation.1 | convolution fusion | flops 941735936 | bytes 20448512 | tf_op jit(solution)/shard_map/dot_general | solution.py:15
  466.3 3.5 all-to-all-start.5
  469.8 7.7 %fusion = bf16[256,8192]{0,1:T(8,128)(2,1)} fusion(f32[256,8192]{0,1:T(8,128)} %convolution_add_fusion.1, bf16[224,4096]{1,0:T(8,128)(2,1)} %bitcast.39, bf16[224,4096]{1,0:T(8,128)(2,1)S(1)} %bitcast.104, s32[256]{0:T(256)S(1)} %fusion.110, pred[256]{0:T(512)(128)(4,1)S(1)} %get-tuple-element.26), kind=kOutput, calls=%fused_computation.4 | convolution fusion | flops 951173120 | bytes 16254208 | tf_op jit(solution)/shard_map/dot_general | solution.py:15
  477.5 6.4 %copy.39 = bf16[256,8192]{1,0:T(8,128)(2,1)} copy(bf16[256,8192]{0,1:T(8,128)(2,1)} %fusion) | data formatting | bytes 8388608
  (163 shorter events, 59.3 us)
Async XLA Ops:
  7.2 24.6 %copy-start.36 = (bf16[512,1024]{1,0:T(8,128)(2,1)S(1)}, bf16[512,1024]{1,0:T(8,128)(2,1)}, u32[]{:S(2)}) copy-start(bf16[512,1024]{1,0:T(8,128)(2,1)} %param.11) | copy-start | bytes 3145732
  7.2 119.4 %all-gather.5.cloned.1.call-start = ((), (), s32[]{:S(2)}) async-start(), calls=%async_computation.8 | async-start | bytes 1310720 | tf_op jit(solution)/shard_map/all_gather | solution.py:113
  12.7 17.3 %all-to-all-start = ((bf16[4,56,2048]{2,1,0:T(8,128)(2,1)}), bf16[4,56,2048]{2,1,0:T(8,128)(2,1)S(1)}, u32[]{:S(2)}, u32[]{:S(2)}) async-start(bf16[4,56,2048]{2,1,0:T(8,128)(2,1)} %bitcast.4), calls=%async_computation | async-start | bytes 1835008 | tf_op jit(solution)/shard_map/all_to_all | solution.py:89
  16.9 415.5 %all-gather.3.cloned.1.call-start = ((), (), s32[]{:S(2)}) async-start(), calls=%async_computation.7 | async-start | bytes 17301504 | tf_op jit(solution)/shard_map/all_gather | solution.py:122
  30.0 182.4 %copy-start.16 = (bf16[4,56,2048]{2,1,0:T(8,128)(2,1)}, bf16[4,56,2048]{2,1,0:T(8,128)(2,1)S(1)}, u32[]{:S(2)}) copy-start(bf16[4,56,2048]{2,1,0:T(8,128)(2,1)S(1)} %all-to-all-done) | copy-start | bytes 2752516
  36.1 60.3 %copy-start.8 = (bf16[256,8192]{1,0:T(8,128)(2,1)S(1)}, bf16[256,8192]{1,0:T(8,128)(2,1)}, u32[]{:S(2)}) copy-start(bf16[256,8192]{1,0:T(8,128)(2,1)} %param.9) | copy-start | bytes 12582916
  99.3 115.1 %all-to-all-start.2 = ((bf16[4,56,8192]{2,1,0:T(8,128)(2,1)}), bf16[4,56,8192]{2,1,0:T(8,128)(2,1)}, u32[]{:S(2)}, u32[]{:S(2)}) async-start(bf16[4,56,8192]{2,1,0:T(8,128)(2,1)} %bitcast.107), calls=%async_computation.2 | async-start | bytes 7340032 | tf_op jit(solution)/shard_map/all_to_all | solution.py:89
  105.7 50.2 %collective-permute-start.1 = (bf16[128,4096]{1,0:T(8,128)(2,1)}, bf16[128,4096]{1,0:T(8,128)(2,1)S(1)}, u32[]{:S(2)}, u32[]{:S(2)}) collective-permute-start(bf16[128,4096]{1,0:T(8,128)(2,1)} %get-tuple-element.40), channel_id=1, source_target_pairs={{0,4},{4,8},{8,12},{1,5},{5,9},{9,13},{2,6},{6,10},{10,14},{3,7},{... | collective-permute-start | bytes 3145736 | tf_op jit(solution)/shard_map/ppermute | solution.py:62
  110.0 53.2 %collective-permute-start = (bf16[128,4096]{1,0:T(8,128)(2,1)}, bf16[128,4096]{1,0:T(8,128)(2,1)}, u32[]{:S(2)}, u32[]{:S(2)}) collective-permute-start(bf16[128,4096]{1,0:T(8,128)(2,1)} %get-tuple-element.40), channel_id=1, source_target_pairs={{4,0},{8,4},{12,8},{5,1},{9,5},{13,9},{6,2},{10,6},{14,10},{7,3},{... | collective-permute-start | bytes 3145736 | tf_op jit(solution)/shard_map/ppermute | solution.py:65
  111.3 85.9 %collective-permute-start.3 = (bf16[128,4096]{1,0:T(8,128)(2,1)}, bf16[128,4096]{1,0:T(8,128)(2,1)S(1)}, u32[]{:S(2)}, u32[]{:S(2)}) collective-permute-start(bf16[128,4096]{1,0:T(8,128)(2,1)} %get-tuple-element.41), channel_id=1, source_target_pairs={{0,4},{4,8},{8,12},{1,5},{5,9},{9,13},{2,6},{6,10},{10,14},{3,7},{... | collective-permute-start | bytes 3145736 | tf_op jit(solution)/shard_map/ppermute | solution.py:62
  115.9 86.5 %collective-permute-start.2 = (bf16[128,4096]{1,0:T(8,128)(2,1)}, bf16[128,4096]{1,0:T(8,128)(2,1)}, u32[]{:S(2)}, u32[]{:S(2)}) collective-permute-start(bf16[128,4096]{1,0:T(8,128)(2,1)} %get-tuple-element.41), channel_id=1, source_target_pairs={{4,0},{8,4},{12,8},{5,1},{9,5},{13,9},{6,2},{10,6},{14,10},{7,3},{... | collective-permute-start | bytes 3145736 | tf_op jit(solution)/shard_map/ppermute | solution.py:65
  126.6 36.6 %copy-start.2 = (bf16[4,56,8192]{2,1,0:T(8,128)(2,1)S(1)}, bf16[4,56,8192]{2,1,0:T(8,128)(2,1)}, u32[]{:S(2)}) copy-start(bf16[4,56,8192]{2,1,0:T(8,128)(2,1)} %copy-done.1) | copy-start | bytes 11010052
  128.8 27.1 %copy-start.33 = (bf16[128,1024]{1,0:T(8,128)(2,1)}, bf16[128,1024]{1,0:T(8,128)(2,1)S(1)}, u32[]{:S(2)}) copy-start(bf16[128,1024]{1,0:T(8,128)(2,1)S(1)} %get-tuple-element.51) | copy-start | bytes 786436
  128.8 27.1 %copy-start.34 = (bf16[128,1024]{1,0:T(8,128)(2,1)}, bf16[128,1024]{1,0:T(8,128)(2,1)S(1)}, u32[]{:S(2)}) copy-start(bf16[128,1024]{1,0:T(8,128)(2,1)S(1)} %get-tuple-element.52) | copy-start | bytes 786436
  129.8 75.7 %copy-start.29 = (bf16[224,256]{1,0:T(8,128)(2,1)}, bf16[224,256]{1,0:T(8,128)(2,1)S(1)}, u32[]{:S(2)}) copy-start(bf16[224,256]{1,0:T(8,128)(2,1)S(1)} %fusion.49) | copy-start | bytes 344068
  166.2 58.7 %collective-permute-start.5 = (bf16[128,4096]{1,0:T(8,128)(2,1)}, bf16[128,4096]{1,0:T(8,128)(2,1)}, u32[]{:S(2)}, u32[]{:S(2)}) collective-permute-start(bf16[128,4096]{1,0:T(8,128)(2,1)} %get-tuple-element.46), channel_id=1, source_target_pairs={{4,0},{8,4},{12,8},{5,1},{9,5},{13,9},{6,2},{10,6},{14,10},{7,3},{... | collective-permute-start | bytes 3145736 | tf_op jit(solution)/shard_map/ppermute | solution.py:65
  167.5 57.4 %collective-permute-start.4 = (bf16[128,4096]{1,0:T(8,128)(2,1)}, bf16[128,4096]{1,0:T(8,128)(2,1)}, u32[]{:S(2)}, u32[]{:S(2)}) collective-permute-start(bf16[128,4096]{1,0:T(8,128)(2,1)} %get-tuple-element.47), channel_id=1, source_target_pairs={{0,4},{4,8},{8,12},{1,5},{5,9},{9,13},{2,6},{6,10},{10,14},{3,7},{... | collective-permute-start | bytes 3145736 | tf_op jit(solution)/shard_map/ppermute | solution.py:62
  205.5 41.5 %collective-permute-start.9 = (bf16[128,4096]{1,0:T(8,128)(2,1)}, bf16[128,4096]{1,0:T(8,128)(2,1)}, u32[]{:S(2)}, u32[]{:S(2)}) collective-permute-start(bf16[128,4096]{1,0:T(8,128)(2,1)} %get-tuple-element.49), channel_id=1, source_target_pairs={{4,0},{8,4},{12,8},{5,1},{9,5},{13,9},{6,2},{10,6},{14,10},{7,3},{... | collective-permute-start | bytes 3145736 | tf_op jit(solution)/shard_map/ppermute | solution.py:65
  206.8 40.2 %collective-permute-start.8 = (bf16[128,4096]{1,0:T(8,128)(2,1)}, bf16[128,4096]{1,0:T(8,128)(2,1)}, u32[]{:S(2)}, u32[]{:S(2)}) collective-permute-start(bf16[128,4096]{1,0:T(8,128)(2,1)} %get-tuple-element.50), channel_id=1, source_target_pairs={{0,4},{4,8},{8,12},{1,5},{5,9},{9,13},{2,6},{6,10},{10,14},{3,7},{... | collective-permute-start | bytes 3145736 | tf_op jit(solution)/shard_map/ppermute | solution.py:62
  224.9 22.2 %copy-start.3 = (bf16[4,56,8192]{2,1,0:T(8,128)(2,1)S(1)}, bf16[4,56,8192]{2,1,0:T(8,128)(2,1)}, u32[]{:S(2)}) copy-start(bf16[4,56,8192]{2,1,0:T(8,128)(2,1)} %copy-done.1) | copy-start | bytes 11010052
  224.9 22.2 %copy-start.30 = (bf16[224,256]{1,0:T(8,128)(2,1)S(1)}, bf16[224,256]{1,0:T(8,128)(2,1)}, u32[]{:S(2)}) copy-start(bf16[224,256]{1,0:T(8,128)(2,1)} %copy-done.29) | copy-start | bytes 344068
  228.8 21.6 %copy-start.9 = (bf16[128,4096]{1,0:T(8,128)(2,1)}, bf16[128,4096]{1,0:T(8,128)(2,1)S(1)}, u32[]{:S(2)}) copy-start(bf16[128,4096]{1,0:T(8,128)(2,1)S(1)} %get-tuple-element.23) | copy-start | bytes 3145732
  266.3 47.5 %all-to-all-start.3 = ((bf16[4,56,8192]{2,1,0:T(8,128)(2,1)}), bf16[4,56,8192]{2,1,0:T(8,128)(2,1)}, u32[]{:S(2)}, u32[]{:S(2)}) async-start(bf16[4,56,8192]{2,1,0:T(8,128)(2,1)} %bitcast.106), calls=%async_computation.3 | async-start | bytes 7340032 | tf_op jit(solution)/shard_map/all_to_all | solution.py:89
  282.0 34.3 %collective-permute-start.10 = (bf16[128,4096]{1,0:T(8,128)(2,1)}, bf16[128,4096]{1,0:T(8,128)(2,1)}, u32[]{:S(2)}, u32[]{:S(2)}) collective-permute-start(bf16[128,4096]{1,0:T(8,128)(2,1)} %get-tuple-element.48), channel_id=1, source_target_pairs={{0,4},{4,8},{8,12},{1,5},{5,9},{9,13},{2,6},{6,10},{10,14},{3,7},{... | collective-permute-start | bytes 3145736 | tf_op jit(solution)/shard_map/ppermute | solution.py:62
  286.3 29.9 %collective-permute-start.11 = (bf16[128,4096]{1,0:T(8,128)(2,1)}, bf16[128,4096]{1,0:T(8,128)(2,1)}, u32[]{:S(2)}, u32[]{:S(2)}) collective-permute-start(bf16[128,4096]{1,0:T(8,128)(2,1)} %get-tuple-element.24), channel_id=1, source_target_pairs={{4,0},{8,4},{12,8},{5,1},{9,5},{13,9},{6,2},{10,6},{14,10},{7,3},{... | collective-permute-start | bytes 3145736 | tf_op jit(solution)/shard_map/ppermute | solution.py:65
  291.4 15.0 %copy-start.39 = (bf16[224,256]{1,0:T(8,128)(2,1)}, bf16[224,256]{1,0:T(8,128)(2,1)S(1)}, u32[]{:S(2)}) copy-start(bf16[224,256]{1,0:T(8,128)(2,1)S(1)} %fusion.57) | copy-start | bytes 344068
  291.5 39.6 %collective-permute-start.6 = (bf16[128,4096]{1,0:T(8,128)(2,1)}, bf16[128,4096]{1,0:T(8,128)(2,1)}, u32[]{:S(2)}, u32[]{:S(2)}) collective-permute-start(bf16[128,4096]{1,0:T(8,128)(2,1)} %get-tuple-element.45), channel_id=1, source_target_pairs={{0,4},{4,8},{8,12},{1,5},{5,9},{9,13},{2,6},{6,10},{10,14},{3,7},{... | collective-permute-start | bytes 3145736 | tf_op jit(solution)/shard_map/ppermute | solution.py:62
  297.0 39.3 %collective-permute-start.7 = (bf16[128,4096]{1,0:T(8,128)(2,1)}, bf16[128,4096]{1,0:T(8,128)(2,1)}, u32[]{:S(2)}, u32[]{:S(2)}) collective-permute-start(bf16[128,4096]{1,0:T(8,128)(2,1)} %get-tuple-element.22), channel_id=1, source_target_pairs={{4,0},{8,4},{12,8},{5,1},{9,5},{13,9},{6,2},{10,6},{14,10},{7,3},{... | collective-permute-start | bytes 3145736 | tf_op jit(solution)/shard_map/ppermute | solution.py:65
  316.3 20.0 %copy-start.7 = (f32[128,4096]{1,0:T(8,128)S(1)}, f32[128,4096]{1,0:T(8,128)}, u32[]{:S(2)}) copy-start(f32[128,4096]{1,0:T(8,128)} %convolution_multiply_fusion.6) | copy-start | bytes 6291460
  316.3 20.0 %copy-start.10 = (bf16[128,4096]{1,0:T(8,128)(2,1)S(1)}, bf16[128,4096]{1,0:T(8,128)(2,1)}, u32[]{:S(2)}) copy-start(bf16[128,4096]{1,0:T(8,128)(2,1)} %copy-done.9) | copy-start | bytes 3145732
  321.7 18.6 %copy-start.19 = (bf16[128,4096]{1,0:T(8,128)(2,1)}, bf16[128,4096]{1,0:T(8,128)(2,1)S(1)}, u32[]{:S(2)}) copy-start(bf16[128,4096]{1,0:T(8,128)(2,1)S(1)} %get-tuple-element.34) | copy-start | bytes 3145732
  321.8 18.6 %copy-start.5 = (bf16[4,56,8192]{2,1,0:T(8,128)(2,1)S(1)}, bf16[4,56,8192]{2,1,0:T(8,128)(2,1)}, u32[]{:S(2)}) copy-start(bf16[4,56,8192]{2,1,0:T(8,128)(2,1)} %copy-done.1) | copy-start | bytes 11010052
  321.8 18.6 %copy-start.23 = (bf16[128,4096]{1,0:T(8,128)(2,1)S(1)}, bf16[128,4096]{1,0:T(8,128)(2,1)}, u32[]{:S(2)}) copy-start(bf16[128,4096]{1,0:T(8,128)(2,1)} %get-tuple-element.38) | copy-start | bytes 3145732
  321.8 18.6 %copy-start.24 = (bf16[128,4096]{1,0:T(8,128)(2,1)S(1)}, bf16[128,4096]{1,0:T(8,128)(2,1)}, u32[]{:S(2)}) copy-start(bf16[128,4096]{1,0:T(8,128)(2,1)} %get-tuple-element.36) | copy-start | bytes 3145732
  341.7 15.6 %copy-start.42 = (bf16[224,256]{1,0:T(8,128)(2,1)}, bf16[224,256]{1,0:T(8,128)(2,1)S(1)}, u32[]{:S(2)}) copy-start(bf16[224,256]{1,0:T(8,128)(2,1)S(1)} %fusion.53) | copy-start | bytes 344068
  343.0 11.1 %collective-permute-start.16 = (bf16[128,1024]{1,0:T(8,128)(2,1)S(1)}, bf16[128,1024]{1,0:T(8,128)(2,1)S(1)}, u32[]{:S(2)}, u32[]{:S(2)}) collective-permute-start(bf16[128,1024]{1,0:T(8,128)(2,1)S(1)} %get-tuple-element.42), channel_id=1, source_target_pairs={{0,4},{4,8},{8,12},{12,0},{1,5},{5,9},{9,13},{13,1},{2,6},{6,10},{... | collective-permute-start | bytes 786440 | tf_op jit(solution)/shard_map/ppermute | solution.py:59
  343.6 72.4 %collective-permute-start.15 = (bf16[128,4096]{1,0:T(8,128)(2,1)}, bf16[128,4096]{1,0:T(8,128)(2,1)}, u32[]{:S(2)}, u32[]{:S(2)}) collective-permute-start(bf16[128,4096]{1,0:T(8,128)(2,1)} %get-tuple-element.32), channel_id=1, source_target_pairs={{4,0},{8,4},{12,8},{5,1},{9,5},{13,9},{6,2},{10,6},{14,10},{7,3},{... | collective-permute-start | bytes 3145736 | tf_op jit(solution)/shard_map/ppermute | solution.py:65
  344.9 71.1 %collective-permute-start.13 = (bf16[128,4096]{1,0:T(8,128)(2,1)}, bf16[128,4096]{1,0:T(8,128)(2,1)}, u32[]{:S(2)}, u32[]{:S(2)}) collective-permute-start(bf16[128,4096]{1,0:T(8,128)(2,1)} %get-tuple-element.33), channel_id=1, source_target_pairs={{0,4},{4,8},{8,12},{1,5},{5,9},{9,13},{2,6},{6,10},{10,14},{3,7},{... | collective-permute-start | bytes 3145736 | tf_op jit(solution)/shard_map/ppermute | solution.py:62
  350.4 30.2 %collective-permute-start.18 = (bf16[128,1024]{1,0:T(8,128)(2,1)}, bf16[128,1024]{1,0:T(8,128)(2,1)}, u32[]{:S(2)}, u32[]{:S(2)}) collective-permute-start(bf16[128,1024]{1,0:T(8,128)(2,1)} %get-tuple-element.43), channel_id=1, source_target_pairs={{0,12},{4,0},{8,4},{12,8},{1,13},{5,1},{9,5},{13,9},{2,14},{6,2},{... | collective-permute-start | bytes 786440 | tf_op jit(solution)/shard_map/ppermute | solution.py:59
  350.4 65.6 %collective-permute-start.14 = (bf16[128,4096]{1,0:T(8,128)(2,1)}, bf16[128,4096]{1,0:T(8,128)(2,1)}, u32[]{:S(2)}, u32[]{:S(2)}) collective-permute-start(bf16[128,4096]{1,0:T(8,128)(2,1)} %get-tuple-element.30), channel_id=1, source_target_pairs={{4,0},{8,4},{12,8},{5,1},{9,5},{13,9},{6,2},{10,6},{14,10},{7,3},{... | collective-permute-start | bytes 3145736 | tf_op jit(solution)/shard_map/ppermute | solution.py:65
  354.1 62.0 %collective-permute-start.12 = (bf16[128,4096]{1,0:T(8,128)(2,1)}, bf16[128,4096]{1,0:T(8,128)(2,1)}, u32[]{:S(2)}, u32[]{:S(2)}) collective-permute-start(bf16[128,4096]{1,0:T(8,128)(2,1)} %get-tuple-element.31), channel_id=1, source_target_pairs={{0,4},{4,8},{8,12},{1,5},{5,9},{9,13},{2,6},{6,10},{10,14},{3,7},{... | collective-permute-start | bytes 3145736 | tf_op jit(solution)/shard_map/ppermute | solution.py:62
  359.2 54.9 %copy-start.12 = (f32[256,1024]{1,0:T(8,128)S(1)}, f32[256,1024]{1,0:T(8,128)}, u32[]{:S(2)}) copy-start(f32[256,1024]{1,0:T(8,128)} %get-tuple-element.65) | copy-start | bytes 3145732
  359.2 63.5 %all-to-all-start.4 = ((bf16[4,56,4096]{2,1,0:T(8,128)(2,1)}), bf16[4,56,4096]{2,1,0:T(8,128)(2,1)S(1)}, u32[]{:S(2)}, u32[]{:S(2)}) async-start(bf16[4,56,4096]{2,1,0:T(8,128)(2,1)} %bitcast.119), calls=%async_computation.4 | async-start | bytes 3670016 | tf_op jit(solution)/shard_map/all_to_all | solution.py:89
  362.9 53.1 %copy-start.38 = (bf16[224,256]{1,0:T(8,128)(2,1)S(1)}, bf16[224,256]{1,0:T(8,128)(2,1)}, u32[]{:S(2)}) copy-start(bf16[224,256]{1,0:T(8,128)(2,1)} %fusion.48) | copy-start | bytes 344068
  380.6 33.5 %collective-permute-start.17 = (bf16[128,1024]{1,0:T(8,128)(2,1)}, bf16[128,1024]{1,0:T(8,128)(2,1)S(1)}, u32[]{:S(2)}, u32[]{:S(2)}) collective-permute-start(bf16[128,1024]{1,0:T(8,128)(2,1)} %get-tuple-element.44), channel_id=1, source_target_pairs={{0,8},{4,12},{8,0},{12,4},{1,9},{5,13},{9,1},{13,5},{2,10},{6,14},... | collective-permute-start | bytes 786440 | tf_op jit(solution)/shard_map/ppermute | solution.py:59
  427.7 38.7 %all-to-all-start.6 = ((bf16[4,56,4096]{2,1,0:T(8,128)(2,1)}), bf16[4,56,4096]{2,1,0:T(8,128)(2,1)}, u32[]{:S(2)}, u32[]{:S(2)}) async-start(bf16[4,56,4096]{2,1,0:T(8,128)(2,1)} %bitcast.120), calls=%async_computation.6 | async-start | bytes 3670016 | tf_op jit(solution)/shard_map/all_to_all | solution.py:89
  441.8 13.8 %copy-start.31 = (bf16[224,1024]{1,0:T(8,128)(2,1)S(1)}, bf16[224,1024]{1,0:T(8,128)(2,1)}, u32[]{:S(2)}) copy-start(bf16[224,1024]{1,0:T(8,128)(2,1)} %fusion.47) | copy-start | bytes 1376260
  466.3 17.6 %all-to-all-start.5 = ((bf16[4,56,2048]{2,1,0:T(8,128)(2,1)}), bf16[4,56,2048]{2,1,0:T(8,128)(2,1)S(1)}, u32[]{:S(2)}, u32[]{:S(2)}) async-start(bf16[4,56,2048]{2,1,0:T(8,128)(2,1)} %maximum_select_fusion), calls=%async_computation.5 | async-start | bytes 1835008 | tf_op jit(solution)/shard_map/all_to_all | solution.py:89
  (22 other events, 140.9 us)
Sparse Core Ops, SparseCore 0:
  9.6 30.6 all-gather.4
  43.8 159.2 all-gather.2
